TPU v7x, 32 devices: a whole 2x2x4 slice. The times are simulated.
32 devices in a mesh: parts: 2 (over y), tensor: 4 (over z), example: 4 (over x, core).
Axes of the slice: x: 2, y: 2, z: 4, core: 2. Of those that a mesh axis runs over, the one named last changes fastest.
Arguments:
- activations: bfloat16 [48, 512, 28672], P(('parts', 'example'), None, 'tensor'), parts along dimension 0, may hold values from -6 to 6
- out_grads: bfloat16 [48, 512, 8192], P(('parts', 'example'), None, 'tensor'), parts along dimension 0, may hold values from -6 to 6
- lengths: int32 [48], P(('parts', 'example')), parts along dimension 0, may hold values from 1 to 512, 9216 in all
- proj_in: bfloat16 [28672, 64], P('tensor'), may hold values from -2.362278 to 2.362278
- proj_out: bfloat16 [8192, 64], P('tensor'), may hold values from -4.4194174 to 4.4194174
- queries: bfloat16 [8192, 4096], P(('parts', 'example'), 'tensor'), parts along dimension 0, may hold values from -6 to 6
Outputs:
- scores: float32 [48, 4096], P(('parts', 'example'), 'tensor'), parts along dimension 0
There are 2 independent parts, one for each index of `parts`. A program takes and returns all parts, laid end to end along the dimension named above; an argument that names none is the same for every part. Nothing has to cross between parts.
All inputs are finite; a program needn't handle non-finite values. No bound on the sum of `lengths` on one device may be relied on, other than what follows from the above.
Results may differ from a plain program's by a relative error of at most 0.0029.
Values may be sent and summed in bfloat16 or wider, within the bound.
No kernel may reach another device: no remote copies, remote signals or barrier semaphores. Data moves between devices by JAX's collectives and lax.ppermute only.
A program may use at most 192 MiB of HBM per device.

v0:
```python
import jax
import jax.numpy as jnp
from jax import lax
from jax.sharding import PartitionSpec as P


def local(activations, out_grads, lengths, proj_in, proj_out, queries):
    nlists, slots, hidden_width = activations.shape
    feature_width = out_grads.shape[2]
    rank = proj_in.shape[1]
    left_part = jnp.dot(
        activations.reshape(nlists * slots, hidden_width),
        proj_in,
        preferred_element_type=jnp.float32,
    )
    right_part = jnp.dot(
        out_grads.reshape(nlists * slots, feature_width),
        proj_out,
        preferred_element_type=jnp.float32,
    )
    stacked = jnp.concatenate([left_part, right_part], axis=1).reshape(nlists, slots, 2 * rank)
    groups = lax.axis_size("tensor")
    block_rows = rank // groups
    summed = lax.psum(stacked, "tensor")
    positions = lax.broadcasted_iota(jnp.int32, (nlists, slots), 1)
    keep = (positions < lengths[:, None]).astype(jnp.float32)[:, :, None]
    left_full = summed[:, :, :rank] * keep
    right_full = summed[:, :, rank:]
    sketch = jnp.einsum("ltr,lts->lrs", left_full, right_full, precision=lax.Precision.HIGHEST)
    totals = jnp.sum(sketch * sketch, axis=(1, 2))
    unit_all = (sketch / jnp.sqrt(totals + 1e-06)[:, None, None]).astype(jnp.bfloat16)
    first_row = lax.axis_index("tensor") * block_rows
    mine = lax.dynamic_slice_in_dim(unit_all, first_row, block_rows, 1)
    mine = mine.reshape(nlists, block_rows * rank)
    terms = lax.dot_general(
        mine,
        lax.all_gather(queries, "example", axis=0, tiled=True),
        (((1,), (1,)), ((), ())),
        preferred_element_type=jnp.float32,
    )
    return lax.psum_scatter(terms, "tensor", scatter_dimension=1, tiled=True)


def solution(mesh):
    in_specs = (
        P(("parts", "example"), None, "tensor"),
        P(("parts", "example"), None, "tensor"),
        P(("parts", "example")),
        P("tensor", None),
        P("tensor", None),
        P(("parts", "example"), "tensor"),
    )
    out_specs = P(("parts", "example"), "tensor")
    return jax.shard_map(local, mesh=mesh, in_specs=in_specs, out_specs=out_specs, check_vma=False)
```

profile of v0, /device:TPU:2, one launch (start us, length us, event | category | flops | bytes accessed | tf_op | source)
XLA Modules:
  0.0 148.1 jit_solution(9170714146279140973)
XLA Ops:
  7.4 0.0 copy-start
  7.4 0.0 all-reduce.2.cloned.1.call-start
  7.4 1.2 copy-done
  8.5 0.0 copy-start.2
  8.5 20.9 %fusion.5 = f32[3072,64]{0,1:T(8,128)S(1)} fusion(bf16[3072,7168]{1,0:T(8,128)(2,1)} %bitcast.9, bf16[7168,64]{0,1:T(8,128)(2,1)S(1)} %copy-done), kind=kOutput, calls=%fused_computation.11 | convolution fusion | flops 2818572288 | bytes 45744128 | tf_op jit(solution)/shard_map/dot_general | solution.py:11
  29.4 0.0 copy-done.2
  29.4 8.5 %fusion.6 = f32[3072,64]{0,1:T(8,128)S(1)} fusion(bf16[3072,2048]{1,0:T(8,128)(2,1)} %bitcast.10, bf16[2048,64]{0,1:T(8,128)(2,1)S(1)} %copy-done.2), kind=kOutput, calls=%fused_computation.12 | convolution fusion | flops 805306368 | bytes 13631488 | tf_op jit(solution)/shard_map/dot_general | solution.py:16
  37.9 0.0 copy-start.3
  37.9 0.1 pad_maximum_fusion
  38.1 1.6 %copy.8 = f32[3072,128]{1,0:T(8,128)} copy(f32[3072,128]{0,1:T(8,128)S(1)} %pad_maximum_fusion) | data formatting | bytes 3145728 | tf_op jit(solution)/shard_map/concatenate | solution.py:21
  39.7 0.0 copy-start.1
  39.7 3.2 %copy.9 = f32[6,512,128]{1,2,0:T(8,128)} copy(f32[6,512,128]{2,1,0:T(8,128)} %bitcast.11) | data formatting | bytes 3145728 | tf_op jit(solution)/shard_map/reshape | solution.py:21
  42.9 0.0 all-reduce.2.cloned.1.call-update
  42.9 0.0 all-gather.2.cloned.1.call-start
  42.9 0.5 all-gather.2.cloned.1.call-update
  43.5 0.0 reduce-scatter.2.cloned.1.call-start
  43.5 0.0 copy-done.3
  43.5 0.1 fusion.4
  43.6 69.8 %all-reduce.2.cloned.1.call-done = f32[6,512,128]{1,2,0:T(8,128)} async-done(((f32[6,512,128]{1,2,0:T(8,128)}), f32[6,512,128]{1,2,0:T(8,128)}) %all-reduce.2.cloned.1.call-update) | async-done | bytes 1572880 | tf_op jit(solution)/shard_map/psum | solution.py:24
  113.4 2.3 %multiply_reduce_fusion = (f32[6]{0:T(128)S(1)}, f32[6,64,64]{2,1,0:T(8,128)S(1)}) fusion(f32[6,512,128]{1,2,0:T(8,128)} %all-reduce.2.cloned.1.call-done, f32[6,512]{1,0:T(8,128)S(1)} %fusion.4), kind=kOutput, calls=%fused_computation.5 | convolution fusion | flops 151240704 | bytes 1683480 | tf_op jit(solution)/shard_map/ltr,lts->lrs/dot_general | solution.py:29
  115.7 0.1 fusion.3
  115.8 0.1 reshape.39
  115.9 0.0 all-gather.2.cloned.1.call-done
  115.9 6.3 %fusion.7 = f32[6,4096]{1,0:T(8,128)} fusion(bf16[6,1024]{1,0:T(8,128)(2,1)S(1)} %reshape.39, bf16[4096,1024]{1,0:T(8,128)(2,1)} %all-gather.2.cloned.1.call-done), kind=kOutput, calls=%fused_computation.13 | convolution fusion | flops 50331648 | bytes 8499200 | tf_op jit(solution)/shard_map/dot_general | solution.py:35
  122.2 0.0 reduce-scatter.2.cloned.1.call-update
  122.2 18.4 %reduce-scatter.2.cloned.1.call-done = f32[6,1024]{1,0:T(8,128)} async-done(((f32[6,4096]{1,0:T(8,128)}), f32[6,1024]{1,0:T(8,128)}) %reduce-scatter.2.cloned.1.call-update) | async-done | bytes 24592 | tf_op jit(solution)/shard_map/reduce_scatter | solution.py:41
  140.6 0.0 copy-done.1
  (1 shorter events, 0.0 us)
Async XLA Ops:
  7.4 1.2 copy-start
  7.4 106.0 %all-reduce.2.cloned.1.call-start = ((), (), s32[]{:S(2)}) async-start(), calls=%async_computation.1 | async-start | bytes 3145728 | tf_op jit(solution)/shard_map/psum | solution.py:24
  8.5 20.9 %copy-start.2 = (bf16[2048,64]{0,1:T(8,128)(2,1)S(1)}, bf16[2048,64]{0,1:T(8,128)(2,1)}, u32[]{:S(2)}) copy-start(bf16[2048,64]{0,1:T(8,128)(2,1)} %param.10) | copy-start | bytes 786436
  37.9 5.6 %copy-start.3 = (s32[6]{0:T(128)S(1)}, s32[6]{0:T(128)}, u32[]{:S(2)}) copy-start(s32[6]{0:T(128)} %param.8) | copy-start | bytes 76
  39.7 101.0 %copy-start.1 = (bf16[7168,64]{0,1:T(8,128)(2,1)S(1)}, bf16[7168,64]{0,1:T(8,128)(2,1)}, u32[]{:S(2)}) copy-start(bf16[7168,64]{0,1:T(8,128)(2,1)} %param.9) | copy-start | bytes 2752516
  42.9 73.0 %all-gather.2.cloned.1.call-start = ((), (), s32[]{:S(2)}) async-start(), calls=%async_computation.2 | async-start | bytes 10485760 | tf_op jit(solution)/shard_map/all_gather | solution.py:37
  43.5 97.2 %reduce-scatter.2.cloned.1.call-start = ((), (), s32[]{:S(2)}) async-start(), calls=%async_computation.3 | async-start | bytes 163840 | tf_op jit(solution)/shard_map/reduce_scatter | solution.py:41
Sparse Core Ops, SparseCore 0:
  43.0 70.3 all-reduce.1
  122.4 18.2 reduce-scatter.1
Sparse Core Ops, SparseCore 1:
  44.9 58.2 all-gather.1
where the time goes:
time: 150 us; the launch traced here: 148 us
  waiting for transfers between devices  88.7 us (59%)
  matrix products  38 us (25%)
  between operations  14.9 us (10%)
  local copies, waits for them, and re-layouts  6.09 us (4%)
    psum x1, waiting for transfers between devices, local(): summed = lax.psum(stacked, 'tensor')  69.8 us
    dot_general x1, matrix products, local(): jnp.dot(activations.reshape(nlists * slots, hidden_width), proj_in, prefe...  20.9 us
    reduce_scatter x1, waiting for transfers between devices, local(): return lax.psum_scatter(terms, 'tensor', scatter_dimension=1, tiled=True)  18.4 us
    dot_general x1, matrix products, local(): jnp.dot(out_grads.reshape(nlists * slots, feature_width), proj_out, prefe...  8.5 us
    dot_general x1, matrix products, local(): lax.dot_general(mine, lax.all_gather(queries, 'example', axis=0, tiled=Tr...  6.29 us
    reshape x1, local copies, waits for them, and re-layouts, local(): jnp.concatenate([left_part, right_part], axis=1)  3.18 us
  transfers between devices with their start and end apart: 3, of which 2 were waited for; matrix products, arithmetic and copies ran while one was open for 2% of the time, Pallas kernels for 0%

commit v1 on v0

--- a/solution.py
+++ b/solution.py
@@ -1,7 +1,227 @@
+import functools
+
 import jax
 import jax.numpy as jnp
 from jax import lax
+from jax.experimental import pallas as pl
+from jax.experimental.pallas import tpu as pltpu
 from jax.sharding import PartitionSpec as P
+
+TOP = 14.0
+EXTRA = 8
+NT = (((1,), (1,)), ((), ()))
+NN = (((1,), (0,)), ((), ()))
+
+
+def right_kernel(grads, basis, out):
+    rank = basis.shape[0]
+    right = lax.dot_general(grads[0], basis[...], NT, preferred_element_type=jnp.float32).T
+    largest = jnp.max(jnp.abs(right), axis=0, keepdims=True)
+    exponent = jnp.ceil(jnp.log2(jnp.maximum(largest, 1e-30)))
+    out[:rank] = right * jnp.exp2(TOP - exponent)
+    out[rank:] = jnp.broadcast_to(exponent, (EXTRA, right.shape[1]))
+
+
+def project_right(out_grads, basis):
+    lists, slots, width = out_grads.shape
+    rank = basis.shape[0]
+    return pl.pallas_call(
+        right_kernel,
+        grid=(lists,),
+        in_specs=[
+            pl.BlockSpec((1, slots, width), lambda l: (l, 0, 0)),
+            pl.BlockSpec((rank, width), lambda l: (0, 0)),
+        ],
+        out_specs=pl.BlockSpec((rank + EXTRA, slots), lambda l: (0, l)),
+        out_shape=jax.ShapeDtypeStruct((rank + EXTRA, lists * slots), jnp.float32),
+        cost_estimate=pl.CostEstimate(flops=8 * lists * slots * width * rank, bytes_accessed=2 * out_grads.size, transcendentals=0),
+        compiler_params=pltpu.CompilerParams(vmem_limit_bytes=40 << 20),
+        name="project_right",
+    )(out_grads, basis)
+
+
+def left_kernel(first, depth, lengths, acts, basis, out, total):
+    step = pl.program_id(1)
+    rank = basis.shape[0]
+    columns = pl.ds(pl.multiple_of(step * depth, depth), depth)
+    part = lax.dot_general(acts[0], basis[:, columns], NT, preferred_element_type=jnp.float32)
+
+    @pl.when(step == 0)
+    def _():
+        total[...] = part
+
+    @pl.when(step > 0)
+    def _():
+        total[...] += part
+
+    @pl.when(step == pl.num_programs(1) - 1)
+    def _():
+        count = lengths[pl.program_id(0) + first]
+        rows = lax.broadcasted_iota(jnp.int32, total.shape, 0)
+        left = jnp.where(rows < count, total[...], 0.0)
+        head = left.astype(jnp.bfloat16)
+        out[:, :rank] = head
+        out[:, rank:] = (left - head.astype(jnp.float32)).astype(jnp.bfloat16)
+
+
+def project_left(activations, basis, lengths, first, lists, cuts):
+    slots, width = activations.shape[1:]
+    rank = basis.shape[0]
+    depth = width // cuts
+    return pl.pallas_call(
+        functools.partial(left_kernel, first, depth),
+        grid_spec=pltpu.PrefetchScalarGridSpec(
+            num_scalar_prefetch=1,
+            grid=(lists, cuts),
+            in_specs=[
+                pl.BlockSpec((1, slots, depth), lambda l, k, _: (l + first, 0, k)),
+                pl.BlockSpec((rank, width), lambda l, k, _: (0, 0)),
+            ],
+            out_specs=pl.BlockSpec((slots, 2 * rank), lambda l, k, _: (l, 0)),
+            scratch_shapes=[pltpu.VMEM((slots, rank), jnp.float32)],
+        ),
+        out_shape=jax.ShapeDtypeStruct((lists * slots, 2 * rank), jnp.bfloat16),
+        cost_estimate=pl.CostEstimate(flops=8 * lists * slots * width * rank, bytes_accessed=2 * lists * slots * width, transcendentals=0),
+        compiler_params=pltpu.CompilerParams(vmem_limit_bytes=40 << 20),
+        name="project_left",
+    )(lengths, activations, basis)
+
+
+def sketch_kernel(unit, per_list, half, where, rights, left_a, left_b, out, sums):
+    rank = sums.shape[1]
+    width = rights.shape[2]
+    sums[...] = jnp.zeros_like(sums)
+    for block in range(rights.shape[0]):
+        value = rights[block]
+        head = value.astype(jnp.bfloat16)
+        both = jnp.concatenate([head, (value - head.astype(jnp.float32)).astype(jnp.bfloat16)], axis=0)
+        for piece in range(width // unit):
+            index = where[block] * (width // unit) + piece
+            right = both[:, piece * unit:(piece + 1) * unit]
+
+            def add(left_ref, start):
+                left = left_ref[pl.ds(pl.multiple_of(start * unit, unit), unit), :]
+                full = lax.dot_general(right, left, NN, preferred_element_type=jnp.float32)
+                side = full[:rank] + full[rank:]
+                sums[index // per_list] += side[:, :rank] + side[:, rank:]
+
+            @pl.when(index < half)
+            def _():
+                add(left_a, index)
+
+            @pl.when(index >= half)
+            def _():
+                add(left_b, index - half)
+
+    for l in range(sums.shape[0]):
+        sums[l] = sums[l].T
+    rows = out.shape[2] // rank
+    for i in range(rank):
+        column = (i % rows) * rank
+        out[i // rows, :sums.shape[0], column:column + rank] = sums[:, i, :]
+
+
+def sketch_terms(where, rights, left_a, left_b, lists, slots, groups):
+    rank = rights.shape[1]
+    unit = slots // 2
+    vmem = pl.BlockSpec(memory_space=pltpu.VMEM)
+    return pl.pallas_call(
+        functools.partial(sketch_kernel, unit, slots // unit, left_a.shape[0] // unit),
+        in_specs=[pl.BlockSpec(memory_space=pltpu.SMEM), vmem, vmem, vmem],
+        out_specs=vmem,
+        out_shape=jax.ShapeDtypeStruct((groups, 8, rank * rank // groups), jnp.float32),
+        scratch_shapes=[pltpu.VMEM((lists, rank, rank), jnp.float32)],
+        compiler_params=pltpu.CompilerParams(vmem_limit_bytes=40 << 20),
+        name="sketch_terms",
+    )(where, rights, left_a, left_b)
+
+
+def score_kernel(*refs):
+    sketches, queries, out = refs[:-2], refs[-2], refs[-1]
+    count = queries.shape[0]
+    value = jnp.concatenate([s[...] for s in sketches], axis=0)
+    head = value.astype(jnp.bfloat16)
+    both = jnp.concatenate([head, (value - head.astype(jnp.float32)).astype(jnp.bfloat16)], axis=0)
+    full = lax.dot_general(both, queries[...], NT, preferred_element_type=jnp.float32)
+    rows = value.shape[0]
+    terms = full[:rows] + full[rows:]
+    squares = jnp.sum(value * value, axis=1, keepdims=True)
+    for group in range(len(sketches)):
+        out[group, :, :count] = terms[group * 8:group * 8 + 8]
+        out[group, :, count:] = jnp.broadcast_to(squares[group * 8:group * 8 + 8], (8, 128))
+
+
+def score_terms(sketches, queries):
+    vmem = pl.BlockSpec(memory_space=pltpu.VMEM)
+    return pl.pallas_call(
+        score_kernel,
+        in_specs=[vmem] * (len(sketches) + 1),
+        out_specs=vmem,
+        out_shape=jax.ShapeDtypeStruct((len(sketches), 8, queries.shape[0] + 128), jnp.float32),
+        compiler_params=pltpu.CompilerParams(vmem_limit_bytes=40 << 20),
+        name="score_terms",
+    )(*sketches, queries)
+
+
+def ring(size, shift):
+    return [(i, (i + shift) % size) for i in range(size)]
+
+
+def decoded(coded, rank):
+    wide = coded.astype(jnp.float32)
+    return wide[..., :rank, :] * jnp.exp2(wide[..., rank:rank + 1, :] - TOP)
+
+
+def local_square(activations, out_grads, lengths, proj_in, proj_out, queries):
+    lists, slots, _ = activations.shape
+    rank = proj_in.shape[1]
+    groups = lax.axis_size("tensor")
+    me = lax.axis_index("tensor")
+    shifts = range(1, groups)
+    tokens = lists * slots
+    block = tokens // groups
+
+    right = project_right(out_grads, proj_out.T)
+    coded = right.astype(jnp.float16)
+
+    def part(shift):
+        return lax.dynamic_slice_in_dim(coded, (me + shift) % groups * block, block, 1)
+
+    arrived = [lax.ppermute(part(shift), "tensor", ring(groups, shift)) for shift in shifts]
+    early = lists // 2
+    left_a = project_left(activations, proj_in.T, lengths, 0, early, 2)
+    pieces = [part(0)] + arrived
+    wide = [p.astype(jnp.float32) for p in pieces]
+    summed = sum(w * jnp.exp2(w[rank:rank + 1] - TOP) for w in wide)
+    exponent = functools.reduce(jnp.maximum, [w[rank:rank + 1] for w in wide]) + (groups - 1).bit_length()
+    row = lax.broadcasted_iota(jnp.int32, summed.shape, 0)
+    mine = jnp.where(row < rank, summed * jnp.exp2(TOP - exponent), exponent).astype(jnp.float16)
+    blocks = [mine] + [lax.ppermute(mine, "tensor", ring(groups, shift)) for shift in shifts]
+    left_b = project_left(activations, proj_in.T, lengths, early, lists - early, 2)
+    rights = decoded(jnp.stack(blocks), rank)
+    where = (me - jnp.arange(groups, dtype=jnp.int32)) % groups
+    terms = sketch_terms(where, rights, left_a, left_b, lists, slots, groups)
+
+    def towards(array, index):
+        return lax.dynamic_index_in_dim(array, index, 0, keepdims=False)
+
+    sketch = towards(terms, me)
+    for shift in shifts:
+        sketch = sketch + lax.ppermute(towards(terms, (me + shift) % groups), "tensor", ring(groups, shift))
+    sketches = [sketch] + [lax.ppermute(sketch, "example", ring(groups, shift)) for shift in shifts]
+    scores = score_terms(sketches, queries)
+    here = lax.axis_index("example")
+    final = None
+    for shift in range(groups):
+        target = (me + shift) % groups
+        pairs = [
+            (t * groups + e, e * groups + (t + shift) % groups)
+            for t in range(groups) for e in range(groups)
+        ]
+        moved = lax.ppermute(towards(scores, (here - target) % groups), ("tensor", "example"), pairs)
+        final = moved if final is None else final + moved
+    count = queries.shape[0]
+    return final[:lists, :count] * lax.rsqrt(final[:lists, count:count + 1] + 1e-06)
 
 
 def local(activations, out_grads, lengths, proj_in, proj_out, queries):
@@ -51,4 +271,6 @@
         P(("parts", "example"), "tensor"),
     )
     out_specs = P(("parts", "example"), "tensor")
-    return jax.shard_map(local, mesh=mesh, in_specs=in_specs, out_specs=out_specs, check_vma=False)
+    square = mesh.shape["tensor"] == mesh.shape["example"]
+    plan = local_square if square else local
+    return jax.shard_map(plan, mesh=mesh, in_specs=in_specs, out_specs=out_specs, check_vma=False)

time: 150 us -> 88.7 us (0.59)
  waiting for transfers between devices: 88.7 us -> 19.7 us
  matrix products: 38 us -> 0 us
  Pallas kernels: 0 us -> 32.9 us
  starting transfers between devices: 0.09 us -> 21.3 us
  between operations: 14.9 us -> 0.23 us
  other arithmetic: 0.28 us -> 5.82 us
    psum x1 -> x0, waiting for transfers between devices: 69.8 us -> none  [local(): summed = lax.psum(stacked, 'tensor')]
    dot_general x4 -> x0, matrix products: 38 us -> none  [the longest x1 20.9 us: local(): jnp.dot(activations.reshape(nlists * slots, hidden_width), proj_in, prefe...]
    pallas_call x0 -> x5, Pallas kernels: none -> 32.9 us  [the longest x2 23.9 us: project_left(): pl.pallas_call(functools.partial(left_kernel, first, depth), grid_spec=pl...]
    ppermute x0 -> x16, starting transfers between devices: none -> 21.3 us  [the longest x4 7.17 us: local_square(): lax.ppermute(towards(scores, (here - target) % groups), ('tensor', 'examp...]
    ppermute x0 -> x16, waiting for transfers between devices: none -> 19.7 us  [the longest x3 9.04 us: local_square(): lax.ppermute(mine, 'tensor', ring(groups, shift))]
    reduce_scatter x1 -> x0, waiting for transfers between devices: 18.4 us -> none  [local(): return lax.psum_scatter(terms, 'tensor', scatter_dimension=1, tiled=True)]
    unnamed x8 -> x17, local copies, waits for them, and re-layouts: 1.19 us -> 7.29 us
    convert_element_type x2 -> x7, other arithmetic: 0.16 us -> 4.05 us  [the longest x4 2.76 us: local_square(): wide = [p.astype(jnp.float32) for p in pieces]]
  transfers between devices with their start and end apart: 3 -> 16, of which waited for: 2 -> 9; matrix products, arithmetic and copies ran while one was open for 2% -> 1% of each run, Pallas kernels for 0% -> 27%
where the time goes in v1:
time: 88.7 us; the launch traced here: 87.3 us
  Pallas kernels  32.9 us (37%)
  starting transfers between devices  21.3 us (24%)
  waiting for transfers between devices  19.7 us (22%)
  local copies, waits for them, and re-layouts  7.34 us (8%)
  other arithmetic  5.82 us (7%)
    pallas_call x2, Pallas kernels, project_left(): pl.pallas_call(functools.partial(left_kernel, first, depth), grid_spec=pl...  23.9 us
    ppermute x3, waiting for transfers between devices, local_square(): lax.ppermute(mine, 'tensor', ring(groups, shift))  9.04 us
    unnamed x17, local copies, waits for them, and re-layouts  7.29 us
    ppermute x4, starting transfers between devices, local_square(): lax.ppermute(towards(scores, (here - target) % groups), ('tensor', 'examp...  7.17 us
    ppermute x4, waiting for transfers between devices, local_square(): lax.ppermute(towards(scores, (here - target) % groups), ('tensor', 'examp...  4.83 us
    pallas_call x1, Pallas kernels, project_right(): pl.pallas_call(right_kernel, grid=(lists,), in_specs=[pl.BlockSpec((1, sl...  4.73 us
    ppermute x3, starting transfers between devices, local_square(): lax.ppermute(part(shift), 'tensor', ring(groups, shift))  4.6 us
    ppermute x3, starting transfers between devices, local_square(): lax.ppermute(mine, 'tensor', ring(groups, shift))  4 us
  transfers between devices with their start and end apart: 16, of which 9 were waited for; matrix products, arithmetic and copies ran while one was open for 1% of the time, Pallas kernels for 27%

profile of v1, /device:TPU:2, one launch (start us, length us, event | category | flops | bytes accessed | tf_op | source)
XLA Modules:
  0.0 87.3 jit_solution(6988610521871991592)
XLA Ops:
  0.0 4.6 %copy-done = bf16[6,512,2048]{2,1,0:T(8,128)(2,1)S(1)} copy-done((bf16[6,512,2048]{2,1,0:T(8,128)(2,1)S(1)}, bf16[6,512,2048]{2,1,0:T(8,128)(2,1)}, u32[]{:S(2)}) %copy-start) | copy-done | bytes 12582936
  4.6 0.9 %copy-done.5 = bf16[2048,64]{0,1:T(8,128)(2,1)S(1)} copy-done((bf16[2048,64]{0,1:T(8,128)(2,1)S(1)}, bf16[2048,64]{0,1:T(8,128)(2,1)}, u32[]{:S(2)}) %copy-start.5) | copy-done | bytes 262168
  5.5 4.7 %project_right.1 = f32[72,3072]{1,0:T(8,128)S(1)} custom-call(bf16[6,512,2048]{2,1,0:T(8,128)(2,1)S(1)} %copy-done, bf16[64,2048]{1,0:T(8,128)(2,1)S(1)} %bitcast.31), custom_call_target="tpu_custom_call" | custom-call | flops 3221225472 | bytes 12582912 | tf_op jit(solution)/shard_map/project_right/pallas_call | solution.py:28
  10.4 0.9 %dynamic-slice_convert_fusion = (f32[72,768]{1,0:T(8,128)}, f16[72,768]{1,0:T(8,128)(2,1)}, f16[72,768]{1,0:T(8,128)(2,1)}, f16[72,768]{1,0:T(8,128)(2,1)}) fusion(f16[72,3072]{1,0:T(8,128)(2,1)S(1)} %convert_element_type.21, s32[]{:T(128)S(6)} %select_n.99, s32[]{:T(128)S(6)} %select_n.105, s32[]{:T(128)S(6)} %select_n.103, s32[]{:T(128)S(6)} %select_n.101), kind=kLoop, calls=%fused_computation.3 | loop fusion | flops 55296 | bytes 995344 | tf_op jit(solution)/shard_map/convert_element_type | solution.py:194
  11.3 3.6 %collective-permute-start.2 = (f16[72,768]{1,0:T(8,128)(2,1)}, f16[72,768]{1,0:T(8,128)(2,1)S(1)}, u32[]{:S(2)}, u32[]{:S(2)}) collective-permute-start(f16[72,768]{1,0:T(8,128)(2,1)} %get-tuple-element.8), channel_id=1, source_target_pairs={{0,12},{4,0},{8,4},{12,8},{1,13},{5,1},{9,5},{13,9},{2,14},{6,2},{... | collective-permute-start | bytes 331784 | tf_op jit(solution)/shard_map/ppermute | solution.py:190
  14.9 1.0 %collective-permute-start = (f16[72,768]{1,0:T(8,128)(2,1)}, f16[72,768]{1,0:T(8,128)(2,1)}, u32[]{:S(2)}, u32[]{:S(2)}) collective-permute-start(f16[72,768]{1,0:T(8,128)(2,1)} %get-tuple-element.10), channel_id=1, source_target_pairs={{0,4},{4,8},{8,12},{12,0},{1,5},{5,9},{9,13},{13,1},{2,6},{6,10},{... | collective-permute-start | bytes 331784 | tf_op jit(solution)/shard_map/ppermute | solution.py:190
  15.9 11.9 %project_left.2.left_a = bf16[1536,128]{1,0:T(8,128)(2,1)S(1)} custom-call(s32[6]{0:T(128)S(1)} %copy-done.6, bf16[6,512,7168]{2,1,0:T(8,128)(2,1)} %acts.3, bf16[64,7168]{1,0:T(8,128)(2,1)S(1)} %bitcast.29), custom_call_target="tpu_custom_call" | custom-call | flops 5637144576 | bytes 22020096 | tf_op jit(solution)/shard_map/project_left/pallas_call | solution.py:71
  27.8 12.0 %project_left.3.left_b = bf16[1536,128]{1,0:T(8,128)(2,1)S(1)} custom-call(s32[6]{0:T(128)S(1)} %copy-done.6, bf16[6,512,7168]{2,1,0:T(8,128)(2,1)} %acts.3, bf16[64,7168]{1,0:T(8,128)(2,1)S(1)} %bitcast.30), custom_call_target="tpu_custom_call" | custom-call | flops 5637144576 | bytes 22020096 | tf_op jit(solution)/shard_map/project_left/pallas_call | solution.py:71
  39.8 0.7 copy-done.3
  40.6 0.9 %convert_element_type.24 = f32[72,768]{1,0:T(8,128)S(1)} convert(f16[72,768]{1,0:T(8,128)(2,1)} %collective-permute-done.1) | non-fusion elementwise | flops 55296 | bytes 331776 | tf_op jit(solution)/shard_map/convert_element_type | solution.py:194
  41.5 0.9 %convert_element_type.23 = f32[72,768]{1,0:T(8,128)S(1)} convert(f16[72,768]{1,0:T(8,128)(2,1)} %collective-permute-done) | non-fusion elementwise | flops 55296 | bytes 331776 | tf_op jit(solution)/shard_map/convert_element_type | solution.py:194
  42.4 0.8 exponential_reduce_fusion.4
  43.2 1.1 %select_convert_fusion = f16[72,768]{1,0:T(8,128)(2,1)S(1)} fusion(f32[768]{0:T(1024)S(1)} %get-tuple-element.6, f32[768]{0:T(1024)S(1)} %get-tuple-element.5, f32[768]{0:T(1024)S(1)} %get-tuple-element.15, f32[768]{0:T(1024)S(1)} %get-tuple-element.14, f32[768]{0:T(1024)S(1)} %get-tuple-element.13, f32[768]{0:T(1024)S(1)} %get-tuple-element.11, ...), kind=kLoop, calls=%fused_computation.2 | loop fusion | flops 774144 | bytes 571468 | tf_op jit(solution)/shard_map/convert_element_type | solution.py:198
  44.4 2.9 %collective-permute-start.5 = (f16[72,768]{1,0:T(8,128)(2,1)S(1)}, f16[72,768]{1,0:T(8,128)(2,1)S(1)}, u32[]{:S(2)}, u32[]{:S(2)}) collective-permute-start(f16[72,768]{1,0:T(8,128)(2,1)S(1)} %select_convert_fusion), channel_id=1, source_target_pairs={{0,12},{4,0},{8,4},{12,8},{1,13},{5,1},{9,5},{13,9},{2,14},{6,2},{... | collective-permute-start | bytes 331784 | tf_op jit(solution)/shard_map/ppermute | solution.py:199
  47.2 1.1 %collective-permute-start.4 = (f16[72,768]{1,0:T(8,128)(2,1)S(1)}, f16[72,768]{1,0:T(8,128)(2,1)S(1)}, u32[]{:S(2)}, u32[]{:S(2)}) collective-permute-start(f16[72,768]{1,0:T(8,128)(2,1)S(1)} %select_convert_fusion), channel_id=1, source_target_pairs={{0,8},{4,12},{8,0},{12,4},{1,9},{5,13},{9,1},{13,5},{2,10},{6,14},... | collective-permute-start | bytes 331784 | tf_op jit(solution)/shard_map/ppermute | solution.py:199
  48.4 2.4 %collective-permute-done.5 = f16[72,768]{1,0:T(8,128)(2,1)S(1)} collective-permute-done((f16[72,768]{1,0:T(8,128)(2,1)S(1)}, f16[72,768]{1,0:T(8,128)(2,1)S(1)}, u32[]{:S(2)}, u32[]{:S(2)}) %collective-permute-start.5) | collective-permute-done | bytes 110624 | tf_op jit(solution)/shard_map/ppermute | solution.py:199
  50.7 6.7 %collective-permute-done.4 = f16[72,768]{1,0:T(8,128)(2,1)S(1)} collective-permute-done((f16[72,768]{1,0:T(8,128)(2,1)S(1)}, f16[72,768]{1,0:T(8,128)(2,1)S(1)}, u32[]{:S(2)}, u32[]{:S(2)}) %collective-permute-start.4) | collective-permute-done | bytes 110624 | tf_op jit(solution)/shard_map/ppermute | solution.py:199
  57.7 1.0 %copy-done.4 = bf16[1536,128]{1,0:T(8,128)(2,1)S(1)} copy-done((bf16[1536,128]{1,0:T(8,128)(2,1)S(1)}, bf16[1536,128]{1,0:T(8,128)(2,1)}, u32[]{:S(2)}) %copy-start.4) | copy-done | bytes 393240
  58.7 3.6 %sketch_terms.1 = f32[4,8,1024]{2,1,0:T(8,128)S(1)} custom-call(s32[4]{0:T(128)S(1)} %and_select_fusion.where, f32[4,64,768]{2,1,0:T(8,128)S(1)} %slice_multiply_fusion.rights, bf16[1536,128]{1,0:T(8,128)(2,1)S(1)} %project_left.2.left_a, bf16[1536,128]{1,0:T(8,128)(2,1)S(1)} %copy-done.4), custom_call_target="tpu_custom_call" | custom-call | tf_op jit(solution)/shard_map/sketch_terms/pallas_call | solution.py:128
  62.3 0.8 collective-permute-start.8
  63.1 0.8 collective-permute-start.7
  63.9 1.9 %collective-permute-start.6 = (f32[8,1024]{1,0:T(8,128)S(1)}, f32[8,1024]{1,0:T(8,128)S(1)}, u32[]{:S(2)}, u32[]{:S(2)}) collective-permute-start(f32[8,1024]{1,0:T(8,128)S(1)} %get-tuple-element.20), channel_id=1, source_target_pairs={{0,4},{4,8},{8,12},{12,0},{1,5},{5,9},{9,13},{13,1},{2,6},{6,10},{... | collective-permute-start | bytes 98312 | tf_op jit(solution)/shard_map/ppermute | solution.py:210
  66.2 1.8 %collective-permute-done.7 = f32[8,1024]{1,0:T(8,128)S(1)} collective-permute-done((f32[8,1024]{1,0:T(8,128)S(1)}, f32[8,1024]{1,0:T(8,128)S(1)}, u32[]{:S(2)}, u32[]{:S(2)}) %collective-permute-start.7) | collective-permute-done | bytes 32800 | tf_op jit(solution)/shard_map/ppermute | solution.py:210
  68.0 1.5 %collective-permute-done.6 = f32[8,1024]{1,0:T(8,128)S(1)} collective-permute-done((f32[8,1024]{1,0:T(8,128)S(1)}, f32[8,1024]{1,0:T(8,128)S(1)}, u32[]{:S(2)}, u32[]{:S(2)}) %collective-permute-start.6) | collective-permute-done | bytes 32800 | tf_op jit(solution)/shard_map/ppermute | solution.py:210
  70.2 1.4 %collective-permute-start.11 = (f32[8,1024]{1,0:T(8,128)S(1)}, f32[8,1024]{1,0:T(8,128)S(1)}, u32[]{:S(2)}, u32[]{:S(2)}) collective-permute-start(f32[8,1024]{1,0:T(8,128)S(1)} %fusion.1.refs_0_), channel_id=1, source_target_pairs={{0,3},{1,0},{2,1},{3,2},{4,7},{5,4},{6,5},{7,6},{8,11},{9,8},{10,9... | collective-permute-start | bytes 98312 | tf_op jit(solution)/shard_map/ppermute | solution.py:211
  71.6 1.3 %collective-permute-done.9.refs_1_ = f32[8,1024]{1,0:T(8,128)S(1)} collective-permute-done((f32[8,1024]{1,0:T(8,128)S(1)}, f32[8,1024]{1,0:T(8,128)S(1)}, u32[]{:S(2)}, u32[]{:S(2)}) %collective-permute-start.9) | collective-permute-done | bytes 32800 | tf_op jit(solution)/shard_map/ppermute | solution.py:211
  73.0 0.7 collective-permute-done.10.refs_2_
  73.7 0.7 score_terms.1
  74.5 1.2 %collective-permute-start.15 = (f32[8,1152]{1,0:T(8,128)S(1)}, f32[8,1152]{1,0:T(8,128)S(1)}, u32[]{:S(2)}, u32[]{:S(2)}) collective-permute-start(f32[8,1152]{1,0:T(8,128)S(1)} %get-tuple-element.17), channel_id=1, source_target_pairs={{0,3},{1,7},{2,11},{3,15},{4,0},{5,4},{6,8},{7,12},{8,1},{9,5},{10... | collective-permute-start | bytes 110600 | tf_op jit(solution)/shard_map/ppermute | solution.py:221
  76.2 5.4 %collective-permute-start.12 = (f32[8,1152]{1,0:T(8,128)S(1)}, f32[8,1152]{1,0:T(8,128)S(1)}, u32[]{:S(2)}, u32[]{:S(2)}) collective-permute-start(f32[8,1152]{1,0:T(8,128)S(1)} %get-tuple-element.19), channel_id=1, source_target_pairs={{0,0},{1,4},{2,8},{3,12},{4,1},{5,5},{6,9},{7,13},{8,2},{9,6},{10,... | collective-permute-start | bytes 110600 | tf_op jit(solution)/shard_map/ppermute | solution.py:221
  81.7 2.3 %collective-permute-done.12 = f32[8,1152]{1,0:T(8,128)S(1)} collective-permute-done((f32[8,1152]{1,0:T(8,128)S(1)}, f32[8,1152]{1,0:T(8,128)S(1)}, u32[]{:S(2)}, u32[]{:S(2)}) %collective-permute-start.12) | collective-permute-done | bytes 36896 | tf_op jit(solution)/shard_map/ppermute | solution.py:221
  84.0 2.5 %collective-permute-done.13 = f32[8,1152]{1,0:T(8,128)S(1)} collective-permute-done((f32[8,1152]{1,0:T(8,128)S(1)}, f32[8,1152]{1,0:T(8,128)S(1)}, u32[]{:S(2)}, u32[]{:S(2)}) %collective-permute-start.13) | collective-permute-done | bytes 36896 | tf_op jit(solution)/shard_map/ppermute | solution.py:221
  (41 shorter events, 3.0 us)
Async XLA Ops:
  0.0 15.9 %copy-start.6 = (s32[6]{0:T(128)S(1)}, s32[6]{0:T(128)}, u32[]{:S(2)}) copy-start(s32[6]{0:T(128)} %lengths.3) | copy-start | bytes 76
  0.0 4.6 %copy-start = (bf16[6,512,2048]{2,1,0:T(8,128)(2,1)S(1)}, bf16[6,512,2048]{2,1,0:T(8,128)(2,1)}, u32[]{:S(2)}) copy-start(bf16[6,512,2048]{2,1,0:T(8,128)(2,1)} %grads.1) | copy-start | bytes 37748740
  4.6 0.9 %copy-start.5 = (bf16[2048,64]{0,1:T(8,128)(2,1)S(1)}, bf16[2048,64]{0,1:T(8,128)(2,1)}, u32[]{:S(2)}) copy-start(bf16[2048,64]{0,1:T(8,128)(2,1)} %param.10) | copy-start | bytes 786436
  5.5 10.4 %copy-start.1 = (bf16[7168,64]{0,1:T(8,128)(2,1)S(1)}, bf16[7168,64]{0,1:T(8,128)(2,1)}, u32[]{:S(2)}) copy-start(bf16[7168,64]{0,1:T(8,128)(2,1)} %param.9) | copy-start | bytes 2752516
  10.3 5.6 %copy-start.7 = (f16[72,3072]{1,0:T(8,128)(2,1)}, f16[72,3072]{1,0:T(8,128)(2,1)S(1)}, u32[]{:S(2)}) copy-start(f16[72,3072]{1,0:T(8,128)(2,1)S(1)} %convert_element_type.21) | copy-start | bytes 1327108
  11.3 29.3 %collective-permute-start.2 = (f16[72,768]{1,0:T(8,128)(2,1)}, f16[72,768]{1,0:T(8,128)(2,1)S(1)}, u32[]{:S(2)}, u32[]{:S(2)}) collective-permute-start(f16[72,768]{1,0:T(8,128)(2,1)} %get-tuple-element.8), channel_id=1, source_target_pairs={{0,12},{4,0},{8,4},{12,8},{1,13},{5,1},{9,5},{13,9},{2,14},{6,2},{... | collective-permute-start | bytes 331784 | tf_op jit(solution)/shard_map/ppermute | solution.py:190
  14.9 25.7 %collective-permute-start.1 = (f16[72,768]{1,0:T(8,128)(2,1)}, f16[72,768]{1,0:T(8,128)(2,1)}, u32[]{:S(2)}, u32[]{:S(2)}) collective-permute-start(f16[72,768]{1,0:T(8,128)(2,1)} %get-tuple-element.9), channel_id=1, source_target_pairs={{0,8},{4,12},{8,0},{12,4},{1,9},{5,13},{9,1},{13,5},{2,10},{6,14},... | collective-permute-start | bytes 331784 | tf_op jit(solution)/shard_map/ppermute | solution.py:190
  14.9 26.6 %collective-permute-start = (f16[72,768]{1,0:T(8,128)(2,1)}, f16[72,768]{1,0:T(8,128)(2,1)}, u32[]{:S(2)}, u32[]{:S(2)}) collective-permute-start(f16[72,768]{1,0:T(8,128)(2,1)} %get-tuple-element.10), channel_id=1, source_target_pairs={{0,4},{4,8},{8,12},{12,0},{1,5},{5,9},{9,13},{13,1},{2,6},{6,10},{... | collective-permute-start | bytes 331784 | tf_op jit(solution)/shard_map/ppermute | solution.py:190
  27.8 45.9 %copy-start.2 = (bf16[1024,1024]{1,0:T(8,128)(2,1)S(1)}, bf16[1024,1024]{1,0:T(8,128)(2,1)}, u32[]{:S(2)}) copy-start(bf16[1024,1024]{1,0:T(8,128)(2,1)} %refs_4_.1) | copy-start | bytes 6291460
  39.8 0.7 copy-start.3
  44.4 6.4 %collective-permute-start.5 = (f16[72,768]{1,0:T(8,128)(2,1)S(1)}, f16[72,768]{1,0:T(8,128)(2,1)S(1)}, u32[]{:S(2)}, u32[]{:S(2)}) collective-permute-start(f16[72,768]{1,0:T(8,128)(2,1)S(1)} %select_convert_fusion), channel_id=1, source_target_pairs={{0,12},{4,0},{8,4},{12,8},{1,13},{5,1},{9,5},{13,9},{2,14},{6,2},{... | collective-permute-start | bytes 331784 | tf_op jit(solution)/shard_map/ppermute | solution.py:199
  47.2 10.2 %collective-permute-start.4 = (f16[72,768]{1,0:T(8,128)(2,1)S(1)}, f16[72,768]{1,0:T(8,128)(2,1)S(1)}, u32[]{:S(2)}, u32[]{:S(2)}) collective-permute-start(f16[72,768]{1,0:T(8,128)(2,1)S(1)} %select_convert_fusion), channel_id=1, source_target_pairs={{0,8},{4,12},{8,0},{12,4},{1,9},{5,13},{9,1},{13,5},{2,10},{6,14},... | collective-permute-start | bytes 331784 | tf_op jit(solution)/shard_map/ppermute | solution.py:199
  48.4 9.1 %collective-permute-start.3 = (f16[72,768]{1,0:T(8,128)(2,1)S(1)}, f16[72,768]{1,0:T(8,128)(2,1)S(1)}, u32[]{:S(2)}, u32[]{:S(2)}) collective-permute-start(f16[72,768]{1,0:T(8,128)(2,1)S(1)} %select_convert_fusion), channel_id=1, source_target_pairs={{0,4},{4,8},{8,12},{12,0},{1,5},{5,9},{9,13},{13,1},{2,6},{6,10},{... | collective-permute-start | bytes 331784 | tf_op jit(solution)/shard_map/ppermute | solution.py:199
  57.7 1.0 %copy-start.4 = (bf16[1536,128]{1,0:T(8,128)(2,1)S(1)}, bf16[1536,128]{1,0:T(8,128)(2,1)}, u32[]{:S(2)}) copy-start(bf16[1536,128]{1,0:T(8,128)(2,1)} %copy-done.3) | copy-start | bytes 1179652
  62.3 4.0 %collective-permute-start.8 = (f32[8,1024]{1,0:T(8,128)S(1)}, f32[8,1024]{1,0:T(8,128)S(1)}, u32[]{:S(2)}, u32[]{:S(2)}) collective-permute-start(f32[8,1024]{1,0:T(8,128)S(1)} %get-tuple-element.21), channel_id=1, source_target_pairs={{0,12},{4,0},{8,4},{12,8},{1,13},{5,1},{9,5},{13,9},{2,14},{6,2},{... | collective-permute-start | bytes 98312 | tf_op jit(solution)/shard_map/ppermute | solution.py:210
  63.1 5.0 %collective-permute-start.7 = (f32[8,1024]{1,0:T(8,128)S(1)}, f32[8,1024]{1,0:T(8,128)S(1)}, u32[]{:S(2)}, u32[]{:S(2)}) collective-permute-start(f32[8,1024]{1,0:T(8,128)S(1)} %get-tuple-element.22), channel_id=1, source_target_pairs={{0,8},{4,12},{8,0},{12,4},{1,9},{5,13},{9,1},{13,5},{2,10},{6,14},... | collective-permute-start | bytes 98312 | tf_op jit(solution)/shard_map/ppermute | solution.py:210
  63.9 5.7 %collective-permute-start.6 = (f32[8,1024]{1,0:T(8,128)S(1)}, f32[8,1024]{1,0:T(8,128)S(1)}, u32[]{:S(2)}, u32[]{:S(2)}) collective-permute-start(f32[8,1024]{1,0:T(8,128)S(1)} %get-tuple-element.20), channel_id=1, source_target_pairs={{0,4},{4,8},{8,12},{12,0},{1,5},{5,9},{9,13},{13,1},{2,6},{6,10},{... | collective-permute-start | bytes 98312 | tf_op jit(solution)/shard_map/ppermute | solution.py:210
  69.6 3.4 %collective-permute-start.9 = (f32[8,1024]{1,0:T(8,128)S(1)}, f32[8,1024]{1,0:T(8,128)S(1)}, u32[]{:S(2)}, u32[]{:S(2)}) collective-permute-start(f32[8,1024]{1,0:T(8,128)S(1)} %fusion.1.refs_0_), channel_id=1, source_target_pairs={{0,1},{1,2},{2,3},{3,0},{4,5},{5,6},{6,7},{7,4},{8,9},{9,10},{10,1... | collective-permute-start | bytes 98312 | tf_op jit(solution)/shard_map/ppermute | solution.py:211
  69.6 4.0 %collective-permute-start.10 = (f32[8,1024]{1,0:T(8,128)S(1)}, f32[8,1024]{1,0:T(8,128)S(1)}, u32[]{:S(2)}, u32[]{:S(2)}) collective-permute-start(f32[8,1024]{1,0:T(8,128)S(1)} %fusion.1.refs_0_), channel_id=1, source_target_pairs={{0,2},{1,3},{2,0},{3,1},{4,6},{5,7},{6,4},{7,5},{8,10},{9,11},{10,... | collective-permute-start | bytes 98312 | tf_op jit(solution)/shard_map/ppermute | solution.py:211
  70.2 3.4 %collective-permute-start.11 = (f32[8,1024]{1,0:T(8,128)S(1)}, f32[8,1024]{1,0:T(8,128)S(1)}, u32[]{:S(2)}, u32[]{:S(2)}) collective-permute-start(f32[8,1024]{1,0:T(8,128)S(1)} %fusion.1.refs_0_), channel_id=1, source_target_pairs={{0,3},{1,0},{2,1},{3,2},{4,7},{5,4},{6,5},{7,6},{8,11},{9,8},{10,9... | collective-permute-start | bytes 98312 | tf_op jit(solution)/shard_map/ppermute | solution.py:211
  74.5 7.2 %collective-permute-start.15 = (f32[8,1152]{1,0:T(8,128)S(1)}, f32[8,1152]{1,0:T(8,128)S(1)}, u32[]{:S(2)}, u32[]{:S(2)}) collective-permute-start(f32[8,1152]{1,0:T(8,128)S(1)} %get-tuple-element.17), channel_id=1, source_target_pairs={{0,3},{1,7},{2,11},{3,15},{4,0},{5,4},{6,8},{7,12},{8,1},{9,5},{10... | collective-permute-start | bytes 110600 | tf_op jit(solution)/shard_map/ppermute | solution.py:221
  75.6 6.0 %collective-permute-start.14 = (f32[8,1152]{1,0:T(8,128)S(1)}, f32[8,1152]{1,0:T(8,128)S(1)}, u32[]{:S(2)}, u32[]{:S(2)}) collective-permute-start(f32[8,1152]{1,0:T(8,128)S(1)} %get-tuple-element.18), channel_id=1, source_target_pairs={{0,2},{1,6},{2,10},{3,14},{4,3},{5,7},{6,11},{7,15},{8,0},{9,4},{1... | collective-permute-start | bytes 110600 | tf_op jit(solution)/shard_map/ppermute | solution.py:221
  76.2 7.9 %collective-permute-start.12 = (f32[8,1152]{1,0:T(8,128)S(1)}, f32[8,1152]{1,0:T(8,128)S(1)}, u32[]{:S(2)}, u32[]{:S(2)}) collective-permute-start(f32[8,1152]{1,0:T(8,128)S(1)} %get-tuple-element.19), channel_id=1, source_target_pairs={{0,0},{1,4},{2,8},{3,12},{4,1},{5,5},{6,9},{7,13},{8,2},{9,6},{10,... | collective-permute-start | bytes 110600 | tf_op jit(solution)/shard_map/ppermute | solution.py:221
  81.6 4.9 %collective-permute-start.13 = (f32[8,1152]{1,0:T(8,128)S(1)}, f32[8,1152]{1,0:T(8,128)S(1)}, u32[]{:S(2)}, u32[]{:S(2)}) collective-permute-start(f32[8,1152]{1,0:T(8,128)S(1)} %get-tuple-element.16), channel_id=1, source_target_pairs={{0,1},{1,5},{2,9},{3,13},{4,2},{5,6},{6,10},{7,14},{8,3},{9,7},{10... | collective-permute-start | bytes 110600 | tf_op jit(solution)/shard_map/ppermute | solution.py:221

commit v2 on v1

--- a/solution.py
+++ b/solution.py
@@ -9,6 +9,7 @@
 
 TOP = 14.0
 EXTRA = 8
+UNITS = 4
 NT = (((1,), (1,)), ((), ()))
 NN = (((1,), (0,)), ((), ()))
 
@@ -35,103 +36,105 @@
         out_specs=pl.BlockSpec((rank + EXTRA, slots), lambda l: (0, l)),
         out_shape=jax.ShapeDtypeStruct((rank + EXTRA, lists * slots), jnp.float32),
         cost_estimate=pl.CostEstimate(flops=8 * lists * slots * width * rank, bytes_accessed=2 * out_grads.size, transcendentals=0),
-        compiler_params=pltpu.CompilerParams(vmem_limit_bytes=40 << 20),
+        compiler_params=pltpu.CompilerParams(vmem_limit_bytes=52 << 20),
         name="project_right",
     )(out_grads, basis)
 
 
-def left_kernel(first, depth, lengths, acts, basis, out, total):
-    step = pl.program_id(1)
-    rank = basis.shape[0]
-    columns = pl.ds(pl.multiple_of(step * depth, depth), depth)
-    part = lax.dot_general(acts[0], basis[:, columns], NT, preferred_element_type=jnp.float32)
-
-    @pl.when(step == 0)
-    def _():
-        total[...] = part
-
-    @pl.when(step > 0)
-    def _():
-        total[...] += part
-
-    @pl.when(step == pl.num_programs(1) - 1)
-    def _():
-        count = lengths[pl.program_id(0) + first]
-        rows = lax.broadcasted_iota(jnp.int32, total.shape, 0)
-        left = jnp.where(rows < count, total[...], 0.0)
-        head = left.astype(jnp.bfloat16)
-        out[:, :rank] = head
-        out[:, rank:] = (left - head.astype(jnp.float32)).astype(jnp.bfloat16)
-
-
-def project_left(activations, basis, lengths, first, lists, cuts):
+def left_kernel(first, lists, lengths, acts, basis, out, held, arrived):
+    rank = basis.shape[0]
+    depth, slots = held.shape[:2]
+    pieces = arrived.shape[1]
+    rows = slots // pieces
+    unit = slots // UNITS
+
+    def each(l, slot, act):
+        for piece in range(pieces):
+            @pl.when(piece * rows < lengths[first + l])
+            def _():
+                part = pl.ds(piece * rows, rows)
+                act(pltpu.make_async_copy(acts.at[first + l, part, :], held.at[slot, part, :], arrived.at[slot, piece]))
+
+    for l in range(min(depth, lists)):
+        each(l, l, lambda copy: copy.start())
+    out[...] = jnp.zeros_like(out)
+
+    def step(l, carry):
+        slot = lax.rem(l, depth)
+        each(l, slot, lambda copy: copy.wait())
+        count = lengths[first + l]
+        for units in range(1, UNITS + 1):
+            @pl.when((count + unit - 1) // unit == units)
+            def _():
+                size = units * unit
+                left = lax.dot_general(held[slot, :size, :], basis[...], NT, preferred_element_type=jnp.float32)
+                row = lax.broadcasted_iota(jnp.int32, left.shape, 0)
+                left = jnp.where(row < count, left, 0.0)
+                head = left.astype(jnp.bfloat16)
+                place = pl.ds(pl.multiple_of(l * slots, slots), size)
+                out[place, :rank] = head
+                out[place, rank:] = (left - head.astype(jnp.float32)).astype(jnp.bfloat16)
+
+        @pl.when(l + depth < lists)
+        def _():
+            each(l + depth, slot, lambda copy: copy.start())
+        return carry
+
+    lax.fori_loop(0, lists, step, 0)
+
+
+def project_left(activations, basis, lengths, first, lists):
     slots, width = activations.shape[1:]
     rank = basis.shape[0]
-    depth = width // cuts
-    return pl.pallas_call(
-        functools.partial(left_kernel, first, depth),
-        grid_spec=pltpu.PrefetchScalarGridSpec(
-            num_scalar_prefetch=1,
-            grid=(lists, cuts),
-            in_specs=[
-                pl.BlockSpec((1, slots, depth), lambda l, k, _: (l + first, 0, k)),
-                pl.BlockSpec((rank, width), lambda l, k, _: (0, 0)),
-            ],
-            out_specs=pl.BlockSpec((slots, 2 * rank), lambda l, k, _: (l, 0)),
-            scratch_shapes=[pltpu.VMEM((slots, rank), jnp.float32)],
-        ),
+    depth, pieces = 3, slots // 64
+    return pl.pallas_call(
+        functools.partial(left_kernel, first, lists),
+        in_specs=[
+            pl.BlockSpec(memory_space=pltpu.SMEM),
+            pl.BlockSpec(memory_space=pl.ANY),
+            pl.BlockSpec(memory_space=pltpu.VMEM),
+        ],
+        out_specs=pl.BlockSpec(memory_space=pltpu.VMEM),
         out_shape=jax.ShapeDtypeStruct((lists * slots, 2 * rank), jnp.bfloat16),
+        scratch_shapes=[pltpu.VMEM((depth, slots, width), activations.dtype), pltpu.SemaphoreType.DMA((depth, pieces))],
         cost_estimate=pl.CostEstimate(flops=8 * lists * slots * width * rank, bytes_accessed=2 * lists * slots * width, transcendentals=0),
-        compiler_params=pltpu.CompilerParams(vmem_limit_bytes=40 << 20),
+        compiler_params=pltpu.CompilerParams(vmem_limit_bytes=32 << 20),
         name="project_left",
     )(lengths, activations, basis)
 
 
-def sketch_kernel(unit, per_list, half, where, rights, left_a, left_b, out, sums):
-    rank = sums.shape[1]
+def sketch_kernel(where, rights, left_a, left_b, out, both, sums):
+    lists, rank = sums.shape[:2]
     width = rights.shape[2]
-    sums[...] = jnp.zeros_like(sums)
+    slots = both.shape[1] // lists
     for block in range(rights.shape[0]):
         value = rights[block]
         head = value.astype(jnp.bfloat16)
-        both = jnp.concatenate([head, (value - head.astype(jnp.float32)).astype(jnp.bfloat16)], axis=0)
-        for piece in range(width // unit):
-            index = where[block] * (width // unit) + piece
-            right = both[:, piece * unit:(piece + 1) * unit]
-
-            def add(left_ref, start):
-                left = left_ref[pl.ds(pl.multiple_of(start * unit, unit), unit), :]
-                full = lax.dot_general(right, left, NN, preferred_element_type=jnp.float32)
-                side = full[:rank] + full[rank:]
-                sums[index // per_list] += side[:, :rank] + side[:, rank:]
-
-            @pl.when(index < half)
-            def _():
-                add(left_a, index)
-
-            @pl.when(index >= half)
-            def _():
-                add(left_b, index - half)
-
-    for l in range(sums.shape[0]):
-        sums[l] = sums[l].T
+        columns = pl.ds(pl.multiple_of(where[block] * width, width), width)
+        both[:rank, columns] = head
+        both[rank:, columns] = (value - head.astype(jnp.float32)).astype(jnp.bfloat16)
+    early = left_a.shape[0] // slots
+    for l in range(lists):
+        left = left_a[l * slots:(l + 1) * slots] if l < early else left_b[(l - early) * slots:(l - early + 1) * slots]
+        full = lax.dot_general(both[:, l * slots:(l + 1) * slots], left, NN, preferred_element_type=jnp.float32)
+        side = full[:rank] + full[rank:]
+        sums[l] = (side[:, :rank] + side[:, rank:]).T
     rows = out.shape[2] // rank
     for i in range(rank):
         column = (i % rows) * rank
-        out[i // rows, :sums.shape[0], column:column + rank] = sums[:, i, :]
+        out[i // rows, :lists, column:column + rank] = sums[:, i, :]
 
 
 def sketch_terms(where, rights, left_a, left_b, lists, slots, groups):
     rank = rights.shape[1]
-    unit = slots // 2
     vmem = pl.BlockSpec(memory_space=pltpu.VMEM)
     return pl.pallas_call(
-        functools.partial(sketch_kernel, unit, slots // unit, left_a.shape[0] // unit),
+        sketch_kernel,
         in_specs=[pl.BlockSpec(memory_space=pltpu.SMEM), vmem, vmem, vmem],
         out_specs=vmem,
         out_shape=jax.ShapeDtypeStruct((groups, 8, rank * rank // groups), jnp.float32),
-        scratch_shapes=[pltpu.VMEM((lists, rank, rank), jnp.float32)],
-        compiler_params=pltpu.CompilerParams(vmem_limit_bytes=40 << 20),
+        scratch_shapes=[pltpu.VMEM((2 * rank, lists * slots), jnp.bfloat16), pltpu.VMEM((lists, rank, rank), jnp.float32)],
+        compiler_params=pltpu.CompilerParams(vmem_limit_bytes=32 << 20),
         name="sketch_terms",
     )(where, rights, left_a, left_b)
 
@@ -189,15 +192,16 @@
 
     arrived = [lax.ppermute(part(shift), "tensor", ring(groups, shift)) for shift in shifts]
     early = lists // 2
-    left_a = project_left(activations, proj_in.T, lengths, 0, early, 2)
+    left_a = project_left(activations, proj_in.T, lengths, 0, early)
     pieces = [part(0)] + arrived
     wide = [p.astype(jnp.float32) for p in pieces]
     summed = sum(w * jnp.exp2(w[rank:rank + 1] - TOP) for w in wide)
     exponent = functools.reduce(jnp.maximum, [w[rank:rank + 1] for w in wide]) + (groups - 1).bit_length()
     row = lax.broadcasted_iota(jnp.int32, summed.shape, 0)
     mine = jnp.where(row < rank, summed * jnp.exp2(TOP - exponent), exponent).astype(jnp.float16)
+    mine, later = lax.optimization_barrier((mine, lengths))
     blocks = [mine] + [lax.ppermute(mine, "tensor", ring(groups, shift)) for shift in shifts]
-    left_b = project_left(activations, proj_in.T, lengths, early, lists - early, 2)
+    left_b = project_left(activations, proj_in.T, later, early, lists - early)
     rights = decoded(jnp.stack(blocks), rank)
     where = (me - jnp.arange(groups, dtype=jnp.int32)) % groups
     terms = sketch_terms(where, rights, left_a, left_b, lists, slots, groups)

time: 88.7 us -> 67.3 us (0.76)
  waiting for transfers between devices: 19.7 us -> 12.7 us
  local copies, waits for them, and re-layouts: 7.34 us -> 1.1 us
  other arithmetic: 5.82 us -> 1.45 us
  Pallas kernels: 32.9 us -> 29.1 us
    ppermute x3, waiting for transfers between devices: 9.04 us -> 0.01 us  [local_square(): lax.ppermute(mine, 'tensor', ring(groups, shift))]
    pallas_call x3, Pallas kernels: 27.4 us -> 20 us  [the longest x2 18.7 us: project_left(): pl.pallas_call(functools.partial(left_kernel, first, lists), in_specs=[pl...]
    unnamed x17 -> x9, local copies, waits for them, and re-layouts: 7.29 us -> 1.05 us
    pallas_call x1, Pallas kernels: 4.73 us -> 8.27 us  [project_right(): pl.pallas_call(right_kernel, grid=(lists,), in_specs=[pl.BlockSpec((1, sl...]
    convert_element_type x4, other arithmetic: 2.76 us -> 0.13 us  [local_square(): wide = [p.astype(jnp.float32) for p in pieces]]
    ppermute x3, waiting for transfers between devices: 3.76 us -> 5.08 us  [local_square(): lax.ppermute(towards(terms, (me + shift) % groups), 'tensor', ring(groups...]
    convert_element_type x1, other arithmetic: 1.13 us -> 0.13 us  [local_square(): jnp.where(row < rank, summed * jnp.exp2(TOP - exponent), exponent)]
  transfers between devices with their start and end apart: 16 -> 16, of which waited for: 9 -> 8; matrix products, arithmetic and copies ran while one was open for 1% -> 0% of each run, Pallas kernels for 27% -> 28%
where the time goes in v2:
time: 67.3 us; the launch traced here: 66.6 us
  Pallas kernels  29.1 us (43%)
  starting transfers between devices  22 us (33%)
  waiting for transfers between devices  12.7 us (19%)
  other arithmetic  1.45 us (2%)
  local copies, waits for them, and re-layouts  1.1 us (2%)
    pallas_call x2, Pallas kernels, project_left(): pl.pallas_call(functools.partial(left_kernel, first, lists), in_specs=[pl...  18.7 us
    pallas_call x1, Pallas kernels, project_right(): pl.pallas_call(right_kernel, grid=(lists,), in_specs=[pl.BlockSpec((1, sl...  8.27 us
    ppermute x4, starting transfers between devices, local_square(): lax.ppermute(towards(scores, (here - target) % groups), ('tensor', 'examp...  7.17 us
    ppermute x4, waiting for transfers between devices, local_square(): lax.ppermute(towards(scores, (here - target) % groups), ('tensor', 'examp...  5.22 us
    ppermute x3, waiting for transfers between devices, local_square(): lax.ppermute(towards(terms, (me + shift) % groups), 'tensor', ring(groups...  5.08 us
    ppermute x3, starting transfers between devices, local_square(): lax.ppermute(part(shift), 'tensor', ring(groups, shift))  4.67 us
    ppermute x3, starting transfers between devices, local_square(): lax.ppermute(mine, 'tensor', ring(groups, shift))  4.45 us
    ppermute x3, starting transfers between devices, local_square(): lax.ppermute(towards(terms, (me + shift) % groups), 'tensor', ring(groups...  3.91 us
  transfers between devices with their start and end apart: 16, of which 8 were waited for; matrix products, arithmetic and copies ran while one was open for 0% of the time, Pallas kernels for 28%

profile of v2, /device:TPU:2, one launch (start us, length us, event | category | flops | bytes accessed | tf_op | source)
XLA Modules:
  0.0 66.6 jit_solution(5816264160209393396)
XLA Ops:
  0.0 1.0 %copy-done.2 = bf16[2048,64]{0,1:T(8,128)(2,1)S(1)} copy-done((bf16[2048,64]{0,1:T(8,128)(2,1)S(1)}, bf16[2048,64]{0,1:T(8,128)(2,1)}, u32[]{:S(2)}) %copy-start.2) | copy-done | bytes 262168
  1.0 8.3 %project_right.1 = f32[72,3072]{1,0:T(8,128)S(1)} custom-call(bf16[6,512,2048]{2,1,0:T(8,128)(2,1)} %grads.1, bf16[64,2048]{1,0:T(8,128)(2,1)S(1)} %bitcast.31), custom_call_target="tpu_custom_call" | custom-call | flops 3221225472 | bytes 12582912 | tf_op jit(solution)/shard_map/project_right/pallas_call | solution.py:29
  9.4 0.1 dynamic-slice_convert_fusion
  9.5 3.7 %collective-permute-start.2 = (f16[72,768]{1,0:T(8,128)(2,1)S(1)}, f16[72,768]{1,0:T(8,128)(2,1)S(1)}, u32[]{:S(2)}, u32[]{:S(2)}) collective-permute-start(f16[72,768]{1,0:T(8,128)(2,1)S(1)} %get-tuple-element.12), channel_id=1, source_target_pairs={{0,12},{4,0},{8,4},{12,8},{1,13},{5,1},{9,5},{13,9},{2,14},{6,2},{... | collective-permute-start | bytes 331784 | tf_op jit(solution)/shard_map/ppermute | solution.py:193
  13.1 1.0 %collective-permute-start = (f16[72,768]{1,0:T(8,128)(2,1)S(1)}, f16[72,768]{1,0:T(8,128)(2,1)S(1)}, u32[]{:S(2)}, u32[]{:S(2)}) collective-permute-start(f16[72,768]{1,0:T(8,128)(2,1)S(1)} %get-tuple-element.14), channel_id=1, source_target_pairs={{0,4},{4,8},{8,12},{12,0},{1,5},{5,9},{9,13},{13,1},{2,6},{6,10},{... | collective-permute-start | bytes 331784 | tf_op jit(solution)/shard_map/ppermute | solution.py:193
  14.2 8.4 %project_left.2.left_a = bf16[1536,128]{1,0:T(8,128)(2,1)S(1)} custom-call(s32[6]{0:T(128)S(1)} %copy-done.3, bf16[6,512,7168]{2,1,0:T(8,128)(2,1)} %acts.3, bf16[64,7168]{1,0:T(8,128)(2,1)S(1)} %bitcast.29), custom_call_target="tpu_custom_call" | custom-call | flops 5637144576 | bytes 22020096 | tf_op jit(solution)/shard_map/project_left/pallas_call | solution.py:90
  22.6 0.2 collective-permute-done.1
  23.0 0.1 select_convert_fusion
  23.1 2.7 %collective-permute-start.5 = (f16[72,768]{1,0:T(8,128)(2,1)S(1)}, f16[72,768]{1,0:T(8,128)(2,1)S(1)}, u32[]{:S(2)}, u32[]{:S(2)}) collective-permute-start(f16[72,768]{1,0:T(8,128)(2,1)S(1)} %select_convert_fusion), channel_id=1, source_target_pairs={{0,12},{4,0},{8,4},{12,8},{1,13},{5,1},{9,5},{13,9},{2,14},{6,2},{... | collective-permute-start | bytes 331784 | tf_op jit(solution)/shard_map/ppermute | solution.py:203
  25.8 1.1 %collective-permute-start.4 = (f16[72,768]{1,0:T(8,128)(2,1)S(1)}, f16[72,768]{1,0:T(8,128)(2,1)S(1)}, u32[]{:S(2)}, u32[]{:S(2)}) collective-permute-start(f16[72,768]{1,0:T(8,128)(2,1)S(1)} %select_convert_fusion), channel_id=1, source_target_pairs={{0,8},{4,12},{8,0},{12,4},{1,9},{5,13},{9,1},{13,5},{2,10},{6,14},... | collective-permute-start | bytes 331784 | tf_op jit(solution)/shard_map/ppermute | solution.py:203
  26.9 0.6 collective-permute-start.3
  27.5 10.3 %project_left.3.left_b = bf16[1536,128]{1,0:T(8,128)(2,1)S(1)} custom-call(s32[6]{0:T(128)S(1)} %copy-done.3, bf16[6,512,7168]{2,1,0:T(8,128)(2,1)} %acts.3, bf16[64,7168]{1,0:T(8,128)(2,1)S(1)} %bitcast.30), custom_call_target="tpu_custom_call" | custom-call | flops 5637144576 | bytes 22020096 | tf_op jit(solution)/shard_map/project_left/pallas_call | solution.py:90
  37.9 0.1 maximum_convert_fusion
  38.1 1.3 %sketch_terms.1 = f32[4,8,1024]{2,1,0:T(8,128)S(1)} custom-call(s32[4]{0:T(128)S(1)} %and_select_fusion.where, f32[4,64,768]{2,1,0:T(8,128)S(1)} %slice_multiply_fusion.rights, bf16[1536,128]{1,0:T(8,128)(2,1)S(1)} %project_left.2.left_a, bf16[1536,128]{1,0:T(8,128)(2,1)S(1)} %project_left.3.left_b), custom_call_target="tpu_custom_call" | custom-call | tf_op jit(solution)/shard_map/sketch_terms/pallas_call | solution.py:131
  39.5 3.3 %collective-permute-start.8 = (f32[8,1024]{1,0:T(8,128)S(1)}, f32[8,1024]{1,0:T(8,128)S(1)}, u32[]{:S(2)}, u32[]{:S(2)}) collective-permute-start(f32[8,1024]{1,0:T(8,128)S(1)} %get-tuple-element.25), channel_id=1, source_target_pairs={{0,12},{4,0},{8,4},{12,8},{1,13},{5,1},{9,5},{13,9},{2,14},{6,2},{... | collective-permute-start | bytes 98312 | tf_op jit(solution)/shard_map/ppermute | solution.py:214
  42.8 0.6 collective-permute-start.6
  43.4 1.0 %collective-permute-done.8 = f32[8,1024]{1,0:T(8,128)S(1)} collective-permute-done((f32[8,1024]{1,0:T(8,128)S(1)}, f32[8,1024]{1,0:T(8,128)S(1)}, u32[]{:S(2)}, u32[]{:S(2)}) %collective-permute-start.8) | collective-permute-done | bytes 32800 | tf_op jit(solution)/shard_map/ppermute | solution.py:214
  44.4 3.2 %collective-permute-done.7 = f32[8,1024]{1,0:T(8,128)S(1)} collective-permute-done((f32[8,1024]{1,0:T(8,128)S(1)}, f32[8,1024]{1,0:T(8,128)S(1)}, u32[]{:S(2)}, u32[]{:S(2)}) %collective-permute-start.7) | collective-permute-done | bytes 32800 | tf_op jit(solution)/shard_map/ppermute | solution.py:214
  47.6 0.9 %collective-permute-done.6 = f32[8,1024]{1,0:T(8,128)S(1)} collective-permute-done((f32[8,1024]{1,0:T(8,128)S(1)}, f32[8,1024]{1,0:T(8,128)S(1)}, u32[]{:S(2)}, u32[]{:S(2)}) %collective-permute-start.6) | collective-permute-done | bytes 32800 | tf_op jit(solution)/shard_map/ppermute | solution.py:214
  48.6 0.1 collective-permute-start.10
  48.6 1.7 %collective-permute-start.11 = (f32[8,1024]{1,0:T(8,128)S(1)}, f32[8,1024]{1,0:T(8,128)S(1)}, u32[]{:S(2)}, u32[]{:S(2)}) collective-permute-start(f32[8,1024]{1,0:T(8,128)S(1)} %fusion.1.refs_0_), channel_id=1, source_target_pairs={{0,3},{1,0},{2,1},{3,2},{4,7},{5,4},{6,5},{7,6},{8,11},{9,8},{10,9... | collective-permute-start | bytes 98312 | tf_op jit(solution)/shard_map/ppermute | solution.py:215
  50.3 1.6 %collective-permute-done.9.refs_1_ = f32[8,1024]{1,0:T(8,128)S(1)} collective-permute-done((f32[8,1024]{1,0:T(8,128)S(1)}, f32[8,1024]{1,0:T(8,128)S(1)}, u32[]{:S(2)}, u32[]{:S(2)}) %collective-permute-start.9) | collective-permute-done | bytes 32800 | tf_op jit(solution)/shard_map/ppermute | solution.py:215
  51.9 0.7 %collective-permute-done.10.refs_2_ = f32[8,1024]{1,0:T(8,128)S(1)} collective-permute-done((f32[8,1024]{1,0:T(8,128)S(1)}, f32[8,1024]{1,0:T(8,128)S(1)}, u32[]{:S(2)}, u32[]{:S(2)}) %collective-permute-start.10) | collective-permute-done | bytes 32800 | tf_op jit(solution)/shard_map/ppermute | solution.py:215
  52.6 0.7 %score_terms.1 = f32[4,8,1152]{2,1,0:T(8,128)S(1)} custom-call(f32[8,1024]{1,0:T(8,128)S(1)} %fusion.1.refs_0_, f32[8,1024]{1,0:T(8,128)S(1)} %collective-permute-done.9.refs_1_, f32[8,1024]{1,0:T(8,128)S(1)} %collective-permute-done.10.refs_2_, f32[8,1024]{1,0:T(8,128)S(1)} %collective-permute-done.11.refs_3_, bf16[1024,1024]{1,0:T(8,128)(2,1)S(1)} %copy-done.1), custom_call_target="tpu_custom_call" | custom-call | tf_op jit(solution)/shard_map/score_terms/pallas_call | solution.py:159
  53.4 1.9 %collective-permute-start.15 = (f32[8,1152]{1,0:T(8,128)S(1)}, f32[8,1152]{1,0:T(8,128)S(1)}, u32[]{:S(2)}, u32[]{:S(2)}) collective-permute-start(f32[8,1152]{1,0:T(8,128)S(1)} %get-tuple-element.21), channel_id=1, source_target_pairs={{0,3},{1,7},{2,11},{3,15},{4,0},{5,4},{6,8},{7,12},{8,1},{9,5},{10... | collective-permute-start | bytes 110600 | tf_op jit(solution)/shard_map/ppermute | solution.py:225
  55.3 0.3 collective-permute-start.14
  55.6 4.9 %collective-permute-start.12 = (f32[8,1152]{1,0:T(8,128)S(1)}, f32[8,1152]{1,0:T(8,128)S(1)}, u32[]{:S(2)}, u32[]{:S(2)}) collective-permute-start(f32[8,1152]{1,0:T(8,128)S(1)} %get-tuple-element.23), channel_id=1, source_target_pairs={{0,0},{1,4},{2,8},{3,12},{4,1},{5,5},{6,9},{7,13},{8,2},{9,6},{10,... | collective-permute-start | bytes 110600 | tf_op jit(solution)/shard_map/ppermute | solution.py:225
  60.5 0.1 collective-permute-start.13
  60.6 2.7 %collective-permute-done.12 = f32[8,1152]{1,0:T(8,128)S(1)} collective-permute-done((f32[8,1152]{1,0:T(8,128)S(1)}, f32[8,1152]{1,0:T(8,128)S(1)}, u32[]{:S(2)}, u32[]{:S(2)}) %collective-permute-start.12) | collective-permute-done | bytes 36896 | tf_op jit(solution)/shard_map/ppermute | solution.py:225
  63.3 2.5 %collective-permute-done.13 = f32[8,1152]{1,0:T(8,128)S(1)} collective-permute-done((f32[8,1152]{1,0:T(8,128)S(1)}, f32[8,1152]{1,0:T(8,128)S(1)}, u32[]{:S(2)}, u32[]{:S(2)}) %collective-permute-start.13) | collective-permute-done | bytes 36896 | tf_op jit(solution)/shard_map/ppermute | solution.py:225
  65.8 0.1 fusion.5
  65.9 0.7 %slice_multiply_fusion.1 = f32[6,1024]{1,0:T(8,128)} fusion(f32[8,1152]{1,0:T(8,128)S(1)} %add_add_fusion, f32[6]{0:T(128)S(1)} %fusion.5), kind=kLoop, calls=%fused_computation.9 | loop fusion | flops 6144 | bytes 49176 | tf_op jit(solution)/shard_map/mul | solution.py:228
  (33 shorter events, 0.5 us)
Async XLA Ops:
  0.0 14.2 %copy-start = (bf16[7168,64]{0,1:T(8,128)(2,1)S(1)}, bf16[7168,64]{0,1:T(8,128)(2,1)}, u32[]{:S(2)}) copy-start(bf16[7168,64]{0,1:T(8,128)(2,1)} %param.9) | copy-start | bytes 2752516
  0.0 1.0 %copy-start.2 = (bf16[2048,64]{0,1:T(8,128)(2,1)S(1)}, bf16[2048,64]{0,1:T(8,128)(2,1)}, u32[]{:S(2)}) copy-start(bf16[2048,64]{0,1:T(8,128)(2,1)} %param.10) | copy-start | bytes 786436
  1.0 13.1 %copy-start.3 = (s32[6]{0:T(128)S(1)}, s32[6]{0:T(128)}, u32[]{:S(2)}) copy-start(s32[6]{0:T(128)} %lengths.2) | copy-start | bytes 76
  9.5 13.1 %collective-permute-start.2 = (f16[72,768]{1,0:T(8,128)(2,1)S(1)}, f16[72,768]{1,0:T(8,128)(2,1)S(1)}, u32[]{:S(2)}, u32[]{:S(2)}) collective-permute-start(f16[72,768]{1,0:T(8,128)(2,1)S(1)} %get-tuple-element.12), channel_id=1, source_target_pairs={{0,12},{4,0},{8,4},{12,8},{1,13},{5,1},{9,5},{13,9},{2,14},{6,2},{... | collective-permute-start | bytes 331784 | tf_op jit(solution)/shard_map/ppermute | solution.py:193
  13.1 9.7 %collective-permute-start.1 = (f16[72,768]{1,0:T(8,128)(2,1)S(1)}, f16[72,768]{1,0:T(8,128)(2,1)S(1)}, u32[]{:S(2)}, u32[]{:S(2)}) collective-permute-start(f16[72,768]{1,0:T(8,128)(2,1)S(1)} %get-tuple-element.13), channel_id=1, source_target_pairs={{0,8},{4,12},{8,0},{12,4},{1,9},{5,13},{9,1},{13,5},{2,10},{6,14},... | collective-permute-start | bytes 331784 | tf_op jit(solution)/shard_map/ppermute | solution.py:193
  13.1 9.7 %collective-permute-start = (f16[72,768]{1,0:T(8,128)(2,1)S(1)}, f16[72,768]{1,0:T(8,128)(2,1)S(1)}, u32[]{:S(2)}, u32[]{:S(2)}) collective-permute-start(f16[72,768]{1,0:T(8,128)(2,1)S(1)} %get-tuple-element.14), channel_id=1, source_target_pairs={{0,4},{4,8},{8,12},{12,0},{1,5},{5,9},{9,13},{13,1},{2,6},{6,10},{... | collective-permute-start | bytes 331784 | tf_op jit(solution)/shard_map/ppermute | solution.py:193
  23.1 29.5 %copy-start.1 = (bf16[1024,1024]{1,0:T(8,128)(2,1)S(1)}, bf16[1024,1024]{1,0:T(8,128)(2,1)}, u32[]{:S(2)}) copy-start(bf16[1024,1024]{1,0:T(8,128)(2,1)} %refs_4_.1) | copy-start | bytes 6291460
  23.1 14.7 %collective-permute-start.5 = (f16[72,768]{1,0:T(8,128)(2,1)S(1)}, f16[72,768]{1,0:T(8,128)(2,1)S(1)}, u32[]{:S(2)}, u32[]{:S(2)}) collective-permute-start(f16[72,768]{1,0:T(8,128)(2,1)S(1)} %select_convert_fusion), channel_id=1, source_target_pairs={{0,12},{4,0},{8,4},{12,8},{1,13},{5,1},{9,5},{13,9},{2,14},{6,2},{... | collective-permute-start | bytes 331784 | tf_op jit(solution)/shard_map/ppermute | solution.py:203
  25.8 12.0 %collective-permute-start.4 = (f16[72,768]{1,0:T(8,128)(2,1)S(1)}, f16[72,768]{1,0:T(8,128)(2,1)S(1)}, u32[]{:S(2)}, u32[]{:S(2)}) collective-permute-start(f16[72,768]{1,0:T(8,128)(2,1)S(1)} %select_convert_fusion), channel_id=1, source_target_pairs={{0,8},{4,12},{8,0},{12,4},{1,9},{5,13},{9,1},{13,5},{2,10},{6,14},... | collective-permute-start | bytes 331784 | tf_op jit(solution)/shard_map/ppermute | solution.py:203
  26.9 10.9 %collective-permute-start.3 = (f16[72,768]{1,0:T(8,128)(2,1)S(1)}, f16[72,768]{1,0:T(8,128)(2,1)S(1)}, u32[]{:S(2)}, u32[]{:S(2)}) collective-permute-start(f16[72,768]{1,0:T(8,128)(2,1)S(1)} %select_convert_fusion), channel_id=1, source_target_pairs={{0,4},{4,8},{8,12},{12,0},{1,5},{5,9},{9,13},{13,1},{2,6},{6,10},{... | collective-permute-start | bytes 331784 | tf_op jit(solution)/shard_map/ppermute | solution.py:203
  39.5 4.9 %collective-permute-start.8 = (f32[8,1024]{1,0:T(8,128)S(1)}, f32[8,1024]{1,0:T(8,128)S(1)}, u32[]{:S(2)}, u32[]{:S(2)}) collective-permute-start(f32[8,1024]{1,0:T(8,128)S(1)} %get-tuple-element.25), channel_id=1, source_target_pairs={{0,12},{4,0},{8,4},{12,8},{1,13},{5,1},{9,5},{13,9},{2,14},{6,2},{... | collective-permute-start | bytes 98312 | tf_op jit(solution)/shard_map/ppermute | solution.py:214
  42.8 4.8 %collective-permute-start.7 = (f32[8,1024]{1,0:T(8,128)S(1)}, f32[8,1024]{1,0:T(8,128)S(1)}, u32[]{:S(2)}, u32[]{:S(2)}) collective-permute-start(f32[8,1024]{1,0:T(8,128)S(1)} %get-tuple-element.26), channel_id=1, source_target_pairs={{0,8},{4,12},{8,0},{12,4},{1,9},{5,13},{9,1},{13,5},{2,10},{6,14},... | collective-permute-start | bytes 98312 | tf_op jit(solution)/shard_map/ppermute | solution.py:214
  42.8 5.7 %collective-permute-start.6 = (f32[8,1024]{1,0:T(8,128)S(1)}, f32[8,1024]{1,0:T(8,128)S(1)}, u32[]{:S(2)}, u32[]{:S(2)}) collective-permute-start(f32[8,1024]{1,0:T(8,128)S(1)} %get-tuple-element.24), channel_id=1, source_target_pairs={{0,4},{4,8},{8,12},{12,0},{1,5},{5,9},{9,13},{13,1},{2,6},{6,10},{... | collective-permute-start | bytes 98312 | tf_op jit(solution)/shard_map/ppermute | solution.py:214
  48.5 3.4 %collective-permute-start.9 = (f32[8,1024]{1,0:T(8,128)S(1)}, f32[8,1024]{1,0:T(8,128)S(1)}, u32[]{:S(2)}, u32[]{:S(2)}) collective-permute-start(f32[8,1024]{1,0:T(8,128)S(1)} %fusion.1.refs_0_), channel_id=1, source_target_pairs={{0,1},{1,2},{2,3},{3,0},{4,5},{5,6},{6,7},{7,4},{8,9},{9,10},{10,1... | collective-permute-start | bytes 98312 | tf_op jit(solution)/shard_map/ppermute | solution.py:215
  48.6 4.0 %collective-permute-start.10 = (f32[8,1024]{1,0:T(8,128)S(1)}, f32[8,1024]{1,0:T(8,128)S(1)}, u32[]{:S(2)}, u32[]{:S(2)}) collective-permute-start(f32[8,1024]{1,0:T(8,128)S(1)} %fusion.1.refs_0_), channel_id=1, source_target_pairs={{0,2},{1,3},{2,0},{3,1},{4,6},{5,7},{6,4},{7,5},{8,10},{9,11},{10,... | collective-permute-start | bytes 98312 | tf_op jit(solution)/shard_map/ppermute | solution.py:215
  48.6 4.0 %collective-permute-start.11 = (f32[8,1024]{1,0:T(8,128)S(1)}, f32[8,1024]{1,0:T(8,128)S(1)}, u32[]{:S(2)}, u32[]{:S(2)}) collective-permute-start(f32[8,1024]{1,0:T(8,128)S(1)} %fusion.1.refs_0_), channel_id=1, source_target_pairs={{0,3},{1,0},{2,1},{3,2},{4,7},{5,4},{6,5},{7,6},{8,11},{9,8},{10,9... | collective-permute-start | bytes 98312 | tf_op jit(solution)/shard_map/ppermute | solution.py:215
  53.4 7.2 %collective-permute-start.15 = (f32[8,1152]{1,0:T(8,128)S(1)}, f32[8,1152]{1,0:T(8,128)S(1)}, u32[]{:S(2)}, u32[]{:S(2)}) collective-permute-start(f32[8,1152]{1,0:T(8,128)S(1)} %get-tuple-element.21), channel_id=1, source_target_pairs={{0,3},{1,7},{2,11},{3,15},{4,0},{5,4},{6,8},{7,12},{8,1},{9,5},{10... | collective-permute-start | bytes 110600 | tf_op jit(solution)/shard_map/ppermute | solution.py:225
  55.3 5.3 %collective-permute-start.14 = (f32[8,1152]{1,0:T(8,128)S(1)}, f32[8,1152]{1,0:T(8,128)S(1)}, u32[]{:S(2)}, u32[]{:S(2)}) collective-permute-start(f32[8,1152]{1,0:T(8,128)S(1)} %get-tuple-element.22), channel_id=1, source_target_pairs={{0,2},{1,6},{2,10},{3,14},{4,3},{5,7},{6,11},{7,15},{8,0},{9,4},{1... | collective-permute-start | bytes 110600 | tf_op jit(solution)/shard_map/ppermute | solution.py:225
  55.6 7.6 %collective-permute-start.12 = (f32[8,1152]{1,0:T(8,128)S(1)}, f32[8,1152]{1,0:T(8,128)S(1)}, u32[]{:S(2)}, u32[]{:S(2)}) collective-permute-start(f32[8,1152]{1,0:T(8,128)S(1)} %get-tuple-element.23), channel_id=1, source_target_pairs={{0,0},{1,4},{2,8},{3,12},{4,1},{5,5},{6,9},{7,13},{8,2},{9,6},{10,... | collective-permute-start | bytes 110600 | tf_op jit(solution)/shard_map/ppermute | solution.py:225
  60.5 5.3 %collective-permute-start.13 = (f32[8,1152]{1,0:T(8,128)S(1)}, f32[8,1152]{1,0:T(8,128)S(1)}, u32[]{:S(2)}, u32[]{:S(2)}) collective-permute-start(f32[8,1152]{1,0:T(8,128)S(1)} %get-tuple-element.20), channel_id=1, source_target_pairs={{0,1},{1,5},{2,9},{3,13},{4,2},{5,6},{6,10},{7,14},{8,3},{9,7},{10... | collective-permute-start | bytes 110600 | tf_op jit(solution)/shard_map/ppermute | solution.py:225

commit v3 on v2

--- a/solution.py
+++ b/solution.py
@@ -9,86 +9,118 @@
 
 TOP = 14.0
 EXTRA = 8
+LANES = 128
 UNITS = 4
 NT = (((1,), (1,)), ((), ()))
 NN = (((1,), (0,)), ((), ()))
 
 
-def right_kernel(grads, basis, out):
+def leveled(value):
+    largest = jnp.max(jnp.abs(value), axis=1, keepdims=True)
+    exponent = jnp.ceil(jnp.log2(jnp.maximum(largest, 1e-30)))
+    return value * jnp.exp2(TOP - exponent), exponent
+
+
+def right_kernel(grads, basis, out, held, weights, arrived):
     rank = basis.shape[0]
-    right = lax.dot_general(grads[0], basis[...], NT, preferred_element_type=jnp.float32).T
-    largest = jnp.max(jnp.abs(right), axis=0, keepdims=True)
-    exponent = jnp.ceil(jnp.log2(jnp.maximum(largest, 1e-30)))
-    out[:rank] = right * jnp.exp2(TOP - exponent)
-    out[rank:] = jnp.broadcast_to(exponent, (EXTRA, right.shape[1]))
+    lists, slots = held.shape[:2]
+    load = pltpu.make_async_copy(basis, weights, arrived.at[lists])
+    load.start()
+
+    def copy(l):
+        return pltpu.make_async_copy(grads.at[l], held.at[l], arrived.at[l])
+
+    for l in range(lists):
+        copy(l).start()
+    load.wait()
+
+    def step(l, carry):
+        copy(l).wait()
+        right = lax.dot_general(held[l], weights[...], NT, preferred_element_type=jnp.float32).T
+        largest = jnp.max(jnp.abs(right), axis=0, keepdims=True)
+        exponent = jnp.ceil(jnp.log2(jnp.maximum(largest, 1e-30)))
+        columns = pl.ds(pl.multiple_of(l * slots, slots), slots)
+        out[:rank, columns] = right * jnp.exp2(TOP - exponent)
+        out[rank:, columns] = jnp.broadcast_to(exponent, (EXTRA, slots))
+        return carry
+
+    lax.fori_loop(0, lists, step, 0)
 
 
 def project_right(out_grads, basis):
-    lists, slots, width = out_grads.shape
+    slots, width = out_grads.shape[1:]
     rank = basis.shape[0]
+    tokens = out_grads.shape[0] * slots
+    pieces = out_grads.reshape(tokens // slots, slots, width)
     return pl.pallas_call(
         right_kernel,
-        grid=(lists,),
-        in_specs=[
-            pl.BlockSpec((1, slots, width), lambda l: (l, 0, 0)),
-            pl.BlockSpec((rank, width), lambda l: (0, 0)),
+        in_specs=[pl.BlockSpec(memory_space=pl.ANY)] * 2,
+        out_specs=pl.BlockSpec(memory_space=pltpu.VMEM),
+        out_shape=jax.ShapeDtypeStruct((rank + EXTRA, tokens), jnp.float32),
+        scratch_shapes=[
+            pltpu.VMEM(pieces.shape, out_grads.dtype),
+            pltpu.VMEM(basis.shape, basis.dtype),
+            pltpu.SemaphoreType.DMA((pieces.shape[0] + 1,)),
         ],
-        out_specs=pl.BlockSpec((rank + EXTRA, slots), lambda l: (0, l)),
-        out_shape=jax.ShapeDtypeStruct((rank + EXTRA, lists * slots), jnp.float32),
-        cost_estimate=pl.CostEstimate(flops=8 * lists * slots * width * rank, bytes_accessed=2 * out_grads.size, transcendentals=0),
+        cost_estimate=pl.CostEstimate(flops=8 * tokens * width * rank, bytes_accessed=2 * out_grads.size, transcendentals=0),
         compiler_params=pltpu.CompilerParams(vmem_limit_bytes=52 << 20),
         name="project_right",
-    )(out_grads, basis)
-
-
-def left_kernel(first, lists, lengths, acts, basis, out, held, arrived):
+    )(pieces, basis)
+
+
+def left_kernel(first, slots, lengths, acts, basis, out, held, arrived):
     rank = basis.shape[0]
-    depth, slots = held.shape[:2]
+    depth, size = held.shape[:2]
     pieces = arrived.shape[1]
-    rows = slots // pieces
-    unit = slots // UNITS
-
-    def each(l, slot, act):
+    rows, unit = size // pieces, size // UNITS
+    steps = out.shape[0] // size
+    cuts = slots // size
+
+    def count_of(n):
+        return lengths[first + n // cuts] - n % cuts * size
+
+    def each(n, slot, act):
+        count = count_of(n)
         for piece in range(pieces):
-            @pl.when(piece * rows < lengths[first + l])
+            @pl.when(piece * rows < count)
             def _():
-                part = pl.ds(piece * rows, rows)
-                act(pltpu.make_async_copy(acts.at[first + l, part, :], held.at[slot, part, :], arrived.at[slot, piece]))
-
-    for l in range(min(depth, lists)):
-        each(l, l, lambda copy: copy.start())
+                source = pl.ds(pl.multiple_of(n % cuts * size + piece * rows, rows), rows)
+                act(pltpu.make_async_copy(acts.at[first + n // cuts, source, :], held.at[slot, pl.ds(piece * rows, rows), :], arrived.at[slot, piece]))
+
+    for n in range(min(depth, steps)):
+        each(n, n, lambda copy: copy.start())
     out[...] = jnp.zeros_like(out)
 
-    def step(l, carry):
-        slot = lax.rem(l, depth)
-        each(l, slot, lambda copy: copy.wait())
-        count = lengths[first + l]
+    def step(n, carry):
+        slot = lax.rem(n, depth)
+        each(n, slot, lambda copy: copy.wait())
+        count = count_of(n)
+        needed = jnp.minimum((count + unit - 1) // unit, UNITS)
         for units in range(1, UNITS + 1):
-            @pl.when((count + unit - 1) // unit == units)
+            @pl.when(needed == units)
             def _():
-                size = units * unit
-                left = lax.dot_general(held[slot, :size, :], basis[...], NT, preferred_element_type=jnp.float32)
+                left = lax.dot_general(held[slot, :units * unit, :], basis[...], NT, preferred_element_type=jnp.float32)
                 row = lax.broadcasted_iota(jnp.int32, left.shape, 0)
                 left = jnp.where(row < count, left, 0.0)
                 head = left.astype(jnp.bfloat16)
-                place = pl.ds(pl.multiple_of(l * slots, slots), size)
+                place = pl.ds(pl.multiple_of(n * size, size), units * unit)
                 out[place, :rank] = head
                 out[place, rank:] = (left - head.astype(jnp.float32)).astype(jnp.bfloat16)
 
-        @pl.when(l + depth < lists)
+        @pl.when(n + depth < steps)
         def _():
-            each(l + depth, slot, lambda copy: copy.start())
+            each(n + depth, slot, lambda copy: copy.start())
         return carry
 
-    lax.fori_loop(0, lists, step, 0)
+    lax.fori_loop(0, steps, step, 0)
 
 
 def project_left(activations, basis, lengths, first, lists):
     slots, width = activations.shape[1:]
     rank = basis.shape[0]
-    depth, pieces = 3, slots // 64
+    size, depth = 256, 6
     return pl.pallas_call(
-        functools.partial(left_kernel, first, lists),
+        functools.partial(left_kernel, first, slots),
         in_specs=[
             pl.BlockSpec(memory_space=pltpu.SMEM),
             pl.BlockSpec(memory_space=pl.ANY),
@@ -96,14 +128,15 @@
         ],
         out_specs=pl.BlockSpec(memory_space=pltpu.VMEM),
         out_shape=jax.ShapeDtypeStruct((lists * slots, 2 * rank), jnp.bfloat16),
-        scratch_shapes=[pltpu.VMEM((depth, slots, width), activations.dtype), pltpu.SemaphoreType.DMA((depth, pieces))],
+        scratch_shapes=[pltpu.VMEM((depth, size, width), activations.dtype), pltpu.SemaphoreType.DMA((depth, size // 64))],
         cost_estimate=pl.CostEstimate(flops=8 * lists * slots * width * rank, bytes_accessed=2 * lists * slots * width, transcendentals=0),
-        compiler_params=pltpu.CompilerParams(vmem_limit_bytes=32 << 20),
+        compiler_params=pltpu.CompilerParams(vmem_limit_bytes=36 << 20),
         name="project_left",
     )(lengths, activations, basis)
 
 
 def sketch_kernel(where, rights, left_a, left_b, out, both, sums):
+    out[...] = jnp.zeros_like(out)
     lists, rank = sums.shape[:2]
     width = rights.shape[2]
     slots = both.shape[1] // lists
@@ -119,10 +152,14 @@
         full = lax.dot_general(both[:, l * slots:(l + 1) * slots], left, NN, preferred_element_type=jnp.float32)
         side = full[:rank] + full[rank:]
         sums[l] = (side[:, :rank] + side[:, rank:]).T
-    rows = out.shape[2] // rank
+    rows = rank // out.shape[0]
     for i in range(rank):
         column = (i % rows) * rank
         out[i // rows, :lists, column:column + rank] = sums[:, i, :]
+    for group in range(out.shape[0]):
+        scaled, exponent = leveled(out[group, :lists, :rows * rank])
+        out[group, :lists, :rows * rank] = scaled
+        out[group, :lists, rows * rank:] = jnp.broadcast_to(exponent, (lists, LANES))
 
 
 def sketch_terms(where, rights, left_a, left_b, lists, slots, groups):
@@ -132,7 +169,7 @@
         sketch_kernel,
         in_specs=[pl.BlockSpec(memory_space=pltpu.SMEM), vmem, vmem, vmem],
         out_specs=vmem,
-        out_shape=jax.ShapeDtypeStruct((groups, 8, rank * rank // groups), jnp.float32),
+        out_shape=jax.ShapeDtypeStruct((groups, 8, rank * rank // groups + LANES), jnp.float32),
         scratch_shapes=[pltpu.VMEM((2 * rank, lists * slots), jnp.bfloat16), pltpu.VMEM((lists, rank, rank), jnp.float32)],
         compiler_params=pltpu.CompilerParams(vmem_limit_bytes=32 << 20),
         name="sketch_terms",
@@ -149,9 +186,13 @@
     rows = value.shape[0]
     terms = full[:rows] + full[rows:]
     squares = jnp.sum(value * value, axis=1, keepdims=True)
+    scaled, exponent = leveled(terms)
+    square, power = leveled(squares)
+    lane = lax.broadcasted_iota(jnp.int32, (rows, LANES), 1)
+    notes = jnp.where(lane == 0, exponent, jnp.where(lane == 1, square, power))
     for group in range(len(sketches)):
-        out[group, :, :count] = terms[group * 8:group * 8 + 8]
-        out[group, :, count:] = jnp.broadcast_to(squares[group * 8:group * 8 + 8], (8, 128))
+        out[group, :, :count] = scaled[group * 8:group * 8 + 8]
+        out[group, :, count:] = notes[group * 8:group * 8 + 8]
 
 
 def score_terms(sketches, queries):
@@ -160,7 +201,7 @@
         score_kernel,
         in_specs=[vmem] * (len(sketches) + 1),
         out_specs=vmem,
-        out_shape=jax.ShapeDtypeStruct((len(sketches), 8, queries.shape[0] + 128), jnp.float32),
+        out_shape=jax.ShapeDtypeStruct((len(sketches), 8, queries.shape[0] + LANES), jnp.float32),
         compiler_params=pltpu.CompilerParams(vmem_limit_bytes=40 << 20),
         name="score_terms",
     )(*sketches, queries)
@@ -209,23 +250,31 @@
     def towards(array, index):
         return lax.dynamic_index_in_dim(array, index, 0, keepdims=False)
 
-    sketch = towards(terms, me)
-    for shift in shifts:
-        sketch = sketch + lax.ppermute(towards(terms, (me + shift) % groups), "tensor", ring(groups, shift))
+    coded = terms.astype(jnp.float16)
+    entries = rank * rank // groups
+    sketch = None
+    for shift in range(groups):
+        piece = towards(coded, (me + shift) % groups)
+        if shift:
+            piece = lax.ppermute(piece, "tensor", ring(groups, shift))
+        piece = piece.astype(jnp.float32)
+        piece = piece[:, :entries] * jnp.exp2(piece[:, entries:entries + 1] - TOP)
+        sketch = piece if sketch is None else sketch + piece
     sketches = [sketch] + [lax.ppermute(sketch, "example", ring(groups, shift)) for shift in shifts]
-    scores = score_terms(sketches, queries)
+    scores = score_terms(sketches, queries).astype(jnp.float16)
+    count = queries.shape[0]
     here = lax.axis_index("example")
-    final = None
+    final, square = 0.0, 0.0
     for shift in range(groups):
         target = (me + shift) % groups
         pairs = [
             (t * groups + e, e * groups + (t + shift) % groups)
             for t in range(groups) for e in range(groups)
         ]
-        moved = lax.ppermute(towards(scores, (here - target) % groups), ("tensor", "example"), pairs)
-        final = moved if final is None else final + moved
-    count = queries.shape[0]
-    return final[:lists, :count] * lax.rsqrt(final[:lists, count:count + 1] + 1e-06)
+        moved = lax.ppermute(towards(scores, (here - target) % groups), ("tensor", "example"), pairs).astype(jnp.float32)
+        final += moved[:lists, :count] * jnp.exp2(moved[:lists, count:count + 1] - TOP)
+        square += moved[:lists, count + 1:count + 2] * jnp.exp2(moved[:lists, count + 2:count + 3] - TOP)
+    return final * lax.rsqrt(square + 1e-06)
 
 
 def local(activations, out_grads, lengths, proj_in, proj_out, queries):

time: 67.3 us -> 63.4 us (0.942)
  Pallas kernels: 29.1 us -> 25.3 us
  waiting for transfers between devices: 12.7 us -> 9.44 us
  starting transfers between devices: 22 us -> 24.1 us
  other arithmetic: 1.45 us -> 2.21 us
    pallas_call x3, Pallas kernels: 27 us -> 23 us  [the longest x2 16.7 us: project_left(): pl.pallas_call(functools.partial(left_kernel, first, slots), in_specs=[pl...]
    ppermute x4, waiting for transfers between devices: 5.22 us -> 2.98 us  [local_square(): lax.ppermute(towards(scores, (here - target) % groups), ('tensor', 'examp...]
    ppermute x3, starting transfers between devices: 1.82 us -> 3.15 us  [local_square(): lax.ppermute(sketch, 'example', ring(groups, shift))]
    ppermute x4, starting transfers between devices: 7.17 us -> 8.08 us  [local_square(): lax.ppermute(towards(scores, (here - target) % groups), ('tensor', 'examp...]
    ppermute x3, waiting for transfers between devices: 5.08 us -> 4.26 us  [local_square(): piece = lax.ppermute(piece, 'tensor', ring(groups, shift))]
    exp2 x0 -> x5, other arithmetic: none -> 0.72 us  [the longest x4 0.48 us: local_square(): piece = piece[:, :entries] * jnp.exp2(piece[:, entries:entries + 1] - TOP)]
  transfers between devices with their start and end apart: 16 -> 16, of which waited for: 8 -> 8; matrix products, arithmetic and copies ran while one was open for 0% -> 1% of each run, Pallas kernels for 28% -> 27%
where the time goes in v3:
time: 63.4 us; the launch traced here: 62.5 us
  Pallas kernels  25.3 us (40%)
  starting transfers between devices  24.1 us (38%)
  waiting for transfers between devices  9.44 us (15%)
  other arithmetic  2.21 us (3%)
  local copies, waits for them, and re-layouts  1.08 us (2%)
    pallas_call x2, Pallas kernels, project_left(): pl.pallas_call(functools.partial(left_kernel, first, slots), in_specs=[pl...  16.7 us
    ppermute x4, starting transfers between devices, local_square(): lax.ppermute(towards(scores, (here - target) % groups), ('tensor', 'examp...  8.08 us
    pallas_call x1, Pallas kernels, project_right(): pl.pallas_call(right_kernel, in_specs=[pl.BlockSpec(memory_space=pl.ANY)]...  6.32 us
    ppermute x3, starting transfers between devices, local_square(): lax.ppermute(part(shift), 'tensor', ring(groups, shift))  4.67 us
    ppermute x3, starting transfers between devices, local_square(): lax.ppermute(mine, 'tensor', ring(groups, shift))  4.44 us
    ppermute x3, waiting for transfers between devices, local_square(): piece = lax.ppermute(piece, 'tensor', ring(groups, shift))  4.26 us
    ppermute x3, starting transfers between devices, local_square(): piece = lax.ppermute(piece, 'tensor', ring(groups, shift))  3.8 us
    ppermute x3, starting transfers between devices, local_square(): lax.ppermute(sketch, 'example', ring(groups, shift))  3.15 us
  transfers between devices with their start and end apart: 16, of which 8 were waited for; matrix products, arithmetic and copies ran while one was open for 1% of the time, Pallas kernels for 27%

profile of v3, /device:TPU:2, one launch (start us, length us, event | category | flops | bytes accessed | tf_op | source)
XLA Modules:
  0.0 62.5 jit_solution(2168658201784321542)
XLA Ops:
  0.0 1.0 %copy-done.2 = bf16[2048,64]{0,1:T(8,128)(2,1)S(1)} copy-done((bf16[2048,64]{0,1:T(8,128)(2,1)S(1)}, bf16[2048,64]{0,1:T(8,128)(2,1)}, u32[]{:S(2)}) %copy-start.2) | copy-done | bytes 262168
  1.0 6.3 %project_right.1 = f32[72,3072]{1,0:T(8,128)S(1)} custom-call(bf16[6,512,2048]{2,1,0:T(8,128)(2,1)} %grads.1, bf16[64,2048]{1,0:T(8,128)(2,1)S(1)} %bitcast.28), custom_call_target="tpu_custom_call" | custom-call | flops 3221225472 | bytes 12582912 | tf_op jit(solution)/shard_map/project_right/pallas_call | solution.py:55
  7.5 3.7 %collective-permute-start.2 = (f16[72,768]{1,0:T(8,128)(2,1)S(1)}, f16[72,768]{1,0:T(8,128)(2,1)S(1)}, u32[]{:S(2)}, u32[]{:S(2)}) collective-permute-start(f16[72,768]{1,0:T(8,128)(2,1)S(1)} %get-tuple-element.17), channel_id=1, source_target_pairs={{0,12},{4,0},{8,4},{12,8},{1,13},{5,1},{9,5},{13,9},{2,14},{6,2},{... | collective-permute-start | bytes 331784 | tf_op jit(solution)/shard_map/ppermute | solution.py:234
  11.2 1.0 %collective-permute-start = (f16[72,768]{1,0:T(8,128)(2,1)S(1)}, f16[72,768]{1,0:T(8,128)(2,1)S(1)}, u32[]{:S(2)}, u32[]{:S(2)}) collective-permute-start(f16[72,768]{1,0:T(8,128)(2,1)S(1)} %get-tuple-element.19), channel_id=1, source_target_pairs={{0,4},{4,8},{8,12},{12,0},{1,5},{5,9},{9,13},{13,1},{2,6},{6,10},{... | collective-permute-start | bytes 331784 | tf_op jit(solution)/shard_map/ppermute | solution.py:234
  12.2 8.6 %project_left.2.left_a = bf16[1536,128]{1,0:T(8,128)(2,1)S(1)} custom-call(s32[6]{0:T(128)S(1)} %copy-done.3, bf16[6,512,7168]{2,1,0:T(8,128)(2,1)} %acts.3, bf16[64,7168]{1,0:T(8,128)(2,1)S(1)} %bitcast.26), custom_call_target="tpu_custom_call" | custom-call | flops 5637144576 | bytes 22020096 | tf_op jit(solution)/shard_map/project_left/pallas_call | solution.py:122
  21.0 0.1 select_convert_fusion
  21.2 2.9 %collective-permute-start.5 = (f16[72,768]{1,0:T(8,128)(2,1)S(1)}, f16[72,768]{1,0:T(8,128)(2,1)S(1)}, u32[]{:S(2)}, u32[]{:S(2)}) collective-permute-start(f16[72,768]{1,0:T(8,128)(2,1)S(1)} %select_convert_fusion), channel_id=1, source_target_pairs={{0,12},{4,0},{8,4},{12,8},{1,13},{5,1},{9,5},{13,9},{2,14},{6,2},{... | collective-permute-start | bytes 331784 | tf_op jit(solution)/shard_map/ppermute | solution.py:244
  24.0 1.1 %collective-permute-start.4 = (f16[72,768]{1,0:T(8,128)(2,1)S(1)}, f16[72,768]{1,0:T(8,128)(2,1)S(1)}, u32[]{:S(2)}, u32[]{:S(2)}) collective-permute-start(f16[72,768]{1,0:T(8,128)(2,1)S(1)} %select_convert_fusion), channel_id=1, source_target_pairs={{0,8},{4,12},{8,0},{12,4},{1,9},{5,13},{9,1},{13,5},{2,10},{6,14},... | collective-permute-start | bytes 331784 | tf_op jit(solution)/shard_map/ppermute | solution.py:244
  25.2 0.4 collective-permute-start.3
  25.6 8.1 %project_left.3.left_b = bf16[1536,128]{1,0:T(8,128)(2,1)S(1)} custom-call(s32[6]{0:T(128)S(1)} %copy-done.3, bf16[6,512,7168]{2,1,0:T(8,128)(2,1)} %acts.3, bf16[64,7168]{1,0:T(8,128)(2,1)S(1)} %bitcast.27), custom_call_target="tpu_custom_call" | custom-call | flops 5637144576 | bytes 22020096 | tf_op jit(solution)/shard_map/project_left/pallas_call | solution.py:122
  33.7 0.6 collective-permute-done.4
  34.6 1.4 %sketch_terms.1 = f32[4,8,1152]{2,1,0:T(8,128)S(1)} custom-call(s32[4]{0:T(128)S(1)} %and_select_fusion.where, f32[4,64,768]{2,1,0:T(8,128)S(1)} %slice_multiply_fusion.rights, bf16[1536,128]{1,0:T(8,128)(2,1)S(1)} %project_left.2.left_a, bf16[1536,128]{1,0:T(8,128)(2,1)S(1)} %project_left.3.left_b), custom_call_target="tpu_custom_call" | custom-call | tf_op jit(solution)/shard_map/sketch_terms/pallas_call | solution.py:168
  36.1 2.9 %collective-permute-start.8 = (f16[8,1152]{1,0:T(8,128)(2,1)S(1)}, f16[8,1152]{1,0:T(8,128)(2,1)S(1)}, u32[]{:S(2)}, u32[]{:S(2)}) collective-permute-start(f16[8,1152]{1,0:T(8,128)(2,1)S(1)} %get-tuple-element.30), channel_id=1, source_target_pairs={{0,12},{4,0},{8,4},{12,8},{1,13},{5,1},{9,5},{13,9},{2,14},{6,2},{... | collective-permute-start | bytes 55304 | tf_op jit(solution)/shard_map/ppermute | solution.py:259
  39.0 0.9 %collective-permute-start.6 = (f16[8,1152]{1,0:T(8,128)(2,1)S(1)}, f16[8,1152]{1,0:T(8,128)(2,1)S(1)}, u32[]{:S(2)}, u32[]{:S(2)}) collective-permute-start(f16[8,1152]{1,0:T(8,128)(2,1)S(1)} %get-tuple-element.32), channel_id=1, source_target_pairs={{0,4},{4,8},{8,12},{12,0},{1,5},{5,9},{9,13},{13,1},{2,6},{6,10},{... | collective-permute-start | bytes 55304 | tf_op jit(solution)/shard_map/ppermute | solution.py:259
  40.0 0.4 collective-permute-done.8
  40.4 0.1 fusion.41
  40.5 3.1 %collective-permute-done.7 = f16[8,1152]{1,0:T(8,128)(2,1)S(1)} collective-permute-done((f16[8,1152]{1,0:T(8,128)(2,1)S(1)}, f16[8,1152]{1,0:T(8,128)(2,1)S(1)}, u32[]{:S(2)}, u32[]{:S(2)}) %collective-permute-start.7) | collective-permute-done | bytes 18464 | tf_op jit(solution)/shard_map/ppermute | solution.py:259
  43.6 0.1 fusion.44
  43.7 0.8 %collective-permute-done.6 = f16[8,1152]{1,0:T(8,128)(2,1)S(1)} collective-permute-done((f16[8,1152]{1,0:T(8,128)(2,1)S(1)}, f16[8,1152]{1,0:T(8,128)(2,1)S(1)}, u32[]{:S(2)}, u32[]{:S(2)}) %collective-permute-start.6) | collective-permute-done | bytes 18464 | tf_op jit(solution)/shard_map/ppermute | solution.py:259
  44.8 1.7 %collective-permute-start.10 = (f32[8,1024]{1,0:T(8,128)S(1)}, f32[8,1024]{1,0:T(8,128)S(1)}, u32[]{:S(2)}, u32[]{:S(2)}) collective-permute-start(f32[8,1024]{1,0:T(8,128)S(1)} %fusion.4.refs_0_), channel_id=1, source_target_pairs={{0,2},{1,3},{2,0},{3,1},{4,6},{5,7},{6,4},{7,5},{8,10},{9,11},{10,... | collective-permute-start | bytes 98312 | tf_op jit(solution)/shard_map/ppermute | solution.py:263
  46.5 1.4 %collective-permute-start.11 = (f32[8,1024]{1,0:T(8,128)S(1)}, f32[8,1024]{1,0:T(8,128)S(1)}, u32[]{:S(2)}, u32[]{:S(2)}) collective-permute-start(f32[8,1024]{1,0:T(8,128)S(1)} %fusion.4.refs_0_), channel_id=1, source_target_pairs={{0,3},{1,0},{2,1},{3,2},{4,7},{5,4},{6,5},{7,6},{8,11},{9,8},{10,9... | collective-permute-start | bytes 98312 | tf_op jit(solution)/shard_map/ppermute | solution.py:263
  47.9 0.2 collective-permute-done.9.refs_1_
  48.1 0.7 %collective-permute-done.10.refs_2_ = f32[8,1024]{1,0:T(8,128)S(1)} collective-permute-done((f32[8,1024]{1,0:T(8,128)S(1)}, f32[8,1024]{1,0:T(8,128)S(1)}, u32[]{:S(2)}, u32[]{:S(2)}) %collective-permute-start.10) | collective-permute-done | bytes 32800 | tf_op jit(solution)/shard_map/ppermute | solution.py:263
  48.8 0.7 %collective-permute-done.11.refs_3_ = f32[8,1024]{1,0:T(8,128)S(1)} collective-permute-done((f32[8,1024]{1,0:T(8,128)S(1)}, f32[8,1024]{1,0:T(8,128)S(1)}, u32[]{:S(2)}, u32[]{:S(2)}) %collective-permute-start.11) | collective-permute-done | bytes 32800 | tf_op jit(solution)/shard_map/ppermute | solution.py:263
  49.5 0.9 %score_terms.1 = f32[4,8,1152]{2,1,0:T(8,128)S(1)} custom-call(f32[8,1024]{1,0:T(8,128)S(1)} %fusion.4.refs_0_, f32[8,1024]{1,0:T(8,128)S(1)} %collective-permute-done.9.refs_1_, f32[8,1024]{1,0:T(8,128)S(1)} %collective-permute-done.10.refs_2_, f32[8,1024]{1,0:T(8,128)S(1)} %collective-permute-done.11.refs_3_, bf16[1024,1024]{1,0:T(8,128)(2,1)S(1)} %copy-done.1), custom_call_target="tpu_custom_call" | custom-call | tf_op jit(solution)/shard_map/score_terms/pallas_call | solution.py:200
  50.4 1.3 %collective-permute-start.15 = (f16[8,1152]{1,0:T(8,128)(2,1)S(1)}, f16[8,1152]{1,0:T(8,128)(2,1)S(1)}, u32[]{:S(2)}, u32[]{:S(2)}) collective-permute-start(f16[8,1152]{1,0:T(8,128)(2,1)S(1)} %get-tuple-element.26), channel_id=1, source_target_pairs={{0,3},{1,7},{2,11},{3,15},{4,0},{5,4},{6,8},{7,12},{8,1},{9,5},{10... | collective-permute-start | bytes 55304 | tf_op jit(solution)/shard_map/ppermute | solution.py:274
  51.7 1.6 %collective-permute-start.14 = (f16[8,1152]{1,0:T(8,128)(2,1)S(1)}, f16[8,1152]{1,0:T(8,128)(2,1)S(1)}, u32[]{:S(2)}, u32[]{:S(2)}) collective-permute-start(f16[8,1152]{1,0:T(8,128)(2,1)S(1)} %get-tuple-element.27), channel_id=1, source_target_pairs={{0,2},{1,6},{2,10},{3,14},{4,3},{5,7},{6,11},{7,15},{8,0},{9,4},{1... | collective-permute-start | bytes 55304 | tf_op jit(solution)/shard_map/ppermute | solution.py:274
  53.3 0.8 %collective-permute-start.13 = (f16[8,1152]{1,0:T(8,128)(2,1)S(1)}, f16[8,1152]{1,0:T(8,128)(2,1)S(1)}, u32[]{:S(2)}, u32[]{:S(2)}) collective-permute-start(f16[8,1152]{1,0:T(8,128)(2,1)S(1)} %get-tuple-element.28), channel_id=1, source_target_pairs={{0,1},{1,5},{2,9},{3,13},{4,2},{5,6},{6,10},{7,14},{8,3},{9,7},{10... | collective-permute-start | bytes 55304 | tf_op jit(solution)/shard_map/ppermute | solution.py:274
  54.1 4.4 %collective-permute-start.12 = (f16[8,1152]{1,0:T(8,128)(2,1)S(1)}, f16[8,1152]{1,0:T(8,128)(2,1)S(1)}, u32[]{:S(2)}, u32[]{:S(2)}) collective-permute-start(f16[8,1152]{1,0:T(8,128)(2,1)S(1)} %get-tuple-element.25), channel_id=1, source_target_pairs={{0,0},{1,4},{2,8},{3,12},{4,1},{5,5},{6,9},{7,13},{8,2},{9,6},{10,... | collective-permute-start | bytes 55304 | tf_op jit(solution)/shard_map/ppermute | solution.py:274
  58.6 3.0 %collective-permute-done.12 = f16[8,1152]{1,0:T(8,128)(2,1)S(1)} collective-permute-done((f16[8,1152]{1,0:T(8,128)(2,1)S(1)}, f16[8,1152]{1,0:T(8,128)(2,1)S(1)}, u32[]{:S(2)}, u32[]{:S(2)}) %collective-permute-start.12) | collective-permute-done | bytes 18464 | tf_op jit(solution)/shard_map/ppermute | solution.py:274
  61.5 0.2 fusion.38
  61.8 0.7 %fusion.1 = f32[6,1024]{1,0:T(8,128)} fusion(f32[8,1152]{1,0:T(8,128)S(1)} %convert_element_type.71, f32[8,1152]{1,0:T(8,128)S(1)} %convert_element_type.70, f32[8,1152]{1,0:T(8,128)S(1)} %convert_element_type.69, f32[8,1152]{1,0:T(8,128)S(1)} %convert_element_type.68, f32[6]{0:T(128)S(1)} %get-tuple-element.10, f32[6]{0:T(128)S(1)} %get-tuple-element.13, ...), kind=kLoop, calls=%fused_computation.6 | loop fusion | flops 49152 | bytes 123000 | tf_op jit(solution)/shard_map/mul | solution.py:277
  (45 shorter events, 1.0 us)
Async XLA Ops:
  0.0 12.2 %copy-start = (bf16[7168,64]{0,1:T(8,128)(2,1)S(1)}, bf16[7168,64]{0,1:T(8,128)(2,1)}, u32[]{:S(2)}) copy-start(bf16[7168,64]{0,1:T(8,128)(2,1)} %param.9) | copy-start | bytes 2752516
  0.0 1.0 %copy-start.2 = (bf16[2048,64]{0,1:T(8,128)(2,1)S(1)}, bf16[2048,64]{0,1:T(8,128)(2,1)}, u32[]{:S(2)}) copy-start(bf16[2048,64]{0,1:T(8,128)(2,1)} %param.10) | copy-start | bytes 786436
  1.0 11.2 %copy-start.3 = (s32[6]{0:T(128)S(1)}, s32[6]{0:T(128)}, u32[]{:S(2)}) copy-start(s32[6]{0:T(128)} %lengths.2) | copy-start | bytes 76
  7.5 13.3 %collective-permute-start.2 = (f16[72,768]{1,0:T(8,128)(2,1)S(1)}, f16[72,768]{1,0:T(8,128)(2,1)S(1)}, u32[]{:S(2)}, u32[]{:S(2)}) collective-permute-start(f16[72,768]{1,0:T(8,128)(2,1)S(1)} %get-tuple-element.17), channel_id=1, source_target_pairs={{0,12},{4,0},{8,4},{12,8},{1,13},{5,1},{9,5},{13,9},{2,14},{6,2},{... | collective-permute-start | bytes 331784 | tf_op jit(solution)/shard_map/ppermute | solution.py:234
  11.2 9.7 %collective-permute-start.1 = (f16[72,768]{1,0:T(8,128)(2,1)S(1)}, f16[72,768]{1,0:T(8,128)(2,1)S(1)}, u32[]{:S(2)}, u32[]{:S(2)}) collective-permute-start(f16[72,768]{1,0:T(8,128)(2,1)S(1)} %get-tuple-element.18), channel_id=1, source_target_pairs={{0,8},{4,12},{8,0},{12,4},{1,9},{5,13},{9,1},{13,5},{2,10},{6,14},... | collective-permute-start | bytes 331784 | tf_op jit(solution)/shard_map/ppermute | solution.py:234
  11.2 9.7 %collective-permute-start = (f16[72,768]{1,0:T(8,128)(2,1)S(1)}, f16[72,768]{1,0:T(8,128)(2,1)S(1)}, u32[]{:S(2)}, u32[]{:S(2)}) collective-permute-start(f16[72,768]{1,0:T(8,128)(2,1)S(1)} %get-tuple-element.19), channel_id=1, source_target_pairs={{0,4},{4,8},{8,12},{12,0},{1,5},{5,9},{9,13},{13,1},{2,6},{6,10},{... | collective-permute-start | bytes 331784 | tf_op jit(solution)/shard_map/ppermute | solution.py:234
  21.1 28.3 %copy-start.1 = (bf16[1024,1024]{1,0:T(8,128)(2,1)S(1)}, bf16[1024,1024]{1,0:T(8,128)(2,1)}, u32[]{:S(2)}) copy-start(bf16[1024,1024]{1,0:T(8,128)(2,1)} %refs_4_.1) | copy-start | bytes 6291460
  21.2 12.6 %collective-permute-start.5 = (f16[72,768]{1,0:T(8,128)(2,1)S(1)}, f16[72,768]{1,0:T(8,128)(2,1)S(1)}, u32[]{:S(2)}, u32[]{:S(2)}) collective-permute-start(f16[72,768]{1,0:T(8,128)(2,1)S(1)} %select_convert_fusion), channel_id=1, source_target_pairs={{0,12},{4,0},{8,4},{12,8},{1,13},{5,1},{9,5},{13,9},{2,14},{6,2},{... | collective-permute-start | bytes 331784 | tf_op jit(solution)/shard_map/ppermute | solution.py:244
  24.0 10.3 %collective-permute-start.4 = (f16[72,768]{1,0:T(8,128)(2,1)S(1)}, f16[72,768]{1,0:T(8,128)(2,1)S(1)}, u32[]{:S(2)}, u32[]{:S(2)}) collective-permute-start(f16[72,768]{1,0:T(8,128)(2,1)S(1)} %select_convert_fusion), channel_id=1, source_target_pairs={{0,8},{4,12},{8,0},{12,4},{1,9},{5,13},{9,1},{13,5},{2,10},{6,14},... | collective-permute-start | bytes 331784 | tf_op jit(solution)/shard_map/ppermute | solution.py:244
  25.2 9.2 %collective-permute-start.3 = (f16[72,768]{1,0:T(8,128)(2,1)S(1)}, f16[72,768]{1,0:T(8,128)(2,1)S(1)}, u32[]{:S(2)}, u32[]{:S(2)}) collective-permute-start(f16[72,768]{1,0:T(8,128)(2,1)S(1)} %select_convert_fusion), channel_id=1, source_target_pairs={{0,4},{4,8},{8,12},{12,0},{1,5},{5,9},{9,13},{13,1},{2,6},{6,10},{... | collective-permute-start | bytes 331784 | tf_op jit(solution)/shard_map/ppermute | solution.py:244
  36.1 4.3 %collective-permute-start.8 = (f16[8,1152]{1,0:T(8,128)(2,1)S(1)}, f16[8,1152]{1,0:T(8,128)(2,1)S(1)}, u32[]{:S(2)}, u32[]{:S(2)}) collective-permute-start(f16[8,1152]{1,0:T(8,128)(2,1)S(1)} %get-tuple-element.30), channel_id=1, source_target_pairs={{0,12},{4,0},{8,4},{12,8},{1,13},{5,1},{9,5},{13,9},{2,14},{6,2},{... | collective-permute-start | bytes 55304 | tf_op jit(solution)/shard_map/ppermute | solution.py:259
  39.0 4.7 %collective-permute-start.7 = (f16[8,1152]{1,0:T(8,128)(2,1)S(1)}, f16[8,1152]{1,0:T(8,128)(2,1)S(1)}, u32[]{:S(2)}, u32[]{:S(2)}) collective-permute-start(f16[8,1152]{1,0:T(8,128)(2,1)S(1)} %get-tuple-element.31), channel_id=1, source_target_pairs={{0,8},{4,12},{8,0},{12,4},{1,9},{5,13},{9,1},{13,5},{2,10},{6,14},... | collective-permute-start | bytes 55304 | tf_op jit(solution)/shard_map/ppermute | solution.py:259
  39.0 5.6 %collective-permute-start.6 = (f16[8,1152]{1,0:T(8,128)(2,1)S(1)}, f16[8,1152]{1,0:T(8,128)(2,1)S(1)}, u32[]{:S(2)}, u32[]{:S(2)}) collective-permute-start(f16[8,1152]{1,0:T(8,128)(2,1)S(1)} %get-tuple-element.32), channel_id=1, source_target_pairs={{0,4},{4,8},{8,12},{12,0},{1,5},{5,9},{9,13},{13,1},{2,6},{6,10},{... | collective-permute-start | bytes 55304 | tf_op jit(solution)/shard_map/ppermute | solution.py:259
  44.7 3.4 %collective-permute-start.9 = (f32[8,1024]{1,0:T(8,128)S(1)}, f32[8,1024]{1,0:T(8,128)S(1)}, u32[]{:S(2)}, u32[]{:S(2)}) collective-permute-start(f32[8,1024]{1,0:T(8,128)S(1)} %fusion.4.refs_0_), channel_id=1, source_target_pairs={{0,1},{1,2},{2,3},{3,0},{4,5},{5,6},{6,7},{7,4},{8,9},{9,10},{10,1... | collective-permute-start | bytes 98312 | tf_op jit(solution)/shard_map/ppermute | solution.py:263
  44.8 4.0 %collective-permute-start.10 = (f32[8,1024]{1,0:T(8,128)S(1)}, f32[8,1024]{1,0:T(8,128)S(1)}, u32[]{:S(2)}, u32[]{:S(2)}) collective-permute-start(f32[8,1024]{1,0:T(8,128)S(1)} %fusion.4.refs_0_), channel_id=1, source_target_pairs={{0,2},{1,3},{2,0},{3,1},{4,6},{5,7},{6,4},{7,5},{8,10},{9,11},{10,... | collective-permute-start | bytes 98312 | tf_op jit(solution)/shard_map/ppermute | solution.py:263
  46.5 3.0 %collective-permute-start.11 = (f32[8,1024]{1,0:T(8,128)S(1)}, f32[8,1024]{1,0:T(8,128)S(1)}, u32[]{:S(2)}, u32[]{:S(2)}) collective-permute-start(f32[8,1024]{1,0:T(8,128)S(1)} %fusion.4.refs_0_), channel_id=1, source_target_pairs={{0,3},{1,0},{2,1},{3,2},{4,7},{5,4},{6,5},{7,6},{8,11},{9,8},{10,9... | collective-permute-start | bytes 98312 | tf_op jit(solution)/shard_map/ppermute | solution.py:263
  50.4 8.1 %collective-permute-start.15 = (f16[8,1152]{1,0:T(8,128)(2,1)S(1)}, f16[8,1152]{1,0:T(8,128)(2,1)S(1)}, u32[]{:S(2)}, u32[]{:S(2)}) collective-permute-start(f16[8,1152]{1,0:T(8,128)(2,1)S(1)} %get-tuple-element.26), channel_id=1, source_target_pairs={{0,3},{1,7},{2,11},{3,15},{4,0},{5,4},{6,8},{7,12},{8,1},{9,5},{10... | collective-permute-start | bytes 55304 | tf_op jit(solution)/shard_map/ppermute | solution.py:274
  51.7 6.8 %collective-permute-start.14 = (f16[8,1152]{1,0:T(8,128)(2,1)S(1)}, f16[8,1152]{1,0:T(8,128)(2,1)S(1)}, u32[]{:S(2)}, u32[]{:S(2)}) collective-permute-start(f16[8,1152]{1,0:T(8,128)(2,1)S(1)} %get-tuple-element.27), channel_id=1, source_target_pairs={{0,2},{1,6},{2,10},{3,14},{4,3},{5,7},{6,11},{7,15},{8,0},{9,4},{1... | collective-permute-start | bytes 55304 | tf_op jit(solution)/shard_map/ppermute | solution.py:274
  53.3 5.2 %collective-permute-start.13 = (f16[8,1152]{1,0:T(8,128)(2,1)S(1)}, f16[8,1152]{1,0:T(8,128)(2,1)S(1)}, u32[]{:S(2)}, u32[]{:S(2)}) collective-permute-start(f16[8,1152]{1,0:T(8,128)(2,1)S(1)} %get-tuple-element.28), channel_id=1, source_target_pairs={{0,1},{1,5},{2,9},{3,13},{4,2},{5,6},{6,10},{7,14},{8,3},{9,7},{10... | collective-permute-start | bytes 55304 | tf_op jit(solution)/shard_map/ppermute | solution.py:274
  54.1 7.4 %collective-permute-start.12 = (f16[8,1152]{1,0:T(8,128)(2,1)S(1)}, f16[8,1152]{1,0:T(8,128)(2,1)S(1)}, u32[]{:S(2)}, u32[]{:S(2)}) collective-permute-start(f16[8,1152]{1,0:T(8,128)(2,1)S(1)} %get-tuple-element.25), channel_id=1, source_target_pairs={{0,0},{1,4},{2,8},{3,12},{4,1},{5,5},{6,9},{7,13},{8,2},{9,6},{10,... | collective-permute-start | bytes 55304 | tf_op jit(solution)/shard_map/ppermute | solution.py:274

commit v4 on v3

--- a/solution.py
+++ b/solution.py
@@ -54,7 +54,7 @@
     pieces = out_grads.reshape(tokens // slots, slots, width)
     return pl.pallas_call(
         right_kernel,
-        in_specs=[pl.BlockSpec(memory_space=pl.ANY)] * 2,
+        in_specs=[pl.BlockSpec(memory_space=pltpu.HBM)] * 2,
         out_specs=pl.BlockSpec(memory_space=pltpu.VMEM),
         out_shape=jax.ShapeDtypeStruct((rank + EXTRA, tokens), jnp.float32),
         scratch_shapes=[
@@ -65,7 +65,7 @@
         cost_estimate=pl.CostEstimate(flops=8 * tokens * width * rank, bytes_accessed=2 * out_grads.size, transcendentals=0),
         compiler_params=pltpu.CompilerParams(vmem_limit_bytes=52 << 20),
         name="project_right",
-    )(pieces, basis)
+    )(pieces, pltpu.with_memory_space_constraint(basis, pltpu.HBM))
 
 
 def left_kernel(first, slots, lengths, acts, basis, out, held, arrived):

time: 63.4 us -> 63.1 us (level)
  the two profiles are of different devices: /device:TPU:2 before, /device:TPU:6 now
where the time goes in v4:
time: 63.1 us; the launch traced here: 63.4 us
  Pallas kernels  27.1 us (43%)
  starting transfers between devices  24.4 us (39%)
  waiting for transfers between devices  9.34 us (15%)
  other arithmetic  2.21 us (4%)
    pallas_call x2, Pallas kernels, project_left(): pl.pallas_call(functools.partial(left_kernel, first, slots), in_specs=[pl...  18.3 us
    ppermute x4, starting transfers between devices, local_square(): lax.ppermute(towards(scores, (here - target) % groups), ('tensor', 'examp...  8.09 us
    pallas_call x1, Pallas kernels, project_right(): pl.pallas_call(right_kernel, in_specs=[pl.BlockSpec(memory_space=pltpu.HB...  6.47 us
    ppermute x3, starting transfers between devices, local_square(): lax.ppermute(part(shift), 'tensor', ring(groups, shift))  4.66 us
    ppermute x3, waiting for transfers between devices, local_square(): piece = lax.ppermute(piece, 'tensor', ring(groups, shift))  4.55 us
    ppermute x3, starting transfers between devices, local_square(): lax.ppermute(mine, 'tensor', ring(groups, shift))  4.45 us
    ppermute x3, starting transfers between devices, local_square(): piece = lax.ppermute(piece, 'tensor', ring(groups, shift))  3.84 us
    ppermute x3, starting transfers between devices, local_square(): lax.ppermute(sketch, 'example', ring(groups, shift))  3.41 us
  transfers between devices with their start and end apart: 16, of which 7 were waited for; matrix products, arithmetic and copies ran while one was open for 1% of the time, Pallas kernels for 29%

profile of v4, /device:TPU:6, one launch (start us, length us, event | category | flops | bytes accessed | tf_op | source)
XLA Modules:
  0.0 63.4 jit_solution(16407324083977847408)
XLA Ops:
  0.0 6.5 %project_right.1 = f32[72,3072]{1,0:T(8,128)S(1)} custom-call(bf16[6,512,2048]{2,1,0:T(8,128)(2,1)} %grads.1, bf16[64,2048]{1,0:T(8,128)(2,1)} %bitcast.36), custom_call_target="tpu_custom_call" | custom-call | flops 3221225472 | bytes 12582912 | tf_op jit(solution)/shard_map/project_right/pallas_call | solution.py:55
  6.6 3.6 %collective-permute-start.2 = (f16[72,768]{1,0:T(8,128)(2,1)S(1)}, f16[72,768]{1,0:T(8,128)(2,1)S(1)}, u32[]{:S(2)}, u32[]{:S(2)}) collective-permute-start(f16[72,768]{1,0:T(8,128)(2,1)S(1)} %get-tuple-element.17), channel_id=1, source_target_pairs={{0,12},{4,0},{8,4},{12,8},{1,13},{5,1},{9,5},{13,9},{2,14},{6,2},{... | collective-permute-start | bytes 331784 | tf_op jit(solution)/shard_map/ppermute | solution.py:234
  10.3 1.0 %collective-permute-start = (f16[72,768]{1,0:T(8,128)(2,1)S(1)}, f16[72,768]{1,0:T(8,128)(2,1)S(1)}, u32[]{:S(2)}, u32[]{:S(2)}) collective-permute-start(f16[72,768]{1,0:T(8,128)(2,1)S(1)} %get-tuple-element.19), channel_id=1, source_target_pairs={{0,4},{4,8},{8,12},{12,0},{1,5},{5,9},{9,13},{13,1},{2,6},{6,10},{... | collective-permute-start | bytes 331784 | tf_op jit(solution)/shard_map/ppermute | solution.py:234
  11.3 8.4 %project_left.2.left_a = bf16[1536,128]{1,0:T(8,128)(2,1)S(1)} custom-call(s32[6]{0:T(128)S(1)} %copy-done.2, bf16[6,512,7168]{2,1,0:T(8,128)(2,1)} %acts.3, bf16[64,7168]{1,0:T(8,128)(2,1)S(1)} %bitcast.26), custom_call_target="tpu_custom_call" | custom-call | flops 5637144576 | bytes 22020096 | tf_op jit(solution)/shard_map/project_left/pallas_call | solution.py:122
  19.8 0.2 collective-permute-done.1
  20.1 0.1 select_convert_fusion
  20.3 2.6 %collective-permute-start.5 = (f16[72,768]{1,0:T(8,128)(2,1)S(1)}, f16[72,768]{1,0:T(8,128)(2,1)S(1)}, u32[]{:S(2)}, u32[]{:S(2)}) collective-permute-start(f16[72,768]{1,0:T(8,128)(2,1)S(1)} %select_convert_fusion), channel_id=1, source_target_pairs={{0,12},{4,0},{8,4},{12,8},{1,13},{5,1},{9,5},{13,9},{2,14},{6,2},{... | collective-permute-start | bytes 331784 | tf_op jit(solution)/shard_map/ppermute | solution.py:244
  22.9 1.1 %collective-permute-start.4 = (f16[72,768]{1,0:T(8,128)(2,1)S(1)}, f16[72,768]{1,0:T(8,128)(2,1)S(1)}, u32[]{:S(2)}, u32[]{:S(2)}) collective-permute-start(f16[72,768]{1,0:T(8,128)(2,1)S(1)} %select_convert_fusion), channel_id=1, source_target_pairs={{0,8},{4,12},{8,0},{12,4},{1,9},{5,13},{9,1},{13,5},{2,10},{6,14},... | collective-permute-start | bytes 331784 | tf_op jit(solution)/shard_map/ppermute | solution.py:244
  24.0 0.7 %collective-permute-start.3 = (f16[72,768]{1,0:T(8,128)(2,1)S(1)}, f16[72,768]{1,0:T(8,128)(2,1)S(1)}, u32[]{:S(2)}, u32[]{:S(2)}) collective-permute-start(f16[72,768]{1,0:T(8,128)(2,1)S(1)} %select_convert_fusion), channel_id=1, source_target_pairs={{0,4},{4,8},{8,12},{12,0},{1,5},{5,9},{9,13},{13,1},{2,6},{6,10},{... | collective-permute-start | bytes 331784 | tf_op jit(solution)/shard_map/ppermute | solution.py:244
  24.7 10.0 %project_left.3.left_b = bf16[1536,128]{1,0:T(8,128)(2,1)S(1)} custom-call(s32[6]{0:T(128)S(1)} %copy-done.2, bf16[6,512,7168]{2,1,0:T(8,128)(2,1)} %acts.3, bf16[64,7168]{1,0:T(8,128)(2,1)S(1)} %bitcast.27), custom_call_target="tpu_custom_call" | custom-call | flops 5637144576 | bytes 22020096 | tf_op jit(solution)/shard_map/project_left/pallas_call | solution.py:122
  34.9 1.4 %sketch_terms.1 = f32[4,8,1152]{2,1,0:T(8,128)S(1)} custom-call(s32[4]{0:T(128)S(1)} %and_select_fusion.where, f32[4,64,768]{2,1,0:T(8,128)S(1)} %slice_multiply_fusion.rights, bf16[1536,128]{1,0:T(8,128)(2,1)S(1)} %project_left.2.left_a, bf16[1536,128]{1,0:T(8,128)(2,1)S(1)} %project_left.3.left_b), custom_call_target="tpu_custom_call" | custom-call | tf_op jit(solution)/shard_map/sketch_terms/pallas_call | solution.py:168
  36.5 3.2 %collective-permute-start.8 = (f16[8,1152]{1,0:T(8,128)(2,1)S(1)}, f16[8,1152]{1,0:T(8,128)(2,1)S(1)}, u32[]{:S(2)}, u32[]{:S(2)}) collective-permute-start(f16[8,1152]{1,0:T(8,128)(2,1)S(1)} %get-tuple-element.30), channel_id=1, source_target_pairs={{0,12},{4,0},{8,4},{12,8},{1,13},{5,1},{9,5},{13,9},{2,14},{6,2},{... | collective-permute-start | bytes 55304 | tf_op jit(solution)/shard_map/ppermute | solution.py:259
  39.7 0.6 %collective-permute-start.6 = (f16[8,1152]{1,0:T(8,128)(2,1)S(1)}, f16[8,1152]{1,0:T(8,128)(2,1)S(1)}, u32[]{:S(2)}, u32[]{:S(2)}) collective-permute-start(f16[8,1152]{1,0:T(8,128)(2,1)S(1)} %get-tuple-element.32), channel_id=1, source_target_pairs={{0,4},{4,8},{8,12},{12,0},{1,5},{5,9},{9,13},{13,1},{2,6},{6,10},{... | collective-permute-start | bytes 55304 | tf_op jit(solution)/shard_map/ppermute | solution.py:259
  40.3 0.1 fusion.50
  40.4 0.7 %collective-permute-done.8 = f16[8,1152]{1,0:T(8,128)(2,1)S(1)} collective-permute-done((f16[8,1152]{1,0:T(8,128)(2,1)S(1)}, f16[8,1152]{1,0:T(8,128)(2,1)S(1)}, u32[]{:S(2)}, u32[]{:S(2)}) %collective-permute-start.8) | collective-permute-done | bytes 18464 | tf_op jit(solution)/shard_map/ppermute | solution.py:259
  41.1 0.1 fusion.41
  41.2 3.1 %collective-permute-done.7 = f16[8,1152]{1,0:T(8,128)(2,1)S(1)} collective-permute-done((f16[8,1152]{1,0:T(8,128)(2,1)S(1)}, f16[8,1152]{1,0:T(8,128)(2,1)S(1)}, u32[]{:S(2)}, u32[]{:S(2)}) %collective-permute-start.7) | collective-permute-done | bytes 18464 | tf_op jit(solution)/shard_map/ppermute | solution.py:259
  44.3 0.1 fusion.44
  44.4 0.8 %collective-permute-done.6 = f16[8,1152]{1,0:T(8,128)(2,1)S(1)} collective-permute-done((f16[8,1152]{1,0:T(8,128)(2,1)S(1)}, f16[8,1152]{1,0:T(8,128)(2,1)S(1)}, u32[]{:S(2)}, u32[]{:S(2)}) %collective-permute-start.6) | collective-permute-done | bytes 18464 | tf_op jit(solution)/shard_map/ppermute | solution.py:259
  45.2 0.1 fusion.47
  45.5 2.0 %collective-permute-start.10 = (f32[8,1024]{1,0:T(8,128)S(1)}, f32[8,1024]{1,0:T(8,128)S(1)}, u32[]{:S(2)}, u32[]{:S(2)}) collective-permute-start(f32[8,1024]{1,0:T(8,128)S(1)} %fusion.4.refs_0_), channel_id=1, source_target_pairs={{0,2},{1,3},{2,0},{3,1},{4,6},{5,7},{6,4},{7,5},{8,10},{9,11},{10,... | collective-permute-start | bytes 98312 | tf_op jit(solution)/shard_map/ppermute | solution.py:263
  47.5 1.4 %collective-permute-start.11 = (f32[8,1024]{1,0:T(8,128)S(1)}, f32[8,1024]{1,0:T(8,128)S(1)}, u32[]{:S(2)}, u32[]{:S(2)}) collective-permute-start(f32[8,1024]{1,0:T(8,128)S(1)} %fusion.4.refs_0_), channel_id=1, source_target_pairs={{0,3},{1,0},{2,1},{3,2},{4,7},{5,4},{6,5},{7,6},{8,11},{9,8},{10,9... | collective-permute-start | bytes 98312 | tf_op jit(solution)/shard_map/ppermute | solution.py:263
  48.9 0.6 collective-permute-done.10.refs_2_
  49.5 1.0 %collective-permute-done.11.refs_3_ = f32[8,1024]{1,0:T(8,128)S(1)} collective-permute-done((f32[8,1024]{1,0:T(8,128)S(1)}, f32[8,1024]{1,0:T(8,128)S(1)}, u32[]{:S(2)}, u32[]{:S(2)}) %collective-permute-start.11) | collective-permute-done | bytes 32800 | tf_op jit(solution)/shard_map/ppermute | solution.py:263
  50.4 0.9 %score_terms.1 = f32[4,8,1152]{2,1,0:T(8,128)S(1)} custom-call(f32[8,1024]{1,0:T(8,128)S(1)} %fusion.4.refs_0_, f32[8,1024]{1,0:T(8,128)S(1)} %collective-permute-done.9.refs_1_, f32[8,1024]{1,0:T(8,128)S(1)} %collective-permute-done.10.refs_2_, f32[8,1024]{1,0:T(8,128)S(1)} %collective-permute-done.11.refs_3_, bf16[1024,1024]{1,0:T(8,128)(2,1)S(1)} %copy-done.1), custom_call_target="tpu_custom_call" | custom-call | tf_op jit(solution)/shard_map/score_terms/pallas_call | solution.py:200
  51.4 1.2 %collective-permute-start.15 = (f16[8,1152]{1,0:T(8,128)(2,1)S(1)}, f16[8,1152]{1,0:T(8,128)(2,1)S(1)}, u32[]{:S(2)}, u32[]{:S(2)}) collective-permute-start(f16[8,1152]{1,0:T(8,128)(2,1)S(1)} %get-tuple-element.26), channel_id=1, source_target_pairs={{0,3},{1,7},{2,11},{3,15},{4,0},{5,4},{6,8},{7,12},{8,1},{9,5},{10... | collective-permute-start | bytes 55304 | tf_op jit(solution)/shard_map/ppermute | solution.py:274
  52.6 1.7 %collective-permute-start.14 = (f16[8,1152]{1,0:T(8,128)(2,1)S(1)}, f16[8,1152]{1,0:T(8,128)(2,1)S(1)}, u32[]{:S(2)}, u32[]{:S(2)}) collective-permute-start(f16[8,1152]{1,0:T(8,128)(2,1)S(1)} %get-tuple-element.27), channel_id=1, source_target_pairs={{0,2},{1,6},{2,10},{3,14},{4,3},{5,7},{6,11},{7,15},{8,0},{9,4},{1... | collective-permute-start | bytes 55304 | tf_op jit(solution)/shard_map/ppermute | solution.py:274
  54.3 0.8 %collective-permute-start.13 = (f16[8,1152]{1,0:T(8,128)(2,1)S(1)}, f16[8,1152]{1,0:T(8,128)(2,1)S(1)}, u32[]{:S(2)}, u32[]{:S(2)}) collective-permute-start(f16[8,1152]{1,0:T(8,128)(2,1)S(1)} %get-tuple-element.28), channel_id=1, source_target_pairs={{0,1},{1,5},{2,9},{3,13},{4,2},{5,6},{6,10},{7,14},{8,3},{9,7},{10... | collective-permute-start | bytes 55304 | tf_op jit(solution)/shard_map/ppermute | solution.py:274
  55.1 4.4 %collective-permute-start.12 = (f16[8,1152]{1,0:T(8,128)(2,1)S(1)}, f16[8,1152]{1,0:T(8,128)(2,1)S(1)}, u32[]{:S(2)}, u32[]{:S(2)}) collective-permute-start(f16[8,1152]{1,0:T(8,128)(2,1)S(1)} %get-tuple-element.25), channel_id=1, source_target_pairs={{0,0},{1,4},{2,8},{3,12},{4,1},{5,5},{6,9},{7,13},{8,2},{9,6},{10,... | collective-permute-start | bytes 55304 | tf_op jit(solution)/shard_map/ppermute | solution.py:274
  59.5 3.0 %collective-permute-done.12 = f16[8,1152]{1,0:T(8,128)(2,1)S(1)} collective-permute-done((f16[8,1152]{1,0:T(8,128)(2,1)S(1)}, f16[8,1152]{1,0:T(8,128)(2,1)S(1)}, u32[]{:S(2)}, u32[]{:S(2)}) %collective-permute-start.12) | collective-permute-done | bytes 18464 | tf_op jit(solution)/shard_map/ppermute | solution.py:274
  62.5 0.2 fusion.38
  62.7 0.7 %fusion.1 = f32[6,1024]{1,0:T(8,128)} fusion(f32[8,1152]{1,0:T(8,128)S(1)} %convert_element_type.71, f32[8,1152]{1,0:T(8,128)S(1)} %convert_element_type.70, f32[8,1152]{1,0:T(8,128)S(1)} %convert_element_type.69, f32[8,1152]{1,0:T(8,128)S(1)} %convert_element_type.68, f32[6]{0:T(128)S(1)} %get-tuple-element.10, f32[6]{0:T(128)S(1)} %get-tuple-element.13, ...), kind=kLoop, calls=%fused_computation.6 | loop fusion | flops 49152 | bytes 123000 | tf_op jit(solution)/shard_map/mul | solution.py:277
  (43 shorter events, 0.8 us)
Async XLA Ops:
  0.0 11.3 %copy-start.2 = (s32[6]{0:T(128)S(1)}, s32[6]{0:T(128)}, u32[]{:S(2)}) copy-start(s32[6]{0:T(128)} %lengths.2) | copy-start | bytes 76
  0.0 11.3 %copy-start = (bf16[7168,64]{0,1:T(8,128)(2,1)S(1)}, bf16[7168,64]{0,1:T(8,128)(2,1)}, u32[]{:S(2)}) copy-start(bf16[7168,64]{0,1:T(8,128)(2,1)} %param.9) | copy-start | bytes 2752516
  6.6 13.1 %collective-permute-start.2 = (f16[72,768]{1,0:T(8,128)(2,1)S(1)}, f16[72,768]{1,0:T(8,128)(2,1)S(1)}, u32[]{:S(2)}, u32[]{:S(2)}) collective-permute-start(f16[72,768]{1,0:T(8,128)(2,1)S(1)} %get-tuple-element.17), channel_id=1, source_target_pairs={{0,12},{4,0},{8,4},{12,8},{1,13},{5,1},{9,5},{13,9},{2,14},{6,2},{... | collective-permute-start | bytes 331784 | tf_op jit(solution)/shard_map/ppermute | solution.py:234
  10.3 9.7 %collective-permute-start.1 = (f16[72,768]{1,0:T(8,128)(2,1)S(1)}, f16[72,768]{1,0:T(8,128)(2,1)S(1)}, u32[]{:S(2)}, u32[]{:S(2)}) collective-permute-start(f16[72,768]{1,0:T(8,128)(2,1)S(1)} %get-tuple-element.18), channel_id=1, source_target_pairs={{0,8},{4,12},{8,0},{12,4},{1,9},{5,13},{9,1},{13,5},{2,10},{6,14},... | collective-permute-start | bytes 331784 | tf_op jit(solution)/shard_map/ppermute | solution.py:234
  10.3 9.7 %collective-permute-start = (f16[72,768]{1,0:T(8,128)(2,1)S(1)}, f16[72,768]{1,0:T(8,128)(2,1)S(1)}, u32[]{:S(2)}, u32[]{:S(2)}) collective-permute-start(f16[72,768]{1,0:T(8,128)(2,1)S(1)} %get-tuple-element.19), channel_id=1, source_target_pairs={{0,4},{4,8},{8,12},{12,0},{1,5},{5,9},{9,13},{13,1},{2,6},{6,10},{... | collective-permute-start | bytes 331784 | tf_op jit(solution)/shard_map/ppermute | solution.py:234
  20.2 30.2 %copy-start.1 = (bf16[1024,1024]{1,0:T(8,128)(2,1)S(1)}, bf16[1024,1024]{1,0:T(8,128)(2,1)}, u32[]{:S(2)}) copy-start(bf16[1024,1024]{1,0:T(8,128)(2,1)} %refs_4_.1) | copy-start | bytes 6291460
  20.3 14.4 %collective-permute-start.5 = (f16[72,768]{1,0:T(8,128)(2,1)S(1)}, f16[72,768]{1,0:T(8,128)(2,1)S(1)}, u32[]{:S(2)}, u32[]{:S(2)}) collective-permute-start(f16[72,768]{1,0:T(8,128)(2,1)S(1)} %select_convert_fusion), channel_id=1, source_target_pairs={{0,12},{4,0},{8,4},{12,8},{1,13},{5,1},{9,5},{13,9},{2,14},{6,2},{... | collective-permute-start | bytes 331784 | tf_op jit(solution)/shard_map/ppermute | solution.py:244
  22.9 11.8 %collective-permute-start.4 = (f16[72,768]{1,0:T(8,128)(2,1)S(1)}, f16[72,768]{1,0:T(8,128)(2,1)S(1)}, u32[]{:S(2)}, u32[]{:S(2)}) collective-permute-start(f16[72,768]{1,0:T(8,128)(2,1)S(1)} %select_convert_fusion), channel_id=1, source_target_pairs={{0,8},{4,12},{8,0},{12,4},{1,9},{5,13},{9,1},{13,5},{2,10},{6,14},... | collective-permute-start | bytes 331784 | tf_op jit(solution)/shard_map/ppermute | solution.py:244
  24.0 10.7 %collective-permute-start.3 = (f16[72,768]{1,0:T(8,128)(2,1)S(1)}, f16[72,768]{1,0:T(8,128)(2,1)S(1)}, u32[]{:S(2)}, u32[]{:S(2)}) collective-permute-start(f16[72,768]{1,0:T(8,128)(2,1)S(1)} %select_convert_fusion), channel_id=1, source_target_pairs={{0,4},{4,8},{8,12},{12,0},{1,5},{5,9},{9,13},{13,1},{2,6},{6,10},{... | collective-permute-start | bytes 331784 | tf_op jit(solution)/shard_map/ppermute | solution.py:244
  36.5 4.7 %collective-permute-start.8 = (f16[8,1152]{1,0:T(8,128)(2,1)S(1)}, f16[8,1152]{1,0:T(8,128)(2,1)S(1)}, u32[]{:S(2)}, u32[]{:S(2)}) collective-permute-start(f16[8,1152]{1,0:T(8,128)(2,1)S(1)} %get-tuple-element.30), channel_id=1, source_target_pairs={{0,12},{4,0},{8,4},{12,8},{1,13},{5,1},{9,5},{13,9},{2,14},{6,2},{... | collective-permute-start | bytes 55304 | tf_op jit(solution)/shard_map/ppermute | solution.py:259
  39.7 4.7 %collective-permute-start.7 = (f16[8,1152]{1,0:T(8,128)(2,1)S(1)}, f16[8,1152]{1,0:T(8,128)(2,1)S(1)}, u32[]{:S(2)}, u32[]{:S(2)}) collective-permute-start(f16[8,1152]{1,0:T(8,128)(2,1)S(1)} %get-tuple-element.31), channel_id=1, source_target_pairs={{0,8},{4,12},{8,0},{12,4},{1,9},{5,13},{9,1},{13,5},{2,10},{6,14},... | collective-permute-start | bytes 55304 | tf_op jit(solution)/shard_map/ppermute | solution.py:259
  39.7 5.6 %collective-permute-start.6 = (f16[8,1152]{1,0:T(8,128)(2,1)S(1)}, f16[8,1152]{1,0:T(8,128)(2,1)S(1)}, u32[]{:S(2)}, u32[]{:S(2)}) collective-permute-start(f16[8,1152]{1,0:T(8,128)(2,1)S(1)} %get-tuple-element.32), channel_id=1, source_target_pairs={{0,4},{4,8},{8,12},{12,0},{1,5},{5,9},{9,13},{13,1},{2,6},{6,10},{... | collective-permute-start | bytes 55304 | tf_op jit(solution)/shard_map/ppermute | solution.py:259
  45.4 3.4 %collective-permute-start.9 = (f32[8,1024]{1,0:T(8,128)S(1)}, f32[8,1024]{1,0:T(8,128)S(1)}, u32[]{:S(2)}, u32[]{:S(2)}) collective-permute-start(f32[8,1024]{1,0:T(8,128)S(1)} %fusion.4.refs_0_), channel_id=1, source_target_pairs={{0,1},{1,2},{2,3},{3,0},{4,5},{5,6},{6,7},{7,4},{8,9},{9,10},{10,1... | collective-permute-start | bytes 98312 | tf_op jit(solution)/shard_map/ppermute | solution.py:263
  45.5 4.0 %collective-permute-start.10 = (f32[8,1024]{1,0:T(8,128)S(1)}, f32[8,1024]{1,0:T(8,128)S(1)}, u32[]{:S(2)}, u32[]{:S(2)}) collective-permute-start(f32[8,1024]{1,0:T(8,128)S(1)} %fusion.4.refs_0_), channel_id=1, source_target_pairs={{0,2},{1,3},{2,0},{3,1},{4,6},{5,7},{6,4},{7,5},{8,10},{9,11},{10,... | collective-permute-start | bytes 98312 | tf_op jit(solution)/shard_map/ppermute | solution.py:263
  47.5 3.0 %collective-permute-start.11 = (f32[8,1024]{1,0:T(8,128)S(1)}, f32[8,1024]{1,0:T(8,128)S(1)}, u32[]{:S(2)}, u32[]{:S(2)}) collective-permute-start(f32[8,1024]{1,0:T(8,128)S(1)} %fusion.4.refs_0_), channel_id=1, source_target_pairs={{0,3},{1,0},{2,1},{3,2},{4,7},{5,4},{6,5},{7,6},{8,11},{9,8},{10,9... | collective-permute-start | bytes 98312 | tf_op jit(solution)/shard_map/ppermute | solution.py:263
  51.4 8.1 %collective-permute-start.15 = (f16[8,1152]{1,0:T(8,128)(2,1)S(1)}, f16[8,1152]{1,0:T(8,128)(2,1)S(1)}, u32[]{:S(2)}, u32[]{:S(2)}) collective-permute-start(f16[8,1152]{1,0:T(8,128)(2,1)S(1)} %get-tuple-element.26), channel_id=1, source_target_pairs={{0,3},{1,7},{2,11},{3,15},{4,0},{5,4},{6,8},{7,12},{8,1},{9,5},{10... | collective-permute-start | bytes 55304 | tf_op jit(solution)/shard_map/ppermute | solution.py:274
  52.6 6.9 %collective-permute-start.14 = (f16[8,1152]{1,0:T(8,128)(2,1)S(1)}, f16[8,1152]{1,0:T(8,128)(2,1)S(1)}, u32[]{:S(2)}, u32[]{:S(2)}) collective-permute-start(f16[8,1152]{1,0:T(8,128)(2,1)S(1)} %get-tuple-element.27), channel_id=1, source_target_pairs={{0,2},{1,6},{2,10},{3,14},{4,3},{5,7},{6,11},{7,15},{8,0},{9,4},{1... | collective-permute-start | bytes 55304 | tf_op jit(solution)/shard_map/ppermute | solution.py:274
  54.3 5.2 %collective-permute-start.13 = (f16[8,1152]{1,0:T(8,128)(2,1)S(1)}, f16[8,1152]{1,0:T(8,128)(2,1)S(1)}, u32[]{:S(2)}, u32[]{:S(2)}) collective-permute-start(f16[8,1152]{1,0:T(8,128)(2,1)S(1)} %get-tuple-element.28), channel_id=1, source_target_pairs={{0,1},{1,5},{2,9},{3,13},{4,2},{5,6},{6,10},{7,14},{8,3},{9,7},{10... | collective-permute-start | bytes 55304 | tf_op jit(solution)/shard_map/ppermute | solution.py:274
  55.1 7.4 %collective-permute-start.12 = (f16[8,1152]{1,0:T(8,128)(2,1)S(1)}, f16[8,1152]{1,0:T(8,128)(2,1)S(1)}, u32[]{:S(2)}, u32[]{:S(2)}) collective-permute-start(f16[8,1152]{1,0:T(8,128)(2,1)S(1)} %get-tuple-element.25), channel_id=1, source_target_pairs={{0,0},{1,4},{2,8},{3,12},{4,1},{5,5},{6,9},{7,13},{8,2},{9,6},{10,... | collective-permute-start | bytes 55304 | tf_op jit(solution)/shard_map/ppermute | solution.py:274

commit v5 on v4

--- a/solution.py
+++ b/solution.py
@@ -9,6 +9,7 @@
 
 TOP = 14.0
 EXTRA = 8
+AHEAD = 3
 LANES = 128
 UNITS = 4
 NT = (((1,), (1,)), ((), ()))
@@ -30,12 +31,17 @@
     def copy(l):
         return pltpu.make_async_copy(grads.at[l], held.at[l], arrived.at[l])
 
-    for l in range(lists):
+    for l in range(min(AHEAD, lists)):
         copy(l).start()
     load.wait()
 
     def step(l, carry):
         copy(l).wait()
+
+        @pl.when(l + AHEAD < lists)
+        def _():
+            copy(l + AHEAD).start()
+
         right = lax.dot_general(held[l], weights[...], NT, preferred_element_type=jnp.float32).T
         largest = jnp.max(jnp.abs(right), axis=0, keepdims=True)
         exponent = jnp.ceil(jnp.log2(jnp.maximum(largest, 1e-30)))
@@ -118,7 +124,7 @@
 def project_left(activations, basis, lengths, first, lists):
     slots, width = activations.shape[1:]
     rank = basis.shape[0]
-    size, depth = 256, 6
+    size, depth = 256, 4
     return pl.pallas_call(
         functools.partial(left_kernel, first, slots),
         in_specs=[
@@ -226,6 +232,7 @@
     block = tokens // groups
 
     right = project_right(out_grads, proj_out.T)
+    right, proj_in = lax.optimization_barrier((right, proj_in))
     coded = right.astype(jnp.float16)
 
     def part(shift):
@@ -250,6 +257,7 @@
     def towards(array, index):
         return lax.dynamic_index_in_dim(array, index, 0, keepdims=False)
 
+    terms, queries = lax.optimization_barrier((terms, queries))
     coded = terms.astype(jnp.float16)
     entries = rank * rank // groups
     sketch = None

time: 63.1 us -> 62.6 us (level)
  the two profiles are of different devices: /device:TPU:6 before, /device:TPU:2 now
where the time goes in v5:
time: 62.6 us; the launch traced here: 61.8 us
  Pallas kernels  26.2 us (42%)
  starting transfers between devices  22.8 us (36%)
  waiting for transfers between devices  10.2 us (16%)
  other arithmetic  2.21 us (4%)
    pallas_call x2, Pallas kernels, project_left(): pl.pallas_call(functools.partial(left_kernel, first, slots), in_specs=[pl...  17.4 us
    ppermute x4, starting transfers between devices, local_square(): lax.ppermute(towards(scores, (here - target) % groups), ('tensor', 'examp...  8.09 us
    pallas_call x1, Pallas kernels, project_right(): pl.pallas_call(right_kernel, in_specs=[pl.BlockSpec(memory_space=pltpu.HB...  6.46 us
    ppermute x3, starting transfers between devices, local_square(): lax.ppermute(part(shift), 'tensor', ring(groups, shift))  4.67 us
    ppermute x3, waiting for transfers between devices, local_square(): piece = lax.ppermute(piece, 'tensor', ring(groups, shift))  4.55 us
    ppermute x3, starting transfers between devices, local_square(): lax.ppermute(mine, 'tensor', ring(groups, shift))  4.45 us
    ppermute x3, starting transfers between devices, local_square(): piece = lax.ppermute(piece, 'tensor', ring(groups, shift))  3.78 us
    ppermute x4, waiting for transfers between devices, local_square(): lax.ppermute(towards(scores, (here - target) % groups), ('tensor', 'examp...  3.03 us
  transfers between devices with their start and end apart: 16, of which 7 were waited for; matrix products, arithmetic and copies ran while one was open for 1% of the time, Pallas kernels for 28%

profile of v5, /device:TPU:2, one launch (start us, length us, event | category | flops | bytes accessed | tf_op | source)
XLA Modules:
  0.0 61.8 jit_solution(5454419508131420127)
XLA Ops:
  0.0 6.5 %project_right.1 = f32[72,3072]{1,0:T(8,128)S(1)} custom-call(bf16[6,512,2048]{2,1,0:T(8,128)(2,1)} %grads.1, bf16[64,2048]{1,0:T(8,128)(2,1)} %bitcast.36), custom_call_target="tpu_custom_call" | custom-call | flops 3221225472 | bytes 12582912 | tf_op jit(solution)/shard_map/project_right/pallas_call | solution.py:61
  6.6 3.7 %collective-permute-start.2 = (f16[72,768]{1,0:T(8,128)(2,1)S(1)}, f16[72,768]{1,0:T(8,128)(2,1)S(1)}, u32[]{:S(2)}, u32[]{:S(2)}) collective-permute-start(f16[72,768]{1,0:T(8,128)(2,1)S(1)} %get-tuple-element.25), channel_id=1, source_target_pairs={{0,12},{4,0},{8,4},{12,8},{1,13},{5,1},{9,5},{13,9},{2,14},{6,2},{... | collective-permute-start | bytes 331784 | tf_op jit(solution)/shard_map/ppermute | solution.py:241
  10.3 1.0 %collective-permute-start = (f16[72,768]{1,0:T(8,128)(2,1)S(1)}, f16[72,768]{1,0:T(8,128)(2,1)S(1)}, u32[]{:S(2)}, u32[]{:S(2)}) collective-permute-start(f16[72,768]{1,0:T(8,128)(2,1)S(1)} %get-tuple-element.27), channel_id=1, source_target_pairs={{0,4},{4,8},{8,12},{12,0},{1,5},{5,9},{9,13},{13,1},{2,6},{6,10},{... | collective-permute-start | bytes 331784 | tf_op jit(solution)/shard_map/ppermute | solution.py:241
  11.3 8.3 %project_left.2.left_a = bf16[1536,128]{1,0:T(8,128)(2,1)S(1)} custom-call(s32[6]{0:T(128)S(1)} %copy-done.2, bf16[6,512,7168]{2,1,0:T(8,128)(2,1)} %acts.3, bf16[64,7168]{1,0:T(8,128)(2,1)S(1)} %bitcast.26), custom_call_target="tpu_custom_call" | custom-call | flops 5637144576 | bytes 22020096 | tf_op jit(solution)/shard_map/project_left/pallas_call | solution.py:128
  19.7 0.3 collective-permute-done.1
  20.1 0.1 select_convert_fusion
  20.3 2.6 %collective-permute-start.5 = (f16[72,768]{1,0:T(8,128)(2,1)S(1)}, f16[72,768]{1,0:T(8,128)(2,1)S(1)}, u32[]{:S(2)}, u32[]{:S(2)}) collective-permute-start(f16[72,768]{1,0:T(8,128)(2,1)S(1)} %select_convert_fusion), channel_id=1, source_target_pairs={{0,12},{4,0},{8,4},{12,8},{1,13},{5,1},{9,5},{13,9},{2,14},{6,2},{... | collective-permute-start | bytes 331784 | tf_op jit(solution)/shard_map/ppermute | solution.py:251
  22.8 1.1 %collective-permute-start.4 = (f16[72,768]{1,0:T(8,128)(2,1)S(1)}, f16[72,768]{1,0:T(8,128)(2,1)S(1)}, u32[]{:S(2)}, u32[]{:S(2)}) collective-permute-start(f16[72,768]{1,0:T(8,128)(2,1)S(1)} %select_convert_fusion), channel_id=1, source_target_pairs={{0,8},{4,12},{8,0},{12,4},{1,9},{5,13},{9,1},{13,5},{2,10},{6,14},... | collective-permute-start | bytes 331784 | tf_op jit(solution)/shard_map/ppermute | solution.py:251
  24.0 0.7 %collective-permute-start.3 = (f16[72,768]{1,0:T(8,128)(2,1)S(1)}, f16[72,768]{1,0:T(8,128)(2,1)S(1)}, u32[]{:S(2)}, u32[]{:S(2)}) collective-permute-start(f16[72,768]{1,0:T(8,128)(2,1)S(1)} %select_convert_fusion), channel_id=1, source_target_pairs={{0,4},{4,8},{8,12},{12,0},{1,5},{5,9},{9,13},{13,1},{2,6},{6,10},{... | collective-permute-start | bytes 331784 | tf_op jit(solution)/shard_map/ppermute | solution.py:251
  24.7 9.2 %project_left.3.left_b = bf16[1536,128]{1,0:T(8,128)(2,1)S(1)} custom-call(s32[6]{0:T(128)S(1)} %copy-done.2, bf16[6,512,7168]{2,1,0:T(8,128)(2,1)} %acts.3, bf16[64,7168]{1,0:T(8,128)(2,1)S(1)} %bitcast.27), custom_call_target="tpu_custom_call" | custom-call | flops 5637144576 | bytes 22020096 | tf_op jit(solution)/shard_map/project_left/pallas_call | solution.py:128
  33.9 0.1 maximum_convert_fusion
  34.2 1.5 %sketch_terms.1 = f32[4,8,1152]{2,1,0:T(8,128)S(1)} custom-call(s32[4]{0:T(128)S(1)} %and_select_fusion.where, f32[4,64,768]{2,1,0:T(8,128)S(1)} %slice_multiply_fusion.rights, bf16[1536,128]{1,0:T(8,128)(2,1)S(1)} %project_left.2.left_a, bf16[1536,128]{1,0:T(8,128)(2,1)S(1)} %project_left.3.left_b), custom_call_target="tpu_custom_call" | custom-call | tf_op jit(solution)/shard_map/sketch_terms/pallas_call | solution.py:174
  35.7 3.1 %collective-permute-start.8 = (f16[8,1152]{1,0:T(8,128)(2,1)S(1)}, f16[8,1152]{1,0:T(8,128)(2,1)S(1)}, u32[]{:S(2)}, u32[]{:S(2)}) collective-permute-start(f16[8,1152]{1,0:T(8,128)(2,1)S(1)} %get-tuple-element.38), channel_id=1, source_target_pairs={{0,12},{4,0},{8,4},{12,8},{1,13},{5,1},{9,5},{13,9},{2,14},{6,2},{... | collective-permute-start | bytes 55304 | tf_op jit(solution)/shard_map/ppermute | solution.py:267
  38.8 0.6 %collective-permute-start.6 = (f16[8,1152]{1,0:T(8,128)(2,1)S(1)}, f16[8,1152]{1,0:T(8,128)(2,1)S(1)}, u32[]{:S(2)}, u32[]{:S(2)}) collective-permute-start(f16[8,1152]{1,0:T(8,128)(2,1)S(1)} %get-tuple-element.40), channel_id=1, source_target_pairs={{0,4},{4,8},{8,12},{12,0},{1,5},{5,9},{9,13},{13,1},{2,6},{6,10},{... | collective-permute-start | bytes 55304 | tf_op jit(solution)/shard_map/ppermute | solution.py:267
  39.5 0.1 fusion.50
  39.6 0.7 %collective-permute-done.8 = f16[8,1152]{1,0:T(8,128)(2,1)S(1)} collective-permute-done((f16[8,1152]{1,0:T(8,128)(2,1)S(1)}, f16[8,1152]{1,0:T(8,128)(2,1)S(1)}, u32[]{:S(2)}, u32[]{:S(2)}) %collective-permute-start.8) | collective-permute-done | bytes 18464 | tf_op jit(solution)/shard_map/ppermute | solution.py:267
  40.3 0.1 fusion.41
  40.4 3.1 %collective-permute-done.7 = f16[8,1152]{1,0:T(8,128)(2,1)S(1)} collective-permute-done((f16[8,1152]{1,0:T(8,128)(2,1)S(1)}, f16[8,1152]{1,0:T(8,128)(2,1)S(1)}, u32[]{:S(2)}, u32[]{:S(2)}) %collective-permute-start.7) | collective-permute-done | bytes 18464 | tf_op jit(solution)/shard_map/ppermute | solution.py:267
  43.5 0.1 fusion.44
  43.6 0.8 %collective-permute-done.6 = f16[8,1152]{1,0:T(8,128)(2,1)S(1)} collective-permute-done((f16[8,1152]{1,0:T(8,128)(2,1)S(1)}, f16[8,1152]{1,0:T(8,128)(2,1)S(1)}, u32[]{:S(2)}, u32[]{:S(2)}) %collective-permute-start.6) | collective-permute-done | bytes 18464 | tf_op jit(solution)/shard_map/ppermute | solution.py:267
  44.4 0.1 fusion.47
  44.7 1.7 %collective-permute-start.11 = (f32[8,1024]{1,0:T(8,128)S(1)}, f32[8,1024]{1,0:T(8,128)S(1)}, u32[]{:S(2)}, u32[]{:S(2)}) collective-permute-start(f32[8,1024]{1,0:T(8,128)S(1)} %fusion.4.refs_0_), channel_id=1, source_target_pairs={{0,3},{1,0},{2,1},{3,2},{4,7},{5,4},{6,5},{7,6},{8,11},{9,8},{10,9... | collective-permute-start | bytes 98312 | tf_op jit(solution)/shard_map/ppermute | solution.py:271
  46.4 1.6 %collective-permute-done.9.refs_1_ = f32[8,1024]{1,0:T(8,128)S(1)} collective-permute-done((f32[8,1024]{1,0:T(8,128)S(1)}, f32[8,1024]{1,0:T(8,128)S(1)}, u32[]{:S(2)}, u32[]{:S(2)}) %collective-permute-start.9) | collective-permute-done | bytes 32800 | tf_op jit(solution)/shard_map/ppermute | solution.py:271
  48.0 0.7 %collective-permute-done.10.refs_2_ = f32[8,1024]{1,0:T(8,128)S(1)} collective-permute-done((f32[8,1024]{1,0:T(8,128)S(1)}, f32[8,1024]{1,0:T(8,128)S(1)}, u32[]{:S(2)}, u32[]{:S(2)}) %collective-permute-start.10) | collective-permute-done | bytes 32800 | tf_op jit(solution)/shard_map/ppermute | solution.py:271
  48.7 0.9 %score_terms.1 = f32[4,8,1152]{2,1,0:T(8,128)S(1)} custom-call(f32[8,1024]{1,0:T(8,128)S(1)} %fusion.4.refs_0_, f32[8,1024]{1,0:T(8,128)S(1)} %collective-permute-done.9.refs_1_, f32[8,1024]{1,0:T(8,128)S(1)} %collective-permute-done.10.refs_2_, f32[8,1024]{1,0:T(8,128)S(1)} %collective-permute-done.11.refs_3_, bf16[1024,1024]{1,0:T(8,128)(2,1)S(1)} %copy-done.1), custom_call_target="tpu_custom_call" | custom-call | tf_op jit(solution)/shard_map/score_terms/pallas_call | solution.py:206
  49.6 1.9 %collective-permute-start.15 = (f16[8,1152]{1,0:T(8,128)(2,1)S(1)}, f16[8,1152]{1,0:T(8,128)(2,1)S(1)}, u32[]{:S(2)}, u32[]{:S(2)}) collective-permute-start(f16[8,1152]{1,0:T(8,128)(2,1)S(1)} %get-tuple-element.34), channel_id=1, source_target_pairs={{0,3},{1,7},{2,11},{3,15},{4,0},{5,4},{6,8},{7,12},{8,1},{9,5},{10... | collective-permute-start | bytes 55304 | tf_op jit(solution)/shard_map/ppermute | solution.py:282
  51.6 0.3 collective-permute-start.14
  51.9 1.5 %collective-permute-start.13 = (f16[8,1152]{1,0:T(8,128)(2,1)S(1)}, f16[8,1152]{1,0:T(8,128)(2,1)S(1)}, u32[]{:S(2)}, u32[]{:S(2)}) collective-permute-start(f16[8,1152]{1,0:T(8,128)(2,1)S(1)} %get-tuple-element.36), channel_id=1, source_target_pairs={{0,1},{1,5},{2,9},{3,13},{4,2},{5,6},{6,10},{7,14},{8,3},{9,7},{10... | collective-permute-start | bytes 55304 | tf_op jit(solution)/shard_map/ppermute | solution.py:282
  53.4 4.3 %collective-permute-start.12 = (f16[8,1152]{1,0:T(8,128)(2,1)S(1)}, f16[8,1152]{1,0:T(8,128)(2,1)S(1)}, u32[]{:S(2)}, u32[]{:S(2)}) collective-permute-start(f16[8,1152]{1,0:T(8,128)(2,1)S(1)} %get-tuple-element.33), channel_id=1, source_target_pairs={{0,0},{1,4},{2,8},{3,12},{4,1},{5,5},{6,9},{7,13},{8,2},{9,6},{10,... | collective-permute-start | bytes 55304 | tf_op jit(solution)/shard_map/ppermute | solution.py:282
  57.8 3.0 %collective-permute-done.12 = f16[8,1152]{1,0:T(8,128)(2,1)S(1)} collective-permute-done((f16[8,1152]{1,0:T(8,128)(2,1)S(1)}, f16[8,1152]{1,0:T(8,128)(2,1)S(1)}, u32[]{:S(2)}, u32[]{:S(2)}) %collective-permute-start.12) | collective-permute-done | bytes 18464 | tf_op jit(solution)/shard_map/ppermute | solution.py:282
  60.8 0.2 fusion.38
  61.1 0.7 %fusion.1 = f32[6,1024]{1,0:T(8,128)} fusion(f32[8,1152]{1,0:T(8,128)S(1)} %convert_element_type.71, f32[8,1152]{1,0:T(8,128)S(1)} %convert_element_type.70, f32[8,1152]{1,0:T(8,128)S(1)} %convert_element_type.69, f32[8,1152]{1,0:T(8,128)S(1)} %convert_element_type.68, f32[6]{0:T(128)S(1)} %get-tuple-element.18, f32[6]{0:T(128)S(1)} %get-tuple-element.21, ...), kind=kLoop, calls=%fused_computation.6 | loop fusion | flops 49152 | bytes 123000 | tf_op jit(solution)/shard_map/mul | solution.py:285
  (43 shorter events, 0.7 us)
Async XLA Ops:
  0.0 11.3 %copy-start = (bf16[7168,64]{0,1:T(8,128)(2,1)S(1)}, bf16[7168,64]{0,1:T(8,128)(2,1)}, u32[]{:S(2)}) copy-start(bf16[7168,64]{0,1:T(8,128)(2,1)} %param.9) | copy-start | bytes 2752516
  0.0 11.3 %copy-start.2 = (s32[6]{0:T(128)S(1)}, s32[6]{0:T(128)}, u32[]{:S(2)}) copy-start(s32[6]{0:T(128)} %lengths.2) | copy-start | bytes 76
  6.6 13.0 %collective-permute-start.2 = (f16[72,768]{1,0:T(8,128)(2,1)S(1)}, f16[72,768]{1,0:T(8,128)(2,1)S(1)}, u32[]{:S(2)}, u32[]{:S(2)}) collective-permute-start(f16[72,768]{1,0:T(8,128)(2,1)S(1)} %get-tuple-element.25), channel_id=1, source_target_pairs={{0,12},{4,0},{8,4},{12,8},{1,13},{5,1},{9,5},{13,9},{2,14},{6,2},{... | collective-permute-start | bytes 331784 | tf_op jit(solution)/shard_map/ppermute | solution.py:241
  10.3 9.7 %collective-permute-start.1 = (f16[72,768]{1,0:T(8,128)(2,1)S(1)}, f16[72,768]{1,0:T(8,128)(2,1)S(1)}, u32[]{:S(2)}, u32[]{:S(2)}) collective-permute-start(f16[72,768]{1,0:T(8,128)(2,1)S(1)} %get-tuple-element.26), channel_id=1, source_target_pairs={{0,8},{4,12},{8,0},{12,4},{1,9},{5,13},{9,1},{13,5},{2,10},{6,14},... | collective-permute-start | bytes 331784 | tf_op jit(solution)/shard_map/ppermute | solution.py:241
  10.3 9.7 %collective-permute-start = (f16[72,768]{1,0:T(8,128)(2,1)S(1)}, f16[72,768]{1,0:T(8,128)(2,1)S(1)}, u32[]{:S(2)}, u32[]{:S(2)}) collective-permute-start(f16[72,768]{1,0:T(8,128)(2,1)S(1)} %get-tuple-element.27), channel_id=1, source_target_pairs={{0,4},{4,8},{8,12},{12,0},{1,5},{5,9},{9,13},{13,1},{2,6},{6,10},{... | collective-permute-start | bytes 331784 | tf_op jit(solution)/shard_map/ppermute | solution.py:241
  20.2 28.4 %copy-start.1 = (bf16[1024,1024]{1,0:T(8,128)(2,1)S(1)}, bf16[1024,1024]{1,0:T(8,128)(2,1)}, u32[]{:S(2)}) copy-start(bf16[1024,1024]{1,0:T(8,128)(2,1)} %refs_4_) | copy-start | bytes 6291460
  20.3 13.6 %collective-permute-start.5 = (f16[72,768]{1,0:T(8,128)(2,1)S(1)}, f16[72,768]{1,0:T(8,128)(2,1)S(1)}, u32[]{:S(2)}, u32[]{:S(2)}) collective-permute-start(f16[72,768]{1,0:T(8,128)(2,1)S(1)} %select_convert_fusion), channel_id=1, source_target_pairs={{0,12},{4,0},{8,4},{12,8},{1,13},{5,1},{9,5},{13,9},{2,14},{6,2},{... | collective-permute-start | bytes 331784 | tf_op jit(solution)/shard_map/ppermute | solution.py:251
  22.8 11.0 %collective-permute-start.4 = (f16[72,768]{1,0:T(8,128)(2,1)S(1)}, f16[72,768]{1,0:T(8,128)(2,1)S(1)}, u32[]{:S(2)}, u32[]{:S(2)}) collective-permute-start(f16[72,768]{1,0:T(8,128)(2,1)S(1)} %select_convert_fusion), channel_id=1, source_target_pairs={{0,8},{4,12},{8,0},{12,4},{1,9},{5,13},{9,1},{13,5},{2,10},{6,14},... | collective-permute-start | bytes 331784 | tf_op jit(solution)/shard_map/ppermute | solution.py:251
  24.0 9.9 %collective-permute-start.3 = (f16[72,768]{1,0:T(8,128)(2,1)S(1)}, f16[72,768]{1,0:T(8,128)(2,1)S(1)}, u32[]{:S(2)}, u32[]{:S(2)}) collective-permute-start(f16[72,768]{1,0:T(8,128)(2,1)S(1)} %select_convert_fusion), channel_id=1, source_target_pairs={{0,4},{4,8},{8,12},{12,0},{1,5},{5,9},{9,13},{13,1},{2,6},{6,10},{... | collective-permute-start | bytes 331784 | tf_op jit(solution)/shard_map/ppermute | solution.py:251
  35.7 4.6 %collective-permute-start.8 = (f16[8,1152]{1,0:T(8,128)(2,1)S(1)}, f16[8,1152]{1,0:T(8,128)(2,1)S(1)}, u32[]{:S(2)}, u32[]{:S(2)}) collective-permute-start(f16[8,1152]{1,0:T(8,128)(2,1)S(1)} %get-tuple-element.38), channel_id=1, source_target_pairs={{0,12},{4,0},{8,4},{12,8},{1,13},{5,1},{9,5},{13,9},{2,14},{6,2},{... | collective-permute-start | bytes 55304 | tf_op jit(solution)/shard_map/ppermute | solution.py:267
  38.8 4.7 %collective-permute-start.7 = (f16[8,1152]{1,0:T(8,128)(2,1)S(1)}, f16[8,1152]{1,0:T(8,128)(2,1)S(1)}, u32[]{:S(2)}, u32[]{:S(2)}) collective-permute-start(f16[8,1152]{1,0:T(8,128)(2,1)S(1)} %get-tuple-element.39), channel_id=1, source_target_pairs={{0,8},{4,12},{8,0},{12,4},{1,9},{5,13},{9,1},{13,5},{2,10},{6,14},... | collective-permute-start | bytes 55304 | tf_op jit(solution)/shard_map/ppermute | solution.py:267
  38.8 5.6 %collective-permute-start.6 = (f16[8,1152]{1,0:T(8,128)(2,1)S(1)}, f16[8,1152]{1,0:T(8,128)(2,1)S(1)}, u32[]{:S(2)}, u32[]{:S(2)}) collective-permute-start(f16[8,1152]{1,0:T(8,128)(2,1)S(1)} %get-tuple-element.40), channel_id=1, source_target_pairs={{0,4},{4,8},{8,12},{12,0},{1,5},{5,9},{9,13},{13,1},{2,6},{6,10},{... | collective-permute-start | bytes 55304 | tf_op jit(solution)/shard_map/ppermute | solution.py:267
  44.6 3.4 %collective-permute-start.9 = (f32[8,1024]{1,0:T(8,128)S(1)}, f32[8,1024]{1,0:T(8,128)S(1)}, u32[]{:S(2)}, u32[]{:S(2)}) collective-permute-start(f32[8,1024]{1,0:T(8,128)S(1)} %fusion.4.refs_0_), channel_id=1, source_target_pairs={{0,1},{1,2},{2,3},{3,0},{4,5},{5,6},{6,7},{7,4},{8,9},{9,10},{10,1... | collective-permute-start | bytes 98312 | tf_op jit(solution)/shard_map/ppermute | solution.py:271
  44.7 4.0 %collective-permute-start.10 = (f32[8,1024]{1,0:T(8,128)S(1)}, f32[8,1024]{1,0:T(8,128)S(1)}, u32[]{:S(2)}, u32[]{:S(2)}) collective-permute-start(f32[8,1024]{1,0:T(8,128)S(1)} %fusion.4.refs_0_), channel_id=1, source_target_pairs={{0,2},{1,3},{2,0},{3,1},{4,6},{5,7},{6,4},{7,5},{8,10},{9,11},{10,... | collective-permute-start | bytes 98312 | tf_op jit(solution)/shard_map/ppermute | solution.py:271
  44.7 4.0 %collective-permute-start.11 = (f32[8,1024]{1,0:T(8,128)S(1)}, f32[8,1024]{1,0:T(8,128)S(1)}, u32[]{:S(2)}, u32[]{:S(2)}) collective-permute-start(f32[8,1024]{1,0:T(8,128)S(1)} %fusion.4.refs_0_), channel_id=1, source_target_pairs={{0,3},{1,0},{2,1},{3,2},{4,7},{5,4},{6,5},{7,6},{8,11},{9,8},{10,9... | collective-permute-start | bytes 98312 | tf_op jit(solution)/shard_map/ppermute | solution.py:271
  49.6 8.1 %collective-permute-start.15 = (f16[8,1152]{1,0:T(8,128)(2,1)S(1)}, f16[8,1152]{1,0:T(8,128)(2,1)S(1)}, u32[]{:S(2)}, u32[]{:S(2)}) collective-permute-start(f16[8,1152]{1,0:T(8,128)(2,1)S(1)} %get-tuple-element.34), channel_id=1, source_target_pairs={{0,3},{1,7},{2,11},{3,15},{4,0},{5,4},{6,8},{7,12},{8,1},{9,5},{10... | collective-permute-start | bytes 55304 | tf_op jit(solution)/shard_map/ppermute | solution.py:282
  51.6 6.2 %collective-permute-start.14 = (f16[8,1152]{1,0:T(8,128)(2,1)S(1)}, f16[8,1152]{1,0:T(8,128)(2,1)S(1)}, u32[]{:S(2)}, u32[]{:S(2)}) collective-permute-start(f16[8,1152]{1,0:T(8,128)(2,1)S(1)} %get-tuple-element.35), channel_id=1, source_target_pairs={{0,2},{1,6},{2,10},{3,14},{4,3},{5,7},{6,11},{7,15},{8,0},{9,4},{1... | collective-permute-start | bytes 55304 | tf_op jit(solution)/shard_map/ppermute | solution.py:282
  51.9 5.9 %collective-permute-start.13 = (f16[8,1152]{1,0:T(8,128)(2,1)S(1)}, f16[8,1152]{1,0:T(8,128)(2,1)S(1)}, u32[]{:S(2)}, u32[]{:S(2)}) collective-permute-start(f16[8,1152]{1,0:T(8,128)(2,1)S(1)} %get-tuple-element.36), channel_id=1, source_target_pairs={{0,1},{1,5},{2,9},{3,13},{4,2},{5,6},{6,10},{7,14},{8,3},{9,7},{10... | collective-permute-start | bytes 55304 | tf_op jit(solution)/shard_map/ppermute | solution.py:282
  53.4 7.4 %collective-permute-start.12 = (f16[8,1152]{1,0:T(8,128)(2,1)S(1)}, f16[8,1152]{1,0:T(8,128)(2,1)S(1)}, u32[]{:S(2)}, u32[]{:S(2)}) collective-permute-start(f16[8,1152]{1,0:T(8,128)(2,1)S(1)} %get-tuple-element.33), channel_id=1, source_target_pairs={{0,0},{1,4},{2,8},{3,12},{4,1},{5,5},{6,9},{7,13},{8,2},{9,6},{10,... | collective-permute-start | bytes 55304 | tf_op jit(solution)/shard_map/ppermute | solution.py:282

commit v6 on v5

--- a/solution.py
+++ b/solution.py
@@ -232,7 +232,6 @@
     block = tokens // groups
 
     right = project_right(out_grads, proj_out.T)
-    right, proj_in = lax.optimization_barrier((right, proj_in))
     coded = right.astype(jnp.float16)
 
     def part(shift):
@@ -257,7 +256,6 @@
     def towards(array, index):
         return lax.dynamic_index_in_dim(array, index, 0, keepdims=False)
 
-    terms, queries = lax.optimization_barrier((terms, queries))
     coded = terms.astype(jnp.float16)
     entries = rank * rank // groups
     sketch = None

time: 62.6 us -> 63.1 us (level)
  starting transfers between devices: 22.8 us -> 23.9 us
    ppermute x3, starting transfers between devices: 1.82 us -> 3.63 us  [local_square(): lax.ppermute(sketch, 'example', ring(groups, shift))]
    ppermute x3, waiting for transfers between devices: 0.31 us -> 1.07 us  [local_square(): lax.ppermute(part(shift), 'tensor', ring(groups, shift))]
    ppermute x3, starting transfers between devices: 3.78 us -> 3.03 us  [local_square(): piece = lax.ppermute(piece, 'tensor', ring(groups, shift))]
    ppermute x3, waiting for transfers between devices: 2.26 us -> 1.6 us  [local_square(): lax.ppermute(sketch, 'example', ring(groups, shift))]
  transfers between devices with their start and end apart: 16 -> 16, of which waited for: 7 -> 7; matrix products, arithmetic and copies ran while one was open for 1% -> 1% of each run, Pallas kernels for 28% -> 27%
where the time goes in v6:
time: 63.1 us; the launch traced here: 62.6 us
  Pallas kernels  25.9 us (41%)
  starting transfers between devices  23.9 us (38%)
  waiting for transfers between devices  10.2 us (16%)
  other arithmetic  2.21 us (4%)
    pallas_call x2, Pallas kernels, project_left(): pl.pallas_call(functools.partial(left_kernel, first, slots), in_specs=[pl...  17.2 us
    ppermute x4, starting transfers between devices, local_square(): lax.ppermute(towards(scores, (here - target) % groups), ('tensor', 'examp...  8.09 us
    pallas_call x1, Pallas kernels, project_right(): pl.pallas_call(right_kernel, in_specs=[pl.BlockSpec(memory_space=pltpu.HB...  6.46 us
    ppermute x3, starting transfers between devices, local_square(): lax.ppermute(part(shift), 'tensor', ring(groups, shift))  4.67 us
    ppermute x3, waiting for transfers between devices, local_square(): piece = lax.ppermute(piece, 'tensor', ring(groups, shift))  4.58 us
    ppermute x3, starting transfers between devices, local_square(): lax.ppermute(mine, 'tensor', ring(groups, shift))  4.45 us
    ppermute x3, starting transfers between devices, local_square(): lax.ppermute(sketch, 'example', ring(groups, shift))  3.63 us
    ppermute x3, starting transfers between devices, local_square(): piece = lax.ppermute(piece, 'tensor', ring(groups, shift))  3.03 us
  transfers between devices with their start and end apart: 16, of which 7 were waited for; matrix products, arithmetic and copies ran while one was open for 1% of the time, Pallas kernels for 27%

profile of v6, /device:TPU:2, one launch (start us, length us, event | category | flops | bytes accessed | tf_op | source)
XLA Modules:
  0.0 62.6 jit_solution(11508341087759276788)
XLA Ops:
  0.0 6.5 %project_right.1 = f32[72,3072]{1,0:T(8,128)S(1)} custom-call(bf16[6,512,2048]{2,1,0:T(8,128)(2,1)} %grads.1, bf16[64,2048]{1,0:T(8,128)(2,1)} %bitcast.36), custom_call_target="tpu_custom_call" | custom-call | flops 3221225472 | bytes 12582912 | tf_op jit(solution)/shard_map/project_right/pallas_call | solution.py:61
  6.6 3.7 %collective-permute-start.2 = (f16[72,768]{1,0:T(8,128)(2,1)S(1)}, f16[72,768]{1,0:T(8,128)(2,1)S(1)}, u32[]{:S(2)}, u32[]{:S(2)}) collective-permute-start(f16[72,768]{1,0:T(8,128)(2,1)S(1)} %get-tuple-element.17), channel_id=1, source_target_pairs={{0,12},{4,0},{8,4},{12,8},{1,13},{5,1},{9,5},{13,9},{2,14},{6,2},{... | collective-permute-start | bytes 331784 | tf_op jit(solution)/shard_map/ppermute | solution.py:240
  10.3 1.0 %collective-permute-start = (f16[72,768]{1,0:T(8,128)(2,1)S(1)}, f16[72,768]{1,0:T(8,128)(2,1)S(1)}, u32[]{:S(2)}, u32[]{:S(2)}) collective-permute-start(f16[72,768]{1,0:T(8,128)(2,1)S(1)} %get-tuple-element.19), channel_id=1, source_target_pairs={{0,4},{4,8},{8,12},{12,0},{1,5},{5,9},{9,13},{13,1},{2,6},{6,10},{... | collective-permute-start | bytes 331784 | tf_op jit(solution)/shard_map/ppermute | solution.py:240
  11.3 7.5 %project_left.2.left_a = bf16[1536,128]{1,0:T(8,128)(2,1)S(1)} custom-call(s32[6]{0:T(128)S(1)} %copy-done.2, bf16[6,512,7168]{2,1,0:T(8,128)(2,1)} %acts.3, bf16[64,7168]{1,0:T(8,128)(2,1)S(1)} %bitcast.26), custom_call_target="tpu_custom_call" | custom-call | flops 5637144576 | bytes 22020096 | tf_op jit(solution)/shard_map/project_left/pallas_call | solution.py:128
  18.9 1.1 %collective-permute-done.1 = f16[72,768]{1,0:T(8,128)(2,1)S(1)} collective-permute-done((f16[72,768]{1,0:T(8,128)(2,1)S(1)}, f16[72,768]{1,0:T(8,128)(2,1)S(1)}, u32[]{:S(2)}, u32[]{:S(2)}) %collective-permute-start.1) | collective-permute-done | bytes 110624 | tf_op jit(solution)/shard_map/ppermute | solution.py:240
  20.1 0.1 select_convert_fusion
  20.3 1.9 %collective-permute-start.5 = (f16[72,768]{1,0:T(8,128)(2,1)S(1)}, f16[72,768]{1,0:T(8,128)(2,1)S(1)}, u32[]{:S(2)}, u32[]{:S(2)}) collective-permute-start(f16[72,768]{1,0:T(8,128)(2,1)S(1)} %select_convert_fusion), channel_id=1, source_target_pairs={{0,12},{4,0},{8,4},{12,8},{1,13},{5,1},{9,5},{13,9},{2,14},{6,2},{... | collective-permute-start | bytes 331784 | tf_op jit(solution)/shard_map/ppermute | solution.py:250
  22.1 1.1 %collective-permute-start.4 = (f16[72,768]{1,0:T(8,128)(2,1)S(1)}, f16[72,768]{1,0:T(8,128)(2,1)S(1)}, u32[]{:S(2)}, u32[]{:S(2)}) collective-permute-start(f16[72,768]{1,0:T(8,128)(2,1)S(1)} %select_convert_fusion), channel_id=1, source_target_pairs={{0,8},{4,12},{8,0},{12,4},{1,9},{5,13},{9,1},{13,5},{2,10},{6,14},... | collective-permute-start | bytes 331784 | tf_op jit(solution)/shard_map/ppermute | solution.py:250
  23.2 1.5 %collective-permute-start.3 = (f16[72,768]{1,0:T(8,128)(2,1)S(1)}, f16[72,768]{1,0:T(8,128)(2,1)S(1)}, u32[]{:S(2)}, u32[]{:S(2)}) collective-permute-start(f16[72,768]{1,0:T(8,128)(2,1)S(1)} %select_convert_fusion), channel_id=1, source_target_pairs={{0,4},{4,8},{8,12},{12,0},{1,5},{5,9},{9,13},{13,1},{2,6},{6,10},{... | collective-permute-start | bytes 331784 | tf_op jit(solution)/shard_map/ppermute | solution.py:250
  24.7 9.6 %project_left.3.left_b = bf16[1536,128]{1,0:T(8,128)(2,1)S(1)} custom-call(s32[6]{0:T(128)S(1)} %copy-done.2, bf16[6,512,7168]{2,1,0:T(8,128)(2,1)} %acts.3, bf16[64,7168]{1,0:T(8,128)(2,1)S(1)} %bitcast.27), custom_call_target="tpu_custom_call" | custom-call | flops 5637144576 | bytes 22020096 | tf_op jit(solution)/shard_map/project_left/pallas_call | solution.py:128
  34.6 1.4 %sketch_terms.1 = f32[4,8,1152]{2,1,0:T(8,128)S(1)} custom-call(s32[4]{0:T(128)S(1)} %and_select_fusion.where, f32[4,64,768]{2,1,0:T(8,128)S(1)} %slice_multiply_fusion.rights, bf16[1536,128]{1,0:T(8,128)(2,1)S(1)} %project_left.2.left_a, bf16[1536,128]{1,0:T(8,128)(2,1)S(1)} %project_left.3.left_b), custom_call_target="tpu_custom_call" | custom-call | tf_op jit(solution)/shard_map/sketch_terms/pallas_call | solution.py:174
  36.1 2.4 %collective-permute-start.8 = (f16[8,1152]{1,0:T(8,128)(2,1)S(1)}, f16[8,1152]{1,0:T(8,128)(2,1)S(1)}, u32[]{:S(2)}, u32[]{:S(2)}) collective-permute-start(f16[8,1152]{1,0:T(8,128)(2,1)S(1)} %get-tuple-element.30), channel_id=1, source_target_pairs={{0,12},{4,0},{8,4},{12,8},{1,13},{5,1},{9,5},{13,9},{2,14},{6,2},{... | collective-permute-start | bytes 55304 | tf_op jit(solution)/shard_map/ppermute | solution.py:265
  38.6 0.6 collective-permute-start.6
  39.2 0.1 fusion.50
  39.3 0.7 %collective-permute-done.8 = f16[8,1152]{1,0:T(8,128)(2,1)S(1)} collective-permute-done((f16[8,1152]{1,0:T(8,128)(2,1)S(1)}, f16[8,1152]{1,0:T(8,128)(2,1)S(1)}, u32[]{:S(2)}, u32[]{:S(2)}) %collective-permute-start.8) | collective-permute-done | bytes 18464 | tf_op jit(solution)/shard_map/ppermute | solution.py:265
  40.0 0.1 fusion.41
  40.1 3.1 %collective-permute-done.7 = f16[8,1152]{1,0:T(8,128)(2,1)S(1)} collective-permute-done((f16[8,1152]{1,0:T(8,128)(2,1)S(1)}, f16[8,1152]{1,0:T(8,128)(2,1)S(1)}, u32[]{:S(2)}, u32[]{:S(2)}) %collective-permute-start.7) | collective-permute-done | bytes 18464 | tf_op jit(solution)/shard_map/ppermute | solution.py:265
  43.2 0.1 fusion.44
  43.3 0.8 %collective-permute-done.6 = f16[8,1152]{1,0:T(8,128)(2,1)S(1)} collective-permute-done((f16[8,1152]{1,0:T(8,128)(2,1)S(1)}, f16[8,1152]{1,0:T(8,128)(2,1)S(1)}, u32[]{:S(2)}, u32[]{:S(2)}) %collective-permute-start.6) | collective-permute-done | bytes 18464 | tf_op jit(solution)/shard_map/ppermute | solution.py:265
  44.1 0.1 fusion.47
  44.4 2.2 %collective-permute-start.10 = (f32[8,1024]{1,0:T(8,128)S(1)}, f32[8,1024]{1,0:T(8,128)S(1)}, u32[]{:S(2)}, u32[]{:S(2)}) collective-permute-start(f32[8,1024]{1,0:T(8,128)S(1)} %fusion.4.refs_0_), channel_id=1, source_target_pairs={{0,2},{1,3},{2,0},{3,1},{4,6},{5,7},{6,4},{7,5},{8,10},{9,11},{10,... | collective-permute-start | bytes 98312 | tf_op jit(solution)/shard_map/ppermute | solution.py:269
  46.6 1.4 %collective-permute-start.11 = (f32[8,1024]{1,0:T(8,128)S(1)}, f32[8,1024]{1,0:T(8,128)S(1)}, u32[]{:S(2)}, u32[]{:S(2)}) collective-permute-start(f32[8,1024]{1,0:T(8,128)S(1)} %fusion.4.refs_0_), channel_id=1, source_target_pairs={{0,3},{1,0},{2,1},{3,2},{4,7},{5,4},{6,5},{7,6},{8,11},{9,8},{10,9... | collective-permute-start | bytes 98312 | tf_op jit(solution)/shard_map/ppermute | solution.py:269
  48.0 0.5 collective-permute-done.10.refs_2_
  48.5 1.1 %collective-permute-done.11.refs_3_ = f32[8,1024]{1,0:T(8,128)S(1)} collective-permute-done((f32[8,1024]{1,0:T(8,128)S(1)}, f32[8,1024]{1,0:T(8,128)S(1)}, u32[]{:S(2)}, u32[]{:S(2)}) %collective-permute-start.11) | collective-permute-done | bytes 32800 | tf_op jit(solution)/shard_map/ppermute | solution.py:269
  49.6 0.9 %score_terms.1 = f32[4,8,1152]{2,1,0:T(8,128)S(1)} custom-call(f32[8,1024]{1,0:T(8,128)S(1)} %fusion.4.refs_0_, f32[8,1024]{1,0:T(8,128)S(1)} %collective-permute-done.9.refs_1_, f32[8,1024]{1,0:T(8,128)S(1)} %collective-permute-done.10.refs_2_, f32[8,1024]{1,0:T(8,128)S(1)} %collective-permute-done.11.refs_3_, bf16[1024,1024]{1,0:T(8,128)(2,1)S(1)} %copy-done.1), custom_call_target="tpu_custom_call" | custom-call | tf_op jit(solution)/shard_map/score_terms/pallas_call | solution.py:206
  50.5 1.2 %collective-permute-start.15 = (f16[8,1152]{1,0:T(8,128)(2,1)S(1)}, f16[8,1152]{1,0:T(8,128)(2,1)S(1)}, u32[]{:S(2)}, u32[]{:S(2)}) collective-permute-start(f16[8,1152]{1,0:T(8,128)(2,1)S(1)} %get-tuple-element.26), channel_id=1, source_target_pairs={{0,3},{1,7},{2,11},{3,15},{4,0},{5,4},{6,8},{7,12},{8,1},{9,5},{10... | collective-permute-start | bytes 55304 | tf_op jit(solution)/shard_map/ppermute | solution.py:280
  51.7 1.7 %collective-permute-start.14 = (f16[8,1152]{1,0:T(8,128)(2,1)S(1)}, f16[8,1152]{1,0:T(8,128)(2,1)S(1)}, u32[]{:S(2)}, u32[]{:S(2)}) collective-permute-start(f16[8,1152]{1,0:T(8,128)(2,1)S(1)} %get-tuple-element.27), channel_id=1, source_target_pairs={{0,2},{1,6},{2,10},{3,14},{4,3},{5,7},{6,11},{7,15},{8,0},{9,4},{1... | collective-permute-start | bytes 55304 | tf_op jit(solution)/shard_map/ppermute | solution.py:280
  53.4 0.8 %collective-permute-start.13 = (f16[8,1152]{1,0:T(8,128)(2,1)S(1)}, f16[8,1152]{1,0:T(8,128)(2,1)S(1)}, u32[]{:S(2)}, u32[]{:S(2)}) collective-permute-start(f16[8,1152]{1,0:T(8,128)(2,1)S(1)} %get-tuple-element.28), channel_id=1, source_target_pairs={{0,1},{1,5},{2,9},{3,13},{4,2},{5,6},{6,10},{7,14},{8,3},{9,7},{10... | collective-permute-start | bytes 55304 | tf_op jit(solution)/shard_map/ppermute | solution.py:280
  54.2 4.4 %collective-permute-start.12 = (f16[8,1152]{1,0:T(8,128)(2,1)S(1)}, f16[8,1152]{1,0:T(8,128)(2,1)S(1)}, u32[]{:S(2)}, u32[]{:S(2)}) collective-permute-start(f16[8,1152]{1,0:T(8,128)(2,1)S(1)} %get-tuple-element.25), channel_id=1, source_target_pairs={{0,0},{1,4},{2,8},{3,12},{4,1},{5,5},{6,9},{7,13},{8,2},{9,6},{10,... | collective-permute-start | bytes 55304 | tf_op jit(solution)/shard_map/ppermute | solution.py:280
  58.7 3.0 %collective-permute-done.12 = f16[8,1152]{1,0:T(8,128)(2,1)S(1)} collective-permute-done((f16[8,1152]{1,0:T(8,128)(2,1)S(1)}, f16[8,1152]{1,0:T(8,128)(2,1)S(1)}, u32[]{:S(2)}, u32[]{:S(2)}) %collective-permute-start.12) | collective-permute-done | bytes 18464 | tf_op jit(solution)/shard_map/ppermute | solution.py:280
  61.6 0.2 fusion.38
  61.9 0.7 %fusion.1 = f32[6,1024]{1,0:T(8,128)} fusion(f32[8,1152]{1,0:T(8,128)S(1)} %convert_element_type.71, f32[8,1152]{1,0:T(8,128)S(1)} %convert_element_type.70, f32[8,1152]{1,0:T(8,128)S(1)} %convert_element_type.69, f32[8,1152]{1,0:T(8,128)S(1)} %convert_element_type.68, f32[6]{0:T(128)S(1)} %get-tuple-element.10, f32[6]{0:T(128)S(1)} %get-tuple-element.13, ...), kind=kLoop, calls=%fused_computation.6 | loop fusion | flops 49152 | bytes 123000 | tf_op jit(solution)/shard_map/mul | solution.py:283
  (43 shorter events, 0.8 us)
Async XLA Ops:
  0.0 11.3 %copy-start.2 = (s32[6]{0:T(128)S(1)}, s32[6]{0:T(128)}, u32[]{:S(2)}) copy-start(s32[6]{0:T(128)} %lengths.2) | copy-start | bytes 76
  0.0 11.3 %copy-start = (bf16[7168,64]{0,1:T(8,128)(2,1)S(1)}, bf16[7168,64]{0,1:T(8,128)(2,1)}, u32[]{:S(2)}) copy-start(bf16[7168,64]{0,1:T(8,128)(2,1)} %param.9) | copy-start | bytes 2752516
  6.6 12.2 %collective-permute-start.2 = (f16[72,768]{1,0:T(8,128)(2,1)S(1)}, f16[72,768]{1,0:T(8,128)(2,1)S(1)}, u32[]{:S(2)}, u32[]{:S(2)}) collective-permute-start(f16[72,768]{1,0:T(8,128)(2,1)S(1)} %get-tuple-element.17), channel_id=1, source_target_pairs={{0,12},{4,0},{8,4},{12,8},{1,13},{5,1},{9,5},{13,9},{2,14},{6,2},{... | collective-permute-start | bytes 331784 | tf_op jit(solution)/shard_map/ppermute | solution.py:240
  10.3 9.7 %collective-permute-start.1 = (f16[72,768]{1,0:T(8,128)(2,1)S(1)}, f16[72,768]{1,0:T(8,128)(2,1)S(1)}, u32[]{:S(2)}, u32[]{:S(2)}) collective-permute-start(f16[72,768]{1,0:T(8,128)(2,1)S(1)} %get-tuple-element.18), channel_id=1, source_target_pairs={{0,8},{4,12},{8,0},{12,4},{1,9},{5,13},{9,1},{13,5},{2,10},{6,14},... | collective-permute-start | bytes 331784 | tf_op jit(solution)/shard_map/ppermute | solution.py:240
  10.3 9.7 %collective-permute-start = (f16[72,768]{1,0:T(8,128)(2,1)S(1)}, f16[72,768]{1,0:T(8,128)(2,1)S(1)}, u32[]{:S(2)}, u32[]{:S(2)}) collective-permute-start(f16[72,768]{1,0:T(8,128)(2,1)S(1)} %get-tuple-element.19), channel_id=1, source_target_pairs={{0,4},{4,8},{8,12},{12,0},{1,5},{5,9},{9,13},{13,1},{2,6},{6,10},{... | collective-permute-start | bytes 331784 | tf_op jit(solution)/shard_map/ppermute | solution.py:240
  20.2 29.3 %copy-start.1 = (bf16[1024,1024]{1,0:T(8,128)(2,1)S(1)}, bf16[1024,1024]{1,0:T(8,128)(2,1)}, u32[]{:S(2)}) copy-start(bf16[1024,1024]{1,0:T(8,128)(2,1)} %refs_4_.1) | copy-start | bytes 6291460
  20.3 14.1 %collective-permute-start.5 = (f16[72,768]{1,0:T(8,128)(2,1)S(1)}, f16[72,768]{1,0:T(8,128)(2,1)S(1)}, u32[]{:S(2)}, u32[]{:S(2)}) collective-permute-start(f16[72,768]{1,0:T(8,128)(2,1)S(1)} %select_convert_fusion), channel_id=1, source_target_pairs={{0,12},{4,0},{8,4},{12,8},{1,13},{5,1},{9,5},{13,9},{2,14},{6,2},{... | collective-permute-start | bytes 331784 | tf_op jit(solution)/shard_map/ppermute | solution.py:250
  22.1 12.2 %collective-permute-start.4 = (f16[72,768]{1,0:T(8,128)(2,1)S(1)}, f16[72,768]{1,0:T(8,128)(2,1)S(1)}, u32[]{:S(2)}, u32[]{:S(2)}) collective-permute-start(f16[72,768]{1,0:T(8,128)(2,1)S(1)} %select_convert_fusion), channel_id=1, source_target_pairs={{0,8},{4,12},{8,0},{12,4},{1,9},{5,13},{9,1},{13,5},{2,10},{6,14},... | collective-permute-start | bytes 331784 | tf_op jit(solution)/shard_map/ppermute | solution.py:250
  23.2 11.2 %collective-permute-start.3 = (f16[72,768]{1,0:T(8,128)(2,1)S(1)}, f16[72,768]{1,0:T(8,128)(2,1)S(1)}, u32[]{:S(2)}, u32[]{:S(2)}) collective-permute-start(f16[72,768]{1,0:T(8,128)(2,1)S(1)} %select_convert_fusion), channel_id=1, source_target_pairs={{0,4},{4,8},{8,12},{12,0},{1,5},{5,9},{9,13},{13,1},{2,6},{6,10},{... | collective-permute-start | bytes 331784 | tf_op jit(solution)/shard_map/ppermute | solution.py:250
  36.1 3.9 %collective-permute-start.8 = (f16[8,1152]{1,0:T(8,128)(2,1)S(1)}, f16[8,1152]{1,0:T(8,128)(2,1)S(1)}, u32[]{:S(2)}, u32[]{:S(2)}) collective-permute-start(f16[8,1152]{1,0:T(8,128)(2,1)S(1)} %get-tuple-element.30), channel_id=1, source_target_pairs={{0,12},{4,0},{8,4},{12,8},{1,13},{5,1},{9,5},{13,9},{2,14},{6,2},{... | collective-permute-start | bytes 55304 | tf_op jit(solution)/shard_map/ppermute | solution.py:265
  38.5 4.7 %collective-permute-start.7 = (f16[8,1152]{1,0:T(8,128)(2,1)S(1)}, f16[8,1152]{1,0:T(8,128)(2,1)S(1)}, u32[]{:S(2)}, u32[]{:S(2)}) collective-permute-start(f16[8,1152]{1,0:T(8,128)(2,1)S(1)} %get-tuple-element.31), channel_id=1, source_target_pairs={{0,8},{4,12},{8,0},{12,4},{1,9},{5,13},{9,1},{13,5},{2,10},{6,14},... | collective-permute-start | bytes 55304 | tf_op jit(solution)/shard_map/ppermute | solution.py:265
  38.6 5.6 %collective-permute-start.6 = (f16[8,1152]{1,0:T(8,128)(2,1)S(1)}, f16[8,1152]{1,0:T(8,128)(2,1)S(1)}, u32[]{:S(2)}, u32[]{:S(2)}) collective-permute-start(f16[8,1152]{1,0:T(8,128)(2,1)S(1)} %get-tuple-element.32), channel_id=1, source_target_pairs={{0,4},{4,8},{8,12},{12,0},{1,5},{5,9},{9,13},{13,1},{2,6},{6,10},{... | collective-permute-start | bytes 55304 | tf_op jit(solution)/shard_map/ppermute | solution.py:265
  44.3 3.6 %collective-permute-start.9 = (f32[8,1024]{1,0:T(8,128)S(1)}, f32[8,1024]{1,0:T(8,128)S(1)}, u32[]{:S(2)}, u32[]{:S(2)}) collective-permute-start(f32[8,1024]{1,0:T(8,128)S(1)} %fusion.4.refs_0_), channel_id=1, source_target_pairs={{0,1},{1,2},{2,3},{3,0},{4,5},{5,6},{6,7},{7,4},{8,9},{9,10},{10,1... | collective-permute-start | bytes 98312 | tf_op jit(solution)/shard_map/ppermute | solution.py:269
  44.4 4.1 %collective-permute-start.10 = (f32[8,1024]{1,0:T(8,128)S(1)}, f32[8,1024]{1,0:T(8,128)S(1)}, u32[]{:S(2)}, u32[]{:S(2)}) collective-permute-start(f32[8,1024]{1,0:T(8,128)S(1)} %fusion.4.refs_0_), channel_id=1, source_target_pairs={{0,2},{1,3},{2,0},{3,1},{4,6},{5,7},{6,4},{7,5},{8,10},{9,11},{10,... | collective-permute-start | bytes 98312 | tf_op jit(solution)/shard_map/ppermute | solution.py:269
  46.6 3.0 %collective-permute-start.11 = (f32[8,1024]{1,0:T(8,128)S(1)}, f32[8,1024]{1,0:T(8,128)S(1)}, u32[]{:S(2)}, u32[]{:S(2)}) collective-permute-start(f32[8,1024]{1,0:T(8,128)S(1)} %fusion.4.refs_0_), channel_id=1, source_target_pairs={{0,3},{1,0},{2,1},{3,2},{4,7},{5,4},{6,5},{7,6},{8,11},{9,8},{10,9... | collective-permute-start | bytes 98312 | tf_op jit(solution)/shard_map/ppermute | solution.py:269
  50.5 8.1 %collective-permute-start.15 = (f16[8,1152]{1,0:T(8,128)(2,1)S(1)}, f16[8,1152]{1,0:T(8,128)(2,1)S(1)}, u32[]{:S(2)}, u32[]{:S(2)}) collective-permute-start(f16[8,1152]{1,0:T(8,128)(2,1)S(1)} %get-tuple-element.26), channel_id=1, source_target_pairs={{0,3},{1,7},{2,11},{3,15},{4,0},{5,4},{6,8},{7,12},{8,1},{9,5},{10... | collective-permute-start | bytes 55304 | tf_op jit(solution)/shard_map/ppermute | solution.py:280
  51.7 6.9 %collective-permute-start.14 = (f16[8,1152]{1,0:T(8,128)(2,1)S(1)}, f16[8,1152]{1,0:T(8,128)(2,1)S(1)}, u32[]{:S(2)}, u32[]{:S(2)}) collective-permute-start(f16[8,1152]{1,0:T(8,128)(2,1)S(1)} %get-tuple-element.27), channel_id=1, source_target_pairs={{0,2},{1,6},{2,10},{3,14},{4,3},{5,7},{6,11},{7,15},{8,0},{9,4},{1... | collective-permute-start | bytes 55304 | tf_op jit(solution)/shard_map/ppermute | solution.py:280
  53.4 5.2 %collective-permute-start.13 = (f16[8,1152]{1,0:T(8,128)(2,1)S(1)}, f16[8,1152]{1,0:T(8,128)(2,1)S(1)}, u32[]{:S(2)}, u32[]{:S(2)}) collective-permute-start(f16[8,1152]{1,0:T(8,128)(2,1)S(1)} %get-tuple-element.28), channel_id=1, source_target_pairs={{0,1},{1,5},{2,9},{3,13},{4,2},{5,6},{6,10},{7,14},{8,3},{9,7},{10... | collective-permute-start | bytes 55304 | tf_op jit(solution)/shard_map/ppermute | solution.py:280
  54.2 7.4 %collective-permute-start.12 = (f16[8,1152]{1,0:T(8,128)(2,1)S(1)}, f16[8,1152]{1,0:T(8,128)(2,1)S(1)}, u32[]{:S(2)}, u32[]{:S(2)}) collective-permute-start(f16[8,1152]{1,0:T(8,128)(2,1)S(1)} %get-tuple-element.25), channel_id=1, source_target_pairs={{0,0},{1,4},{2,8},{3,12},{4,1},{5,5},{6,9},{7,13},{8,2},{9,6},{10,... | collective-permute-start | bytes 55304 | tf_op jit(solution)/shard_map/ppermute | solution.py:280
